TPU v7x, 128 devices: a whole 4x4x4 slice. The times are simulated.
128 devices in a mesh: dp: 64 (over z, y, x), tensor: 2 (over core).
Axes of the slice: x: 4, y: 4, z: 4, core: 2. Of those that a mesh axis runs over, the one named last changes fastest.
Arguments:
- acts: bfloat16 [32768, 2304], P('dp'), may hold values from -6 to 6
- grad_out: bfloat16 [32768, 4608], P('dp', 'tensor'), may hold values from -0.25 to 0.25
- old_error: bfloat16 [147456, 4608], P('dp', 'tensor'), may hold values from -6 to 6
- old_factor: bfloat16 [32, 4608], P(None, 'tensor'), may hold values from -0.09375 to 0.09375
- piece_order: int32 [8], replicated, may hold values from 0 to 7, each once
Outputs:
- new_error: bfloat16 [147456, 4608], P('dp', 'tensor')
- basis: float32 [2304, 32], replicated
- new_factor: float32 [32, 4608], P(None, 'tensor')
Inputs may be any that keep to these rules, and one draw needn't show every extreme that they name: `piece_order`: a permutation of 0 to 7.
All inputs are finite; a program needn't handle non-finite values.
Results may differ from a plain program's by a relative error of at most 0.0049.
Values may be sent and summed in bfloat16 or wider, within the bound.
No kernel may reach another device: no remote copies, remote signals or barrier semaphores. Data moves between devices by JAX's collectives and lax.ppermute only.
A program may use at most 192 MiB of HBM per device.

v0:
```python
import jax
import jax.numpy as jnp
from jax import lax
from jax.sharding import PartitionSpec as P


def order_pieces(block, piece_order):
    rows, width = block.shape
    blocks = piece_order.shape[0]
    split = block.reshape(rows, blocks, width // blocks)
    return jnp.take(split, piece_order, axis=1).reshape(rows, width)


def orthonormal(sums, gram):
    lower = jnp.linalg.cholesky(gram)
    return lax.linalg.triangular_solve(lower, sums, left_side=False, lower=True, transpose_a=True)


def body(acts, grad_out, old_error, old_factor, piece_order):
    error, factor = (
        lax.all_to_all(
            order_pieces(old_error, piece_order), "tensor", split_axis=1, concat_axis=1, tiled=True
        ),
        lax.all_to_all(
            order_pieces(old_factor, piece_order), "tensor", split_axis=1, concat_axis=1, tiled=True
        ),
    )
    grad = lax.dot_general(
        acts, grad_out, (((0,), (0,)), ((), ())), preferred_element_type=jnp.float32
    )
    corrected = (grad + error.astype(jnp.float32)).astype(jnp.bfloat16)
    left_term = lax.dot_general(
        corrected, factor, (((1,), (1,)), ((), ())), preferred_element_type=jnp.float32
    )
    sums = lax.psum(left_term, ("dp", "tensor"))
    gram = jnp.dot(sums.T, sums, precision=lax.Precision.HIGHEST)
    basis = orthonormal(sums, gram)
    basis_b = basis.astype(jnp.bfloat16)
    right_term = lax.dot_general(
        basis_b, corrected, (((0,), (0,)), ((), ())), preferred_element_type=jnp.float32
    )
    new_factor = lax.psum(right_term, "dp") / lax.axis_size("dp")
    factor_b = new_factor.astype(jnp.bfloat16)
    approx = jnp.dot(basis_b, factor_b, preferred_element_type=jnp.float32)
    new_error = (corrected.astype(jnp.float32) - approx).astype(jnp.bfloat16)
    return (new_error, basis, new_factor)


def solution(mesh):
    return jax.shard_map(
        body,
        mesh=mesh,
        in_specs=(P("dp", None), P("dp", "tensor"), P("dp", "tensor"), P(None, "tensor"), P()),
        out_specs=(P("dp", "tensor"), P(), P(None, "tensor")),
        check_vma=False,
    )
```

profile of v0, /device:TPU:0, one launch (start us, length us, event | category | flops | bytes accessed | tf_op | source)
XLA Modules:
  0.0 420.7 jit_solution(2675331802037977464)
XLA Ops:
  7.2 0.0 copy-start
  7.2 0.8 compare_select_fusion
  8.0 0.7 compare_and_fusion
  8.7 15.2 %copy.23 = bf16[2304,2304]{0,1:T(8,128)(2,1)} copy(bf16[2304,2304]{1,0:T(8,128)(2,1)} %param.7) | data formatting | bytes 21233664 | tf_op args[2]
  23.9 0.1 broadcast_in_dim.30
  24.0 0.1 broadcast_in_dim.31
  24.0 0.1 broadcast_in_dim.32
  24.1 9.7 %gather_fusion = bf16[8,2304,288]{1,2,0:T(8,128)(2,1)} fusion(bf16[2304,8,288]{0,2,1:T(8,128)(2,1)} %bitcast.27, s32[1024]{0:T(1024)S(1)} %pad_clamp_fusion), kind=kCustom, calls=%fused_computation | custom fusion | bytes 21233696 | tf_op jit(solution)/shard_map/jit(_take)/gather | solution.py:11
  33.8 10.2 %broadcast_select_fusion = bf16[2304,2,1152]{0,2,1:T(8,128)(2,1)} fusion(bf16[2304,2,1152]{0,2,1:T(8,128)(2,1)} %bitcast.28, pred[2,1152]{1,0:T(4,128)(4,1)S(1)} %broadcast_in_dim.32), kind=kLoop, calls=%fused_computation.6 | loop fusion | flops 5308416 | bytes 21235968 | tf_op jit(solution)/shard_map/jit(_take)/select_n | solution.py:11
  44.0 0.0 copy-start.3
  44.0 7.9 %all-to-all-start = ((bf16[2304,2,1152]{0,2,1:T(8,128)(2,1)}), bf16[2304,2,1152]{0,2,1:T(8,128)(2,1)}, u32[]{:S(2)}, u32[]{:S(2)}) async-start(bf16[2304,2,1152]{0,2,1:T(8,128)(2,1)} %broadcast_select_fusion), calls=%async_computation | async-start | bytes 21233664 | tf_op jit(solution)/shard_map/all_to_all | solution.py:21
  51.9 0.0 copy-done.3
  51.9 0.3 reshape.53
  52.2 0.6 gather_fusion.1
  52.8 0.1 copy.26
  52.9 0.3 gather.15
  53.2 0.1 broadcast_select_fusion.1
  53.3 0.7 copy.27
  54.0 7.0 %all-to-all-done = bf16[2304,2,1152]{0,2,1:T(8,128)(2,1)} async-done(((bf16[2304,2,1152]{0,2,1:T(8,128)(2,1)}), bf16[2304,2,1152]{0,2,1:T(8,128)(2,1)}, u32[]{:S(2)}, u32[]{:S(2)}) %all-to-all-start) | async-done | bytes 10616864 | tf_op jit(solution)/shard_map/all_to_all | solution.py:21
  61.0 3.4 all-to-all-start.1
  64.4 0.0 all-reduce.3.cloned.1.call-start
  64.4 11.7 %bitcast_convert_fusion = f32[2304,2304]{0,1:T(8,128)} fusion(bf16[2304,2,1152]{0,2,1:T(8,128)(2,1)} %all-to-all-done), kind=kLoop, calls=%fused_computation.5 | loop fusion | flops 5308416 | bytes 31850496 | tf_op jit(solution)/shard_map/convert_element_type | solution.py:31
  76.2 22.1 %copy.30 = f32[2304,2304]{1,0:T(8,128)} copy(f32[2304,2304]{0,1:T(8,128)} %bitcast_convert_fusion) | data formatting | bytes 42467328 | tf_op jit(solution)/shard_map/convert_element_type | solution.py:31
  98.3 0.0 all-to-all-done.1
  98.3 0.0 copy-done
  98.3 13.1 %add_convert_fusion = bf16[2304,2304]{1,0:T(8,128)(2,1)} fusion(f32[2304,2304]{1,0:T(8,128)} %copy.30, bf16[512,2304]{1,0:T(8,128)(2,1)S(1)} %copy-done, bf16[512,2304]{1,0:T(8,128)(2,1)} %param.6), kind=kOutput, calls=%fused_computation.3 | convolution fusion | flops 5446434816 | bytes 36569088 | tf_op jit(solution)/shard_map/dot_general | solution.py:28
  111.4 7.9 %fusion.9 = f32[2304,32]{0,1:T(8,128)} fusion(bf16[2304,2304]{1,0:T(8,128)(2,1)} %add_convert_fusion, bf16[32,2304]{1,0:T(8,128)(2,1)S(1)} %bitcast.31), kind=kOutput, calls=%fused_computation.26 | convolution fusion | flops 339738624 | bytes 11059200 | tf_op jit(solution)/shard_map/dot_general | solution.py:32
  119.3 0.0 all-reduce.3.cloned.1.call-update
  119.4 0.2 all-reduce.5.cloned.1.call-start
  119.6 144.7 %all-reduce.3.cloned.1.call-done = f32[2304,32]{0,1:T(8,128)} async-done(((f32[2304,32]{0,1:T(8,128)}), f32[2304,32]{0,1:T(8,128)}) %all-reduce.3.cloned.1.call-update) | async-done | bytes 294928 | tf_op jit(solution)/shard_map/psum | solution.py:35
  264.2 1.4 fusion.10
  265.7 0.1 copy.29
  265.8 2.9 cholesky.16
  268.7 0.6 compare_reduce_fusion
  269.4 0.7 fusion.5
  270.0 2.4 custom-call.6
  272.4 1.4 fusion.6
  273.9 0.0 copy-start.1
  273.9 6.7 %fusion.3 = f32[32,2304]{1,0:T(8,128)} fusion(bf16[2304,2304]{1,0:T(8,128)(2,1)} %add_convert_fusion, f32[2304,32]{0,1:T(8,128)S(1)} %fusion.6), kind=kOutput, calls=%fused_computation.11 | convolution fusion | flops 339812352 | bytes 11206656 | tf_op jit(solution)/shard_map/dot_general | solution.py:39
  280.6 0.0 all-reduce.5.cloned.1.call-update
  280.6 123.9 %all-reduce.5.cloned.1.call-done = f32[32,2304]{1,0:T(8,128)} async-done(((f32[32,2304]{1,0:T(8,128)}), f32[32,2304]{1,0:T(8,128)}) %all-reduce.5.cloned.1.call-update) | async-done | bytes 294928 | tf_op jit(solution)/shard_map/psum | solution.py:42
  404.5 1.0 broadcast_multiply_fusion
  405.5 0.0 copy-start.2
  405.5 8.3 %fusion = bf16[2304,2304]{1,0:T(8,128)(2,1)} fusion(bf16[2304,2304]{1,0:T(8,128)(2,1)} %add_convert_fusion, f32[32,2304]{1,0:T(8,128)S(1)} %broadcast_multiply_fusion, f32[2304,32]{0,1:T(8,128)S(1)} %fusion.6), kind=kOutput, calls=%fused_computation.4 | convolution fusion | flops 355811328 | bytes 21823488 | tf_op jit(solution)/shard_map/dot_general | solution.py:44
  413.9 0.0 copy-done.1
  413.9 0.0 copy-done.2
  (5 shorter events, 0.1 us)
Async XLA Ops:
  7.2 91.1 %copy-start = (bf16[512,2304]{1,0:T(8,128)(2,1)S(1)}, bf16[512,2304]{1,0:T(8,128)(2,1)}, u32[]{:S(2)}) copy-start(bf16[512,2304]{1,0:T(8,128)(2,1)} %param.5) | copy-start | bytes 7077892
  44.0 7.9 %copy-start.3 = (bf16[32,2304]{1,0:T(8,128)(2,1)S(1)}, bf16[32,2304]{1,0:T(8,128)(2,1)}, u32[]{:S(2)}) copy-start(bf16[32,2304]{1,0:T(8,128)(2,1)} %param.8) | copy-start | bytes 442372
  44.0 17.0 %all-to-all-start = ((bf16[2304,2,1152]{0,2,1:T(8,128)(2,1)}), bf16[2304,2,1152]{0,2,1:T(8,128)(2,1)}, u32[]{:S(2)}, u32[]{:S(2)}) async-start(bf16[2304,2,1152]{0,2,1:T(8,128)(2,1)} %broadcast_select_fusion), calls=%async_computation | async-start | bytes 21233664 | tf_op jit(solution)/shard_map/all_to_all | solution.py:21
  61.0 37.3 %all-to-all-start.1 = ((bf16[32,2,1152]{2,0,1:T(8,128)(2,1)}), bf16[32,2,1152]{2,0,1:T(8,128)(2,1)S(1)}, u32[]{:S(2)}, u32[]{:S(2)}) async-start(bf16[32,2,1152]{2,0,1:T(8,128)(2,1)} %copy.27), calls=%async_computation.1 | async-start | bytes 294912 | tf_op jit(solution)/shard_map/all_to_all | solution.py:24
  64.4 199.8 %all-reduce.3.cloned.1.call-start = ((), (), s32[]{:S(2)}) async-start(), calls=%async_computation.2 | async-start | bytes 589824 | tf_op jit(solution)/shard_map/psum | solution.py:35
  119.4 285.2 %all-reduce.5.cloned.1.call-start = ((), (), s32[]{:S(2)}) async-start(), calls=%async_computation.3 | async-start | bytes 589824 | tf_op jit(solution)/shard_map/psum | solution.py:42
  273.9 140.0 %copy-start.1 = (f32[2304,32]{0,1:T(8,128)}, f32[2304,32]{0,1:T(8,128)S(1)}, u32[]{:S(2)}) copy-start(f32[2304,32]{0,1:T(8,128)S(1)} %fusion.6) | copy-start | bytes 884740
  405.5 8.4 %copy-start.2 = (f32[32,2304]{1,0:T(8,128)}, f32[32,2304]{1,0:T(8,128)S(1)}, u32[]{:S(2)}) copy-start(f32[32,2304]{1,0:T(8,128)S(1)} %broadcast_multiply_fusion) | copy-start | bytes 884740
Sparse Core Ops, SparseCore 0:
  119.5 144.7 all-reduce.2
  280.8 123.7 all-reduce.4
where the time goes:
time: 422 us; the launch traced here: 421 us
  waiting for transfers between devices  276 us (65%)
  local copies, waits for them, and re-layouts  49.3 us (12%)
  matrix products  38.9 us (9%)
  other arithmetic  31.2 us (7%)
  between operations  14.2 us (3%)
  starting transfers between devices  11.6 us (3%)
    psum x1, waiting for transfers between devices, body(): sums = lax.psum(left_term, ('dp', 'tensor'))  145 us
    psum x1, waiting for transfers between devices, body(): new_factor = lax.psum(right_term, 'dp') / lax.axis_size('dp')  124 us
    convert_element_type x1, local copies, waits for them, and re-layouts, body(): corrected = (grad + error.astype(jnp.float32)).astype(jnp.bfloat16)  22.1 us
    unnamed x9, local copies, waits for them, and re-layouts  15.2 us
    dot_general x1, matrix products, body(): lax.dot_general(acts, grad_out, (((0,), (0,)), ((), ())), preferred_eleme...  13.1 us
    convert_element_type x1, other arithmetic, body(): corrected = (grad + error.astype(jnp.float32)).astype(jnp.bfloat16)  11.7 us
    select_n x3, other arithmetic, order_pieces(): return jnp.take(split, piece_order, axis=1).reshape(rows, width)  11.1 us
    gather x4, local copies, waits for them, and re-layouts, order_pieces(): return jnp.take(split, piece_order, axis=1).reshape(rows, width)  10.6 us
  transfers between devices with their start and end apart: 4, of which 3 were waited for; matrix products, arithmetic and copies ran while one was open for 9% of the time, Pallas kernels for 0%

commit v1 on v0

v1 whole, which is shorter than its diff:
```python
import functools

import jax
import jax.numpy as jnp
from jax import lax
from jax.experimental import pallas as pl
from jax.experimental.pallas import tpu as pltpu
from jax.sharding import PartitionSpec as P

BF, F32 = jnp.bfloat16, jnp.float32
ROWS, WIDTH, HALF, RANK, TOK = 2304, 2304, 1152, 32, 512
PIECE, QUARTER = 288, 4
LANES = 128
BLK = 256
HI = lax.Precision.HIGHEST
AXES = ("dp", "tensor")


def dot(a, b, dims, precision=None):
    return lax.dot_general(a, b, (dims, ((), ())), precision=precision, preferred_element_type=F32)


def params(mib=40):
    return pltpu.CompilerParams(vmem_limit_bytes=mib * 2**20)


def vmem(shape, dtype):
    return pltpu.VMEM(shape, dtype)


def in_vmem(x):
    return pltpu.with_memory_space_constraint(x, pltpu.VMEM)


WHOLE = pl.BlockSpec(memory_space=pltpu.VMEM)


def regroup(meta_ref, src_ref, dst_ref, first):
    rows = src_ref.shape[0]
    lane = lax.broadcasted_iota(jnp.int32, (rows, LANES), 1)
    carry = None
    for k in range(QUARTER):
        piece = meta_ref[first + k]
        start = pl.multiple_of(((piece * 9) // 4) * LANES, LANES)
        window = src_ref[:, pl.ds(start, 3 * LANES)].astype(F32)
        shift = 32 * k - 32 * (piece % 4)
        window = pltpu.roll(window, jnp.where(shift < 0, shift + 3 * LANES, shift), 1)
        tile = (PIECE * k) // LANES
        tiles = [window[:, i * LANES : (i + 1) * LANES] for i in range(3)]
        if k:
            tiles[0] = jnp.where(lane < 32 * k, carry, tiles[0])
        carry = tiles[2]
        last = 3 if k == QUARTER - 1 else 2
        for i in range(last):
            dst_ref[:, (tile + i) * LANES : (tile + i + 1) * LANES] = tiles[i].astype(dst_ref.dtype)


def left_kernel(meta_ref, err_ref, fac_ref, left_ref, send_ref, own_ref):
    me = meta_ref[8]
    left_ref[...] = dot(fac_ref[...], err_ref[...], ((1,), (1,)))
    regroup(meta_ref, err_ref, send_ref, (1 - me) * QUARTER)
    regroup(meta_ref, err_ref, own_ref, me * QUARTER)


def left_part(meta, old_error, old_factor):
    grid_spec = pltpu.PrefetchScalarGridSpec(
        num_scalar_prefetch=1,
        grid=(ROWS // BLK,),
        in_specs=[
            pl.BlockSpec((BLK, WIDTH), lambda i, m: (i, 0)),
            pl.BlockSpec((RANK, WIDTH), lambda i, m: (0, 0)),
        ],
        out_specs=[
            pl.BlockSpec((RANK, BLK), lambda i, m: (0, i)),
            pl.BlockSpec((BLK, HALF), lambda i, m: (i, 0)),
            pl.BlockSpec((BLK, HALF), lambda i, m: (i, 0)),
        ],
    )
    return pl.pallas_call(
        left_kernel,
        grid_spec=grid_spec,
        out_shape=[
            jax.ShapeDtypeStruct((RANK, ROWS), F32),
            jax.ShapeDtypeStruct((ROWS, HALF), BF),
            jax.ShapeDtypeStruct((ROWS, HALF), BF),
        ],
        compiler_params=params(),
        cost_estimate=pl.CostEstimate(flops=2 * RANK * ROWS * WIDTH, bytes_accessed=20 * 2**20, transcendentals=0),
        name="left_part",
    )(meta, old_error, old_factor)


def grad_term_kernel(meta_ref, fac_ref, other_ref, left_ref, acts_ref, grad_ref, keep_ref, give_ref, fac_new):
    me = meta_ref[8]
    own_at = pl.multiple_of(me * HALF, LANES)
    other_at = pl.multiple_of((1 - me) * HALF, LANES)
    regroup(meta_ref, fac_ref, fac_new.at[:, pl.ds(own_at, HALF)], me * QUARTER)
    regroup(meta_ref, other_ref, fac_new.at[:, pl.ds(other_at, HALF)], me * QUARTER)
    u = dot(fac_new[...], grad_ref[...], ((1,), (1,)))
    high = u.astype(BF)
    low = (u - high.astype(F32)).astype(BF)
    both = dot(jnp.concatenate([high, low], 0), acts_ref[...], ((1,), (0,)))
    total = left_ref[...] + both[:RANK] + both[RANK:]
    half = RANK // 2
    keep_ref[...] = jnp.where(me == 0, total[:half], total[half:])
    give_ref[...] = jnp.where(me == 0, total[half:], total[:half])


def grad_term(meta, old_factor, other_factor, left, acts, grad_out):
    return pl.pallas_call(
        grad_term_kernel,
        in_specs=[pl.BlockSpec(memory_space=pltpu.SMEM)] + [WHOLE] * 5,
        out_specs=[WHOLE, WHOLE],
        out_shape=[jax.ShapeDtypeStruct((RANK // 2, ROWS), F32)] * 2,
        scratch_shapes=[pltpu.VMEM((RANK, WIDTH), BF)],
        compiler_params=params(),
        name="grad_term",
    )(meta, old_factor, other_factor, left, acts, grad_out)


def grad_kernel(meta_ref, acts_ref, grad_ref, err_ref, out_ref):
    g = dot(acts_ref[...], grad_ref[...], ((0,), (0,)))
    out_ref[...] = (g + err_ref[...].astype(F32)).astype(BF)


def corrected_half(meta, acts, grad_out, err, other):
    def column(i, m):
        return (0, (1 - m[8]) if other else m[8])

    grid_spec = pltpu.PrefetchScalarGridSpec(
        num_scalar_prefetch=1,
        grid=(ROWS // BLK,),
        in_specs=[
            pl.BlockSpec((TOK, BLK), lambda i, m: (0, i)),
            pl.BlockSpec((TOK, HALF), column),
            pl.BlockSpec((BLK, HALF), lambda i, m: (i, 0)),
        ],
        out_specs=pl.BlockSpec((BLK, HALF), lambda i, m: (i, 0)),
    )
    return pl.pallas_call(
        grad_kernel,
        grid_spec=grid_spec,
        out_shape=jax.ShapeDtypeStruct((ROWS, HALF), BF),
        compiler_params=params(),
        cost_estimate=pl.CostEstimate(flops=2 * TOK * ROWS * HALF, bytes_accessed=12 * 2**20, transcendentals=0),
        name="corrected_other" if other else "corrected_own",
    )(meta, acts, grad_out, err)


def right_kernel(meta_ref, keep_ref, took_ref, own_ref, other_ref, basis_ref, basis_b_ref, right_ref):
    me = meta_ref[8]
    keep, took = keep_ref[...], took_ref[...]
    sums = jnp.concatenate(
        [jnp.where(me == 0, keep, took), jnp.where(me == 0, took, keep)], 0
    )
    gram = dot(sums, sums, ((1,), (1,)), HI)
    row = lax.broadcasted_iota(jnp.int32, (RANK, RANK), 0)
    col = lax.broadcasted_iota(jnp.int32, (RANK, RANK), 1)
    work = jnp.concatenate([gram, (row == col).astype(F32)], 1)
    row2 = lax.broadcasted_iota(jnp.int32, (RANK, 2 * RANK), 0)
    for k in range(RANK):
        pivot_row = work[k : k + 1, :]
        scale = lax.rsqrt(pivot_row[:, k : k + 1])
        pivot_row = pivot_row * scale
        column = work[:, k : k + 1] * scale
        work = jnp.where(
            row2 == k, pivot_row, jnp.where(row2 > k, work - column * pivot_row, work)
        )
    inverse = work[:, RANK:]
    basis = dot(inverse, sums, ((1,), (0,)), HI)
    basis_ref[...] = basis
    basis_b = basis.astype(BF)
    basis_b_ref[...] = basis_b
    own_at = pl.multiple_of(me * HALF, LANES)
    other_at = pl.multiple_of((1 - me) * HALF, LANES)
    right_ref[:, pl.ds(own_at, HALF)] = dot(basis_b, own_ref[...], ((1,), (0,))).astype(BF)
    right_ref[:, pl.ds(other_at, HALF)] = dot(basis_b, other_ref[...], ((1,), (0,))).astype(BF)


def right_part(meta, keep, took, own, other):
    return pl.pallas_call(
        right_kernel,
        in_specs=[pl.BlockSpec(memory_space=pltpu.SMEM)] + [WHOLE] * 4,
        out_specs=[WHOLE] * 3,
        out_shape=[
            jax.ShapeDtypeStruct((RANK, ROWS), F32),
            jax.ShapeDtypeStruct((RANK, ROWS), BF),
            jax.ShapeDtypeStruct((RANK, WIDTH), BF),
        ],
        compiler_params=params(),
        name="right_part",
    )(meta, keep, took, own, other)


def residue_kernel(scale, meta_ref, a_ref, b_ref, c_ref, d_ref, basis_b_ref, own_ref, other_ref, err_ref, fac_ref, fac_b):
    i = pl.program_id(0)

    @pl.when(i == 0)
    def _():
        total = (a_ref[...].astype(F32) + b_ref[...].astype(F32)) + (
            c_ref[...].astype(F32) + d_ref[...].astype(F32)
        )
        factor = total * scale
        fac_ref[...] = factor
        fac_b[...] = factor.astype(BF)

    me = meta_ref[8]
    basis_b = basis_b_ref[...]
    for src, who in ((own_ref, me), (other_ref, 1 - me)):
        at = pl.multiple_of(who * HALF, LANES)
        approx = dot(basis_b, fac_b[:, pl.ds(at, HALF)], ((0,), (0,)))
        err_ref[:, pl.ds(at, HALF)] = (src[...].astype(F32) - approx).astype(BF)


def residue(meta, terms, basis_b, own, other, scale):
    def fixed(i, m):
        return (0, 0)

    grid_spec = pltpu.PrefetchScalarGridSpec(
        num_scalar_prefetch=1,
        grid=(ROWS // BLK,),
        in_specs=[pl.BlockSpec((RANK, WIDTH), fixed)] * 4
        + [
            pl.BlockSpec((RANK, BLK), lambda i, m: (0, i)),
            pl.BlockSpec((BLK, HALF), lambda i, m: (i, 0)),
            pl.BlockSpec((BLK, HALF), lambda i, m: (i, 0)),
        ],
        out_specs=[
            pl.BlockSpec((BLK, WIDTH), lambda i, m: (i, 0)),
            pl.BlockSpec((RANK, WIDTH), fixed),
        ],
        scratch_shapes=[pltpu.VMEM((RANK, WIDTH), BF)],
    )
    return pl.pallas_call(
        functools.partial(residue_kernel, scale),
        grid_spec=grid_spec,
        out_shape=[
            jax.ShapeDtypeStruct((ROWS, WIDTH), BF),
            jax.ShapeDtypeStruct((RANK, WIDTH), F32),
        ],
        compiler_params=params(),
        name="residue",
    )(meta, *terms, basis_b, own, other)


def ring_pairs(axes, flip):
    pairs = []
    for index in range(64):
        for core in range(2):
            pairs.append((index * 2 + core, (index ^ (flip << (2 * axes[core]))) * 2 + core))
    return pairs


STAGES = ((0, 1), (1, 2), (2, 0))


def spread(x, axes):
    return [x] + [lax.ppermute(x, AXES, ring_pairs(axes, flip)) for flip in (2, 1, 3)]


def add4(terms):
    a, b, c, d = (t.astype(F32) for t in terms)
    return (a + b) + (c + d)


SWAP = [(0, 1), (1, 0)]


def body(acts, grad_out, old_error, old_factor, piece_order):
    me = lax.axis_index("tensor").astype(jnp.int32)
    meta = jnp.concatenate([piece_order, me[None]])
    other_factor = lax.ppermute(old_factor, "tensor", SWAP)
    left, send, own_err = left_part(meta, old_error, old_factor)
    keep, give = grad_term(meta, old_factor, other_factor, left, acts, grad_out)
    took = lax.ppermute(give, "tensor", SWAP)
    other_err = lax.ppermute(send, "tensor", SWAP)
    part = keep + took
    for axes in STAGES:
        part = add4(spread(part, axes))
    other_part = lax.ppermute(part, "tensor", SWAP)
    own = corrected_half(meta, acts, grad_out, own_err, False)
    other = corrected_half(meta, acts, grad_out, other_err, True)
    basis_t, basis_b, right = right_part(meta, part, other_part, own, other)
    for axes in STAGES[:-1]:
        right = add4(spread(right, axes)).astype(BF)
    terms = spread(right, STAGES[-1])
    new_error, new_factor = residue(meta, terms, basis_b, own, other, 1.0 / lax.axis_size("dp"))
    return (new_error, basis_t.T, new_factor)


def solution(mesh):
    return jax.shard_map(
        body,
        mesh=mesh,
        in_specs=(P("dp", None), P("dp", "tensor"), P("dp", "tensor"), P(None, "tensor"), P()),
        out_specs=(P("dp", "tensor"), P(), P(None, "tensor")),
        check_vma=False,
    )
```

time: 422 us -> 114 us (0.27)
  waiting for transfers between devices: 276 us -> 31.4 us
  local copies, waits for them, and re-layouts: 49.3 us -> 0.92 us
  Pallas kernels: 0 us -> 47.8 us
  matrix products: 38.9 us -> 0 us
  other arithmetic: 31.2 us -> 0.99 us
  starting transfers between devices: 11.6 us -> 30.5 us
  between operations: 14.2 us -> 0.76 us
    psum x2 -> x0, waiting for transfers between devices: 269 us -> none  [the longest x1 145 us: body(): sums = lax.psum(left_term, ('dp', 'tensor'))]
    pallas_call x0 -> x6, Pallas kernels: none -> 47.8 us  [the longest x2 17.6 us: corrected_half(): pl.pallas_call(grad_kernel, grid_spec=grid_spec, out_shape=jax.ShapeDtype...]
    dot_general x5 -> x0, matrix products: 37.5 us -> none  [the longest x1 13.1 us: body(): lax.dot_general(acts, grad_out, (((0,), (0,)), ((), ())), preferred_eleme...]
    ppermute x0 -> x22, waiting for transfers between devices: none -> 31.4 us  [the longest x18 24.6 us: spread(): lax.ppermute(x, AXES, ring_pairs(axes, flip))]
    ppermute x0 -> x22, starting transfers between devices: none -> 30.5 us  [the longest x18 29.5 us: spread(): lax.ppermute(x, AXES, ring_pairs(axes, flip))]
    convert_element_type x1 -> x0, local copies, waits for them, and re-layouts: 22.1 us -> none  [body(): corrected = (grad + error.astype(jnp.float32)).astype(jnp.bfloat16)]
    unnamed x9 -> x10, local copies, waits for them, and re-layouts: 15.2 us -> 0.92 us
    convert_element_type x1 -> x2, other arithmetic: 11.7 us -> 0.15 us  [body(): right = add4(spread(right, axes)).astype(BF)]
  transfers between devices with their start and end apart: 4 -> 22, of which waited for: 3 -> 17; matrix products, arithmetic and copies ran while one was open for 9% -> 0% of each run, Pallas kernels for 0% -> 17%
where the time goes in v1:
time: 114 us; the launch traced here: 112 us
  Pallas kernels  47.8 us (42%)
  waiting for transfers between devices  31.4 us (28%)
  starting transfers between devices  30.5 us (27%)
    ppermute x18, starting transfers between devices, spread(): lax.ppermute(x, AXES, ring_pairs(axes, flip))  29.5 us
    ppermute x18, waiting for transfers between devices, spread(): lax.ppermute(x, AXES, ring_pairs(axes, flip))  24.6 us
    pallas_call x2, Pallas kernels, corrected_half(): pl.pallas_call(grad_kernel, grid_spec=grid_spec, out_shape=jax.ShapeDtype...  17.6 us
    pallas_call x1, Pallas kernels, left_part(): pl.pallas_call(left_kernel, grid_spec=grid_spec, out_shape=[jax.ShapeDtyp...  13.6 us
    pallas_call x1, Pallas kernels, residue(): pl.pallas_call(functools.partial(residue_kernel, scale), grid_spec=grid_s...  8.17 us
    pallas_call x1, Pallas kernels, right_part(): pl.pallas_call(right_kernel, in_specs=[pl.BlockSpec(memory_space=pltpu.SM...  6.48 us
    ppermute x1, waiting for transfers between devices, body(): other_factor = lax.ppermute(old_factor, 'tensor', SWAP)  5.78 us
  transfers between devices with their start and end apart: 22, of which 17 were waited for; matrix products, arithmetic and copies ran while one was open for 0% of the time, Pallas kernels for 17%

profile of v1, /device:TPU:0, one launch (start us, length us, event | category | flops | bytes accessed | tf_op | source)
XLA Modules:
  0.0 112.4 jit_solution(11985547393160332746)
XLA Ops:
  0.6 0.7 pad_add_fusion.meta_ref
  1.4 0.9 copy-done.4
  2.3 13.6 %left_part.1 = (f32[32,2304]{1,0:T(8,128)S(1)}, bf16[2304,1152]{1,0:T(8,128)(2,1)}, bf16[2304,1152]{1,0:T(8,128)(2,1)S(1)}) custom-call(s32[9]{0:T(128)S(1)} %pad_add_fusion.meta_ref, bf16[2304,2304]{1,0:T(8,128)(2,1)} %err_ref.1, bf16[32,2304]{1,0:T(8,128)(2,1)S(1)} %copy-done.4), custom_call_target="tpu_custom_call" | custom-call | flops 339738624 | bytes 20971520 | tf_op jit(solution)/shard_map/left_part/pallas_call | solution.py:79
  15.9 0.0 collective-permute-start.12
  15.9 0.5 collective-permute-start
  16.4 5.8 %collective-permute-done.other_ref = bf16[32,2304]{1,0:T(8,128)(2,1)S(1)} collective-permute-done((bf16[32,2304]{1,0:T(8,128)(2,1)S(1)}, bf16[32,2304]{1,0:T(8,128)(2,1)S(1)}, u32[]{:S(2)}, u32[]{:S(2)}) %collective-permute-start) | collective-permute-done | bytes 147488 | tf_op jit(solution)/shard_map/ppermute | solution.py:272
  22.2 1.9 %grad_term.1 = (f32[16,2304]{1,0:T(8,128)S(1)}, f32[16,2304]{1,0:T(8,128)S(1)}) custom-call(s32[9]{0:T(128)S(1)} %pad_add_fusion.meta_ref, bf16[32,2304]{1,0:T(8,128)(2,1)S(1)} %copy-done.4, bf16[32,2304]{1,0:T(8,128)(2,1)S(1)} %collective-permute-done.other_ref, f32[32,2304]{1,0:T(8,128)S(1)} %get-tuple-element.13.left_ref, bf16[512,2304]{1,0:T(8,128)(2,1)S(1)} %copy-done, ...), custom_call_target="tpu_custom_call" | custom-call | tf_op jit(solution)/shard_map/grad_term/pallas_call | solution.py:110
  24.1 0.5 collective-permute-start.1
  24.6 1.0 collective-permute-done.1
  25.6 2.9 %collective-permute-start.4 = (f32[16,2304]{1,0:T(8,128)S(1)}, f32[16,2304]{1,0:T(8,128)S(1)}, u32[]{:S(2)}, u32[]{:S(2)}) collective-permute-start(f32[16,2304]{1,0:T(8,128)S(1)} %add.48), channel_id=1, source_target_pairs={{0,6},{1,25},{2,4},{3,27},{4,2},{5,29},{6,0},{7,31},{8,14},{9,17},... | collective-permute-start | bytes 442376 | tf_op jit(solution)/shard_map/ppermute | solution.py:258
  28.5 0.2 collective-permute-start.3
  28.8 1.6 %collective-permute-start.2 = (f32[16,2304]{1,0:T(8,128)S(1)}, f32[16,2304]{1,0:T(8,128)S(1)}, u32[]{:S(2)}, u32[]{:S(2)}) collective-permute-start(f32[16,2304]{1,0:T(8,128)S(1)} %add.48), channel_id=1, source_target_pairs={{0,4},{1,17},{2,6},{3,19},{4,0},{5,21},{6,2},{7,23},{8,12},{9,25},... | collective-permute-start | bytes 442376 | tf_op jit(solution)/shard_map/ppermute | solution.py:258
  30.4 1.7 %collective-permute-done.4 = f32[16,2304]{1,0:T(8,128)S(1)} collective-permute-done((f32[16,2304]{1,0:T(8,128)S(1)}, f32[16,2304]{1,0:T(8,128)S(1)}, u32[]{:S(2)}, u32[]{:S(2)}) %collective-permute-start.4) | collective-permute-done | bytes 147488 | tf_op jit(solution)/shard_map/ppermute | solution.py:258
  32.0 1.6 %collective-permute-done.3 = f32[16,2304]{1,0:T(8,128)S(1)} collective-permute-done((f32[16,2304]{1,0:T(8,128)S(1)}, f32[16,2304]{1,0:T(8,128)S(1)}, u32[]{:S(2)}, u32[]{:S(2)}) %collective-permute-start.3) | collective-permute-done | bytes 147488 | tf_op jit(solution)/shard_map/ppermute | solution.py:258
  33.7 1.7 %collective-permute-done.2 = f32[16,2304]{1,0:T(8,128)S(1)} collective-permute-done((f32[16,2304]{1,0:T(8,128)S(1)}, f32[16,2304]{1,0:T(8,128)S(1)}, u32[]{:S(2)}, u32[]{:S(2)}) %collective-permute-start.2) | collective-permute-done | bytes 147488 | tf_op jit(solution)/shard_map/ppermute | solution.py:258
  35.4 3.1 %collective-permute-start.7 = (f32[16,2304]{1,0:T(8,128)S(1)}, f32[16,2304]{1,0:T(8,128)S(1)}, u32[]{:S(2)}, u32[]{:S(2)}) collective-permute-start(f32[16,2304]{1,0:T(8,128)S(1)} %add_add_fusion.2), channel_id=1, source_target_pairs={{0,24},{1,97},{2,26},{3,99},{4,28},{5,101},{6,30},{7,103},{8,16},{... | collective-permute-start | bytes 442376 | tf_op jit(solution)/shard_map/ppermute | solution.py:258
  38.5 0.1 collective-permute-start.6
  38.7 1.5 %collective-permute-start.5 = (f32[16,2304]{1,0:T(8,128)S(1)}, f32[16,2304]{1,0:T(8,128)S(1)}, u32[]{:S(2)}, u32[]{:S(2)}) collective-permute-start(f32[16,2304]{1,0:T(8,128)S(1)} %add_add_fusion.2), channel_id=1, source_target_pairs={{0,16},{1,65},{2,18},{3,67},{4,20},{5,69},{6,22},{7,71},{8,24},{9,... | collective-permute-start | bytes 442376 | tf_op jit(solution)/shard_map/ppermute | solution.py:258
  40.2 1.7 %collective-permute-done.7 = f32[16,2304]{1,0:T(8,128)S(1)} collective-permute-done((f32[16,2304]{1,0:T(8,128)S(1)}, f32[16,2304]{1,0:T(8,128)S(1)}, u32[]{:S(2)}, u32[]{:S(2)}) %collective-permute-start.7) | collective-permute-done | bytes 147488 | tf_op jit(solution)/shard_map/ppermute | solution.py:258
  41.9 1.8 %collective-permute-done.6 = f32[16,2304]{1,0:T(8,128)S(1)} collective-permute-done((f32[16,2304]{1,0:T(8,128)S(1)}, f32[16,2304]{1,0:T(8,128)S(1)}, u32[]{:S(2)}, u32[]{:S(2)}) %collective-permute-start.6) | collective-permute-done | bytes 147488 | tf_op jit(solution)/shard_map/ppermute | solution.py:258
  43.7 1.6 %collective-permute-done.5 = f32[16,2304]{1,0:T(8,128)S(1)} collective-permute-done((f32[16,2304]{1,0:T(8,128)S(1)}, f32[16,2304]{1,0:T(8,128)S(1)}, u32[]{:S(2)}, u32[]{:S(2)}) %collective-permute-start.5) | collective-permute-done | bytes 147488 | tf_op jit(solution)/shard_map/ppermute | solution.py:258
  45.4 4.1 %collective-permute-start.10 = (f32[16,2304]{1,0:T(8,128)S(1)}, f32[16,2304]{1,0:T(8,128)S(1)}, u32[]{:S(2)}, u32[]{:S(2)}) collective-permute-start(f32[16,2304]{1,0:T(8,128)S(1)} %add_add_fusion.1), channel_id=1, source_target_pairs={{0,96},{1,7},{2,98},{3,5},{4,100},{5,3},{6,102},{7,1},{8,104},{9,1... | collective-permute-start | bytes 442376 | tf_op jit(solution)/shard_map/ppermute | solution.py:258
  49.5 0.0 collective-permute-start.9
  49.5 1.6 %collective-permute-start.8 = (f32[16,2304]{1,0:T(8,128)S(1)}, f32[16,2304]{1,0:T(8,128)S(1)}, u32[]{:S(2)}, u32[]{:S(2)}) collective-permute-start(f32[16,2304]{1,0:T(8,128)S(1)} %add_add_fusion.1), channel_id=1, source_target_pairs={{0,64},{1,5},{2,66},{3,7},{4,68},{5,1},{6,70},{7,3},{8,72},{9,13},... | collective-permute-start | bytes 442376 | tf_op jit(solution)/shard_map/ppermute | solution.py:258
  51.0 8.9 %corrected_own.1.own_ref = bf16[2304,1152]{1,0:T(8,128)(2,1)S(1)} custom-call(s32[9]{0:T(128)S(1)} %pad_add_fusion.meta_ref, bf16[512,2304]{1,0:T(8,128)(2,1)S(1)} %copy-done, bf16[512,2304]{1,0:T(8,128)(2,1)S(1)} %copy-done.1, bf16[2304,1152]{1,0:T(8,128)(2,1)} %copy-done.3), custom_call_target="tpu_custom_call" | custom-call | flops 2717908992 | bytes 12582912 | tf_op jit(solution)/shard_map/corrected_own/pallas_call | solution.py:140
  59.9 0.0 collective-permute-done.10
  59.9 0.0 collective-permute-done.8
  60.0 0.1 collective-permute-start.11
  60.1 8.7 %corrected_other.1.other_ref = bf16[2304,1152]{1,0:T(8,128)(2,1)S(1)} custom-call(s32[9]{0:T(128)S(1)} %pad_add_fusion.meta_ref, bf16[512,2304]{1,0:T(8,128)(2,1)S(1)} %copy-done, bf16[512,2304]{1,0:T(8,128)(2,1)S(1)} %copy-done.2, bf16[2304,1152]{1,0:T(8,128)(2,1)} %collective-permute-done.12.err_ref), custom_call_target="tpu_custom_call" | custom-call | flops 2717908992 | bytes 12582912 | tf_op jit(solution)/shard_map/corrected_other/pallas_call | solution.py:140
  68.9 6.5 %right_part.1 = (f32[32,2304]{1,0:T(8,128)}, bf16[32,2304]{1,0:T(8,128)(2,1)S(1)}, bf16[32,2304]{1,0:T(8,128)(2,1)S(1)}) custom-call(s32[9]{0:T(128)S(1)} %pad_add_fusion.meta_ref, f32[16,2304]{1,0:T(8,128)S(1)} %add_add_fusion.keep_ref, f32[16,2304]{1,0:T(8,128)S(1)} %collective-permute-done.11.took_ref, bf16[2304,1152]{1,0:T(8,128)(2,1)S(1)} %corrected_own.1.own_ref, ...), custom_call_target="tpu_custom_call" | custom-call | tf_op jit(solution)/shard_map/right_part/pallas_call | solution.py:181
  75.4 2.5 %collective-permute-start.15 = (bf16[32,2304]{1,0:T(8,128)(2,1)S(1)}, bf16[32,2304]{1,0:T(8,128)(2,1)S(1)}, u32[]{:S(2)}, u32[]{:S(2)}) collective-permute-start(bf16[32,2304]{1,0:T(8,128)(2,1)S(1)} %get-tuple-element.18), channel_id=1, source_target_pairs={{0,6},{1,25},{2,4},{3,27},{4,2},{5,29},{6,0},{7,31},{8,14},{9,17},... | collective-permute-start | bytes 442376 | tf_op jit(solution)/shard_map/ppermute | solution.py:258
  77.9 2.2 %collective-permute-start.13 = (bf16[32,2304]{1,0:T(8,128)(2,1)S(1)}, bf16[32,2304]{1,0:T(8,128)(2,1)S(1)}, u32[]{:S(2)}, u32[]{:S(2)}) collective-permute-start(bf16[32,2304]{1,0:T(8,128)(2,1)S(1)} %get-tuple-element.18), channel_id=1, source_target_pairs={{0,4},{1,17},{2,6},{3,19},{4,0},{5,21},{6,2},{7,23},{8,12},{9,25},... | collective-permute-start | bytes 442376 | tf_op jit(solution)/shard_map/ppermute | solution.py:258
  80.1 1.7 %collective-permute-done.15 = bf16[32,2304]{1,0:T(8,128)(2,1)S(1)} collective-permute-done((bf16[32,2304]{1,0:T(8,128)(2,1)S(1)}, bf16[32,2304]{1,0:T(8,128)(2,1)S(1)}, u32[]{:S(2)}, u32[]{:S(2)}) %collective-permute-start.15) | collective-permute-done | bytes 147488 | tf_op jit(solution)/shard_map/ppermute | solution.py:258
  81.7 1.3 %collective-permute-done.14 = bf16[32,2304]{1,0:T(8,128)(2,1)S(1)} collective-permute-done((bf16[32,2304]{1,0:T(8,128)(2,1)S(1)}, bf16[32,2304]{1,0:T(8,128)(2,1)S(1)}, u32[]{:S(2)}, u32[]{:S(2)}) %collective-permute-start.14) | collective-permute-done | bytes 147488 | tf_op jit(solution)/shard_map/ppermute | solution.py:258
  83.0 1.7 %collective-permute-done.13 = bf16[32,2304]{1,0:T(8,128)(2,1)S(1)} collective-permute-done((bf16[32,2304]{1,0:T(8,128)(2,1)S(1)}, bf16[32,2304]{1,0:T(8,128)(2,1)S(1)}, u32[]{:S(2)}, u32[]{:S(2)}) %collective-permute-start.13) | collective-permute-done | bytes 147488 | tf_op jit(solution)/shard_map/ppermute | solution.py:258
  84.8 0.1 add_convert_fusion.1
  84.8 2.7 %collective-permute-start.18 = (bf16[32,2304]{1,0:T(8,128)(2,1)S(1)}, bf16[32,2304]{1,0:T(8,128)(2,1)S(1)}, u32[]{:S(2)}, u32[]{:S(2)}) collective-permute-start(bf16[32,2304]{1,0:T(8,128)(2,1)S(1)} %add_convert_fusion.1), channel_id=1, source_target_pairs={{0,24},{1,97},{2,26},{3,99},{4,28},{5,101},{6,30},{7,103},{8,16},{... | collective-permute-start | bytes 442376 | tf_op jit(solution)/shard_map/ppermute | solution.py:258
  87.5 2.1 %collective-permute-start.16 = (bf16[32,2304]{1,0:T(8,128)(2,1)S(1)}, bf16[32,2304]{1,0:T(8,128)(2,1)S(1)}, u32[]{:S(2)}, u32[]{:S(2)}) collective-permute-start(bf16[32,2304]{1,0:T(8,128)(2,1)S(1)} %add_convert_fusion.1), channel_id=1, source_target_pairs={{0,16},{1,65},{2,18},{3,67},{4,20},{5,69},{6,22},{7,71},{8,24},{9,... | collective-permute-start | bytes 442376 | tf_op jit(solution)/shard_map/ppermute | solution.py:258
  89.6 1.7 %collective-permute-done.18 = bf16[32,2304]{1,0:T(8,128)(2,1)S(1)} collective-permute-done((bf16[32,2304]{1,0:T(8,128)(2,1)S(1)}, bf16[32,2304]{1,0:T(8,128)(2,1)S(1)}, u32[]{:S(2)}, u32[]{:S(2)}) %collective-permute-start.18) | collective-permute-done | bytes 147488 | tf_op jit(solution)/shard_map/ppermute | solution.py:258
  91.3 1.4 %collective-permute-done.17 = bf16[32,2304]{1,0:T(8,128)(2,1)S(1)} collective-permute-done((bf16[32,2304]{1,0:T(8,128)(2,1)S(1)}, bf16[32,2304]{1,0:T(8,128)(2,1)S(1)}, u32[]{:S(2)}, u32[]{:S(2)}) %collective-permute-start.17) | collective-permute-done | bytes 147488 | tf_op jit(solution)/shard_map/ppermute | solution.py:258
  92.7 1.6 %collective-permute-done.16 = bf16[32,2304]{1,0:T(8,128)(2,1)S(1)} collective-permute-done((bf16[32,2304]{1,0:T(8,128)(2,1)S(1)}, bf16[32,2304]{1,0:T(8,128)(2,1)S(1)}, u32[]{:S(2)}, u32[]{:S(2)}) %collective-permute-start.16) | collective-permute-done | bytes 147488 | tf_op jit(solution)/shard_map/ppermute | solution.py:258
  94.3 0.1 add_convert_fusion.a_ref
  94.4 3.2 %collective-permute-start.21 = (bf16[32,2304]{1,0:T(8,128)(2,1)S(1)}, bf16[32,2304]{1,0:T(8,128)(2,1)S(1)}, u32[]{:S(2)}, u32[]{:S(2)}) collective-permute-start(bf16[32,2304]{1,0:T(8,128)(2,1)S(1)} %add_convert_fusion.a_ref), channel_id=1, source_target_pairs={{0,96},{1,7},{2,98},{3,5},{4,100},{5,3},{6,102},{7,1},{8,104},{9,1... | collective-permute-start | bytes 442376 | tf_op jit(solution)/shard_map/ppermute | solution.py:258
  97.6 1.6 %collective-permute-start.19 = (bf16[32,2304]{1,0:T(8,128)(2,1)S(1)}, bf16[32,2304]{1,0:T(8,128)(2,1)S(1)}, u32[]{:S(2)}, u32[]{:S(2)}) collective-permute-start(bf16[32,2304]{1,0:T(8,128)(2,1)S(1)} %add_convert_fusion.a_ref), channel_id=1, source_target_pairs={{0,64},{1,5},{2,66},{3,7},{4,68},{5,1},{6,70},{7,3},{8,72},{9,13},... | collective-permute-start | bytes 442376 | tf_op jit(solution)/shard_map/ppermute | solution.py:258
  99.2 1.7 %collective-permute-done.21.d_ref = bf16[32,2304]{1,0:T(8,128)(2,1)S(1)} collective-permute-done((bf16[32,2304]{1,0:T(8,128)(2,1)S(1)}, bf16[32,2304]{1,0:T(8,128)(2,1)S(1)}, u32[]{:S(2)}, u32[]{:S(2)}) %collective-permute-start.21) | collective-permute-done | bytes 147488 | tf_op jit(solution)/shard_map/ppermute | solution.py:258
  100.8 1.9 %collective-permute-done.20.c_ref = bf16[32,2304]{1,0:T(8,128)(2,1)S(1)} collective-permute-done((bf16[32,2304]{1,0:T(8,128)(2,1)S(1)}, bf16[32,2304]{1,0:T(8,128)(2,1)S(1)}, u32[]{:S(2)}, u32[]{:S(2)}) %collective-permute-start.20) | collective-permute-done | bytes 147488 | tf_op jit(solution)/shard_map/ppermute | solution.py:258
  102.8 1.5 %collective-permute-done.19.b_ref = bf16[32,2304]{1,0:T(8,128)(2,1)S(1)} collective-permute-done((bf16[32,2304]{1,0:T(8,128)(2,1)S(1)}, bf16[32,2304]{1,0:T(8,128)(2,1)S(1)}, u32[]{:S(2)}, u32[]{:S(2)}) %collective-permute-start.19) | collective-permute-done | bytes 147488 | tf_op jit(solution)/shard_map/ppermute | solution.py:258
  104.3 8.2 %residue.1 = (bf16[2304,2304]{1,0:T(8,128)(2,1)}, f32[32,2304]{1,0:T(8,128)}) custom-call(s32[9]{0:T(128)S(1)} %pad_add_fusion.meta_ref, bf16[32,2304]{1,0:T(8,128)(2,1)S(1)} %add_convert_fusion.a_ref, bf16[32,2304]{1,0:T(8,128)(2,1)S(1)} %collective-permute-done.19.b_ref, bf16[32,2304]{1,0:T(8,128)(2,1)S(1)} %collective-permute-done.20.c_ref, ...), custom_call_target="tpu_custom_call" | custom-call | tf_op jit(solution)/shard_map/residue/pallas_call | solution.py:234
  (19 shorter events, 0.1 us)
Async XLA Ops:
  1.4 0.9 copy-start.4
  2.3 19.9 %copy-start = (bf16[512,2304]{1,0:T(8,128)(2,1)S(1)}, bf16[512,2304]{1,0:T(8,128)(2,1)}, u32[]{:S(2)}) copy-start(bf16[512,2304]{1,0:T(8,128)(2,1)} %acts_ref.5) | copy-start | bytes 7077892
  2.3 19.9 %copy-start.1 = (bf16[512,2304]{1,0:T(8,128)(2,1)S(1)}, bf16[512,2304]{1,0:T(8,128)(2,1)}, u32[]{:S(2)}) copy-start(bf16[512,2304]{1,0:T(8,128)(2,1)} %grad_ref.5) | copy-start | bytes 7077892
  15.9 35.2 %copy-start.3 = (bf16[2304,1152]{1,0:T(8,128)(2,1)}, bf16[2304,1152]{1,0:T(8,128)(2,1)S(1)}, u32[]{:S(2)}) copy-start(bf16[2304,1152]{1,0:T(8,128)(2,1)S(1)} %get-tuple-element.16.err_ref) | copy-start | bytes 15925252
  15.9 44.2 %collective-permute-start.12 = (bf16[2304,1152]{1,0:T(8,128)(2,1)}, bf16[2304,1152]{1,0:T(8,128)(2,1)}, u32[]{:S(2)}, u32[]{:S(2)}) collective-permute-start(bf16[2304,1152]{1,0:T(8,128)(2,1)} %get-tuple-element.17), channel_id=1, source_target_pairs={{0,1},{1,0},{2,3},{3,2},{4,5},{5,4},{6,7},{7,6},{8,9},{9,8},{10,11... | collective-permute-start | bytes 15925256 | tf_op jit(solution)/shard_map/ppermute | solution.py:276
  15.9 6.3 %collective-permute-start = (bf16[32,2304]{1,0:T(8,128)(2,1)S(1)}, bf16[32,2304]{1,0:T(8,128)(2,1)S(1)}, u32[]{:S(2)}, u32[]{:S(2)}) collective-permute-start(bf16[32,2304]{1,0:T(8,128)(2,1)S(1)} %copy-done.4), channel_id=1, source_target_pairs={{0,1},{1,0},{2,3},{3,2},{4,5},{5,4},{6,7},{7,6},{8,9},{9,8},{10,11... | collective-permute-start | bytes 442376 | tf_op jit(solution)/shard_map/ppermute | solution.py:272
  24.1 1.5 %collective-permute-start.1 = (f32[16,2304]{1,0:T(8,128)S(1)}, f32[16,2304]{1,0:T(8,128)S(1)}, u32[]{:S(2)}, u32[]{:S(2)}) collective-permute-start(f32[16,2304]{1,0:T(8,128)S(1)} %get-tuple-element.15), channel_id=1, source_target_pairs={{0,1},{1,0},{2,3},{3,2},{4,5},{5,4},{6,7},{7,6},{8,9},{9,8},{10,11... | collective-permute-start | bytes 442376 | tf_op jit(solution)/shard_map/ppermute | solution.py:275
  25.6 6.4 %collective-permute-start.4 = (f32[16,2304]{1,0:T(8,128)S(1)}, f32[16,2304]{1,0:T(8,128)S(1)}, u32[]{:S(2)}, u32[]{:S(2)}) collective-permute-start(f32[16,2304]{1,0:T(8,128)S(1)} %add.48), channel_id=1, source_target_pairs={{0,6},{1,25},{2,4},{3,27},{4,2},{5,29},{6,0},{7,31},{8,14},{9,17},... | collective-permute-start | bytes 442376 | tf_op jit(solution)/shard_map/ppermute | solution.py:258
  28.5 5.1 %collective-permute-start.3 = (f32[16,2304]{1,0:T(8,128)S(1)}, f32[16,2304]{1,0:T(8,128)S(1)}, u32[]{:S(2)}, u32[]{:S(2)}) collective-permute-start(f32[16,2304]{1,0:T(8,128)S(1)} %add.48), channel_id=1, source_target_pairs={{0,2},{1,9},{2,0},{3,11},{4,6},{5,13},{6,4},{7,15},{8,10},{9,1},{1... | collective-permute-start | bytes 442376 | tf_op jit(solution)/shard_map/ppermute | solution.py:258
  28.8 6.6 %collective-permute-start.2 = (f32[16,2304]{1,0:T(8,128)S(1)}, f32[16,2304]{1,0:T(8,128)S(1)}, u32[]{:S(2)}, u32[]{:S(2)}) collective-permute-start(f32[16,2304]{1,0:T(8,128)S(1)} %add.48), channel_id=1, source_target_pairs={{0,4},{1,17},{2,6},{3,19},{4,0},{5,21},{6,2},{7,23},{8,12},{9,25},... | collective-permute-start | bytes 442376 | tf_op jit(solution)/shard_map/ppermute | solution.py:258
  35.4 6.4 %collective-permute-start.7 = (f32[16,2304]{1,0:T(8,128)S(1)}, f32[16,2304]{1,0:T(8,128)S(1)}, u32[]{:S(2)}, u32[]{:S(2)}) collective-permute-start(f32[16,2304]{1,0:T(8,128)S(1)} %add_add_fusion.2), channel_id=1, source_target_pairs={{0,24},{1,97},{2,26},{3,99},{4,28},{5,101},{6,30},{7,103},{8,16},{... | collective-permute-start | bytes 442376 | tf_op jit(solution)/shard_map/ppermute | solution.py:258
  38.5 5.1 %collective-permute-start.6 = (f32[16,2304]{1,0:T(8,128)S(1)}, f32[16,2304]{1,0:T(8,128)S(1)}, u32[]{:S(2)}, u32[]{:S(2)}) collective-permute-start(f32[16,2304]{1,0:T(8,128)S(1)} %add_add_fusion.2), channel_id=1, source_target_pairs={{0,8},{1,33},{2,10},{3,35},{4,12},{5,37},{6,14},{7,39},{8,0},{9,41... | collective-permute-start | bytes 442376 | tf_op jit(solution)/shard_map/ppermute | solution.py:258
  38.7 6.6 %collective-permute-start.5 = (f32[16,2304]{1,0:T(8,128)S(1)}, f32[16,2304]{1,0:T(8,128)S(1)}, u32[]{:S(2)}, u32[]{:S(2)}) collective-permute-start(f32[16,2304]{1,0:T(8,128)S(1)} %add_add_fusion.2), channel_id=1, source_target_pairs={{0,16},{1,65},{2,18},{3,67},{4,20},{5,69},{6,22},{7,71},{8,24},{9,... | collective-permute-start | bytes 442376 | tf_op jit(solution)/shard_map/ppermute | solution.py:258
  45.4 14.6 %collective-permute-start.10 = (f32[16,2304]{1,0:T(8,128)S(1)}, f32[16,2304]{1,0:T(8,128)S(1)}, u32[]{:S(2)}, u32[]{:S(2)}) collective-permute-start(f32[16,2304]{1,0:T(8,128)S(1)} %add_add_fusion.1), channel_id=1, source_target_pairs={{0,96},{1,7},{2,98},{3,5},{4,100},{5,3},{6,102},{7,1},{8,104},{9,1... | collective-permute-start | bytes 442376 | tf_op jit(solution)/shard_map/ppermute | solution.py:258
  49.5 10.5 %collective-permute-start.9 = (f32[16,2304]{1,0:T(8,128)S(1)}, f32[16,2304]{1,0:T(8,128)S(1)}, u32[]{:S(2)}, u32[]{:S(2)}) collective-permute-start(f32[16,2304]{1,0:T(8,128)S(1)} %add_add_fusion.1), channel_id=1, source_target_pairs={{0,32},{1,3},{2,34},{3,1},{4,36},{5,7},{6,38},{7,5},{8,40},{9,11},... | collective-permute-start | bytes 442376 | tf_op jit(solution)/shard_map/ppermute | solution.py:258
  49.5 10.5 %collective-permute-start.8 = (f32[16,2304]{1,0:T(8,128)S(1)}, f32[16,2304]{1,0:T(8,128)S(1)}, u32[]{:S(2)}, u32[]{:S(2)}) collective-permute-start(f32[16,2304]{1,0:T(8,128)S(1)} %add_add_fusion.1), channel_id=1, source_target_pairs={{0,64},{1,5},{2,66},{3,7},{4,68},{5,1},{6,70},{7,3},{8,72},{9,13},... | collective-permute-start | bytes 442376 | tf_op jit(solution)/shard_map/ppermute | solution.py:258
  51.0 9.1 %copy-start.2 = (bf16[512,2304]{1,0:T(8,128)(2,1)S(1)}, bf16[512,2304]{1,0:T(8,128)(2,1)}, u32[]{:S(2)}) copy-start(bf16[512,2304]{1,0:T(8,128)(2,1)} %grad_ref.5) | copy-start | bytes 7077892
  60.0 8.9 %collective-permute-start.11 = (f32[16,2304]{1,0:T(8,128)S(1)}, f32[16,2304]{1,0:T(8,128)S(1)}, u32[]{:S(2)}, u32[]{:S(2)}) collective-permute-start(f32[16,2304]{1,0:T(8,128)S(1)} %add_add_fusion.keep_ref), channel_id=1, source_target_pairs={{0,1},{1,0},{2,3},{3,2},{4,5},{5,4},{6,7},{7,6},{8,9},{9,8},{10,11... | collective-permute-start | bytes 442376 | tf_op jit(solution)/shard_map/ppermute | solution.py:280
  75.4 6.4 %collective-permute-start.15 = (bf16[32,2304]{1,0:T(8,128)(2,1)S(1)}, bf16[32,2304]{1,0:T(8,128)(2,1)S(1)}, u32[]{:S(2)}, u32[]{:S(2)}) collective-permute-start(bf16[32,2304]{1,0:T(8,128)(2,1)S(1)} %get-tuple-element.18), channel_id=1, source_target_pairs={{0,6},{1,25},{2,4},{3,27},{4,2},{5,29},{6,0},{7,31},{8,14},{9,17},... | collective-permute-start | bytes 442376 | tf_op jit(solution)/shard_map/ppermute | solution.py:258
  77.9 5.1 %collective-permute-start.14 = (bf16[32,2304]{1,0:T(8,128)(2,1)S(1)}, bf16[32,2304]{1,0:T(8,128)(2,1)S(1)}, u32[]{:S(2)}, u32[]{:S(2)}) collective-permute-start(bf16[32,2304]{1,0:T(8,128)(2,1)S(1)} %get-tuple-element.18), channel_id=1, source_target_pairs={{0,2},{1,9},{2,0},{3,11},{4,6},{5,13},{6,4},{7,15},{8,10},{9,1},{1... | collective-permute-start | bytes 442376 | tf_op jit(solution)/shard_map/ppermute | solution.py:258
  77.9 6.9 %collective-permute-start.13 = (bf16[32,2304]{1,0:T(8,128)(2,1)S(1)}, bf16[32,2304]{1,0:T(8,128)(2,1)S(1)}, u32[]{:S(2)}, u32[]{:S(2)}) collective-permute-start(bf16[32,2304]{1,0:T(8,128)(2,1)S(1)} %get-tuple-element.18), channel_id=1, source_target_pairs={{0,4},{1,17},{2,6},{3,19},{4,0},{5,21},{6,2},{7,23},{8,12},{9,25},... | collective-permute-start | bytes 442376 | tf_op jit(solution)/shard_map/ppermute | solution.py:258
  84.8 6.4 %collective-permute-start.18 = (bf16[32,2304]{1,0:T(8,128)(2,1)S(1)}, bf16[32,2304]{1,0:T(8,128)(2,1)S(1)}, u32[]{:S(2)}, u32[]{:S(2)}) collective-permute-start(bf16[32,2304]{1,0:T(8,128)(2,1)S(1)} %add_convert_fusion.1), channel_id=1, source_target_pairs={{0,24},{1,97},{2,26},{3,99},{4,28},{5,101},{6,30},{7,103},{8,16},{... | collective-permute-start | bytes 442376 | tf_op jit(solution)/shard_map/ppermute | solution.py:258
  87.5 5.1 %collective-permute-start.17 = (bf16[32,2304]{1,0:T(8,128)(2,1)S(1)}, bf16[32,2304]{1,0:T(8,128)(2,1)S(1)}, u32[]{:S(2)}, u32[]{:S(2)}) collective-permute-start(bf16[32,2304]{1,0:T(8,128)(2,1)S(1)} %add_convert_fusion.1), channel_id=1, source_target_pairs={{0,8},{1,33},{2,10},{3,35},{4,12},{5,37},{6,14},{7,39},{8,0},{9,41... | collective-permute-start | bytes 442376 | tf_op jit(solution)/shard_map/ppermute | solution.py:258
  87.5 6.8 %collective-permute-start.16 = (bf16[32,2304]{1,0:T(8,128)(2,1)S(1)}, bf16[32,2304]{1,0:T(8,128)(2,1)S(1)}, u32[]{:S(2)}, u32[]{:S(2)}) collective-permute-start(bf16[32,2304]{1,0:T(8,128)(2,1)S(1)} %add_convert_fusion.1), channel_id=1, source_target_pairs={{0,16},{1,65},{2,18},{3,67},{4,20},{5,69},{6,22},{7,71},{8,24},{9,... | collective-permute-start | bytes 442376 | tf_op jit(solution)/shard_map/ppermute | solution.py:258
  94.4 6.4 %collective-permute-start.21 = (bf16[32,2304]{1,0:T(8,128)(2,1)S(1)}, bf16[32,2304]{1,0:T(8,128)(2,1)S(1)}, u32[]{:S(2)}, u32[]{:S(2)}) collective-permute-start(bf16[32,2304]{1,0:T(8,128)(2,1)S(1)} %add_convert_fusion.a_ref), channel_id=1, source_target_pairs={{0,96},{1,7},{2,98},{3,5},{4,100},{5,3},{6,102},{7,1},{8,104},{9,1... | collective-permute-start | bytes 442376 | tf_op jit(solution)/shard_map/ppermute | solution.py:258
  97.6 5.1 %collective-permute-start.20 = (bf16[32,2304]{1,0:T(8,128)(2,1)S(1)}, bf16[32,2304]{1,0:T(8,128)(2,1)S(1)}, u32[]{:S(2)}, u32[]{:S(2)}) collective-permute-start(bf16[32,2304]{1,0:T(8,128)(2,1)S(1)} %add_convert_fusion.a_ref), channel_id=1, source_target_pairs={{0,32},{1,3},{2,34},{3,1},{4,36},{5,7},{6,38},{7,5},{8,40},{9,11},... | collective-permute-start | bytes 442376 | tf_op jit(solution)/shard_map/ppermute | solution.py:258
  97.6 6.6 %collective-permute-start.19 = (bf16[32,2304]{1,0:T(8,128)(2,1)S(1)}, bf16[32,2304]{1,0:T(8,128)(2,1)S(1)}, u32[]{:S(2)}, u32[]{:S(2)}) collective-permute-start(bf16[32,2304]{1,0:T(8,128)(2,1)S(1)} %add_convert_fusion.a_ref), channel_id=1, source_target_pairs={{0,64},{1,5},{2,66},{3,7},{4,68},{5,1},{6,70},{7,3},{8,72},{9,13},... | collective-permute-start | bytes 442376 | tf_op jit(solution)/shard_map/ppermute | solution.py:258

commit v2 on v0

v2 whole, which is shorter than its diff:
```python
import functools

import jax
import jax.numpy as jnp
from jax import lax
from jax.experimental import pallas as pl
from jax.experimental.pallas import tpu as pltpu
from jax.sharding import PartitionSpec as P

BF, F32 = jnp.bfloat16, jnp.float32
ROWS, WIDTH, HALF, RANK, TOK = 2304, 2304, 1152, 32, 512
PIECE, QUARTER, LANES = 288, 4, 128
BIG, SMALL = 768, 256
HI = lax.Precision.HIGHEST
AXES = ("dp", "tensor")

WHOLE = pl.BlockSpec(memory_space=pltpu.VMEM)
SCALARS = pl.BlockSpec(memory_space=pltpu.SMEM)
FAR = pl.BlockSpec(memory_space=pltpu.HBM)


def dot(a, b, dims, precision=None):
    return lax.dot_general(a, b, (dims, ((), ())), precision=precision, preferred_element_type=F32)


def in_vmem(x):
    return pltpu.with_memory_space_constraint(x, pltpu.VMEM)


def in_hbm(x):
    return pltpu.with_memory_space_constraint(x, pltpu.HBM)


def call(kernel, name, in_specs, outs, scratch=(), mib=16, flops=0, bytes_accessed=0, aliases=None):
    return pl.pallas_call(
        kernel,
        in_specs=in_specs,
        out_specs=[FAR if o.memory_space == pltpu.HBM else WHOLE for o in outs],
        out_shape=outs,
        scratch_shapes=list(scratch),
        compiler_params=pltpu.CompilerParams(vmem_limit_bytes=mib * 2**20),
        cost_estimate=pl.CostEstimate(flops=flops, bytes_accessed=bytes_accessed, transcendentals=0),
        name=name,
        input_output_aliases=aliases or {},
    )


def columns(who):
    return pl.ds(pl.multiple_of(who * HALF, LANES), HALF)


def regroup(order_ref, src_ref, dst_ref, first, rows=None):
    if rows is None:
        rows = pl.ds(0, src_ref.shape[0])
    lane = lax.broadcasted_iota(jnp.int32, (rows.size, LANES), 1)
    carry = None
    for k in range(QUARTER):
        piece = order_ref[first + k]
        start = pl.multiple_of(((piece * 9) // 4) * LANES, LANES)
        window = src_ref[rows, pl.ds(start, 3 * LANES)]
        shift = 32 * k - 32 * (piece % 4)
        window = pltpu.roll(window, jnp.where(shift < 0, shift + 3 * LANES, shift), 1)
        tile = (PIECE * k) // LANES
        tiles = [window[:, i * LANES : (i + 1) * LANES] for i in range(3)]
        if k:
            tiles[0] = jnp.where(lane < 32 * k, carry, tiles[0])
        carry = tiles[2]
        for i in range(3 if k == QUARTER - 1 else 2):
            dst_ref[rows, (tile + i) * LANES : (tile + i + 1) * LANES] = tiles[i]


def rows_at(i, size):
    return pl.ds(pl.multiple_of(i * size, size), size)


def load_kernel(far_order, far_fac, far_err, far_acts, far_grad, left_ref, own_ref, err_ref, acts_ref, grad_ref, fac, order_ref, sems):
    chunks = ROWS // BIG

    def fetch(i):
        rows = rows_at(i, BIG)
        return pltpu.make_async_copy(far_err.at[rows], err_ref.at[rows], sems.at[i])

    others = [
        pltpu.make_async_copy(src, dst, sems.at[chunks + n])
        for n, (src, dst) in enumerate(((far_fac, fac), (far_order, order_ref), (far_grad, grad_ref), (far_acts, acts_ref)))
    ]
    others[0].start()
    others[1].start()
    for i in range(chunks):
        fetch(i).start()
    others[2].start()
    others[3].start()
    me = lax.axis_index("tensor")
    others[0].wait()
    others[1].wait()

    @pl.loop(0, chunks)
    def _(i):
        fetch(i).wait()
        rows = rows_at(i, BIG)
        left_ref[:, rows] = dot(err_ref[rows, :], fac[...], ((1,), (1,))).T
        regroup(order_ref, err_ref, own_ref, me * QUARTER, rows)

    others[2].wait()
    others[3].wait()


def load_part(order, old_factor, old_error, acts, grad_out):
    return call(
        load_kernel,
        "load_part",
        [FAR] * 5,
        [
            pltpu.VMEM((RANK, ROWS), F32),
            pltpu.VMEM((ROWS, HALF), BF),
            pltpu.VMEM((ROWS, WIDTH), BF),
            pltpu.VMEM((TOK, ROWS), BF),
            pltpu.VMEM((TOK, WIDTH), BF),
        ],
        [
            pltpu.VMEM((RANK, WIDTH), BF),
            pltpu.SMEM((2 * QUARTER,), jnp.int32),
            pltpu.SemaphoreType.DMA((ROWS // BIG + 4,)),
        ],
        flops=2 * RANK * ROWS * WIDTH,
        bytes_accessed=2 * ROWS * WIDTH,
    )(in_hbm(order), in_hbm(old_factor), in_hbm(old_error), in_hbm(acts), in_hbm(grad_out))


def term_kernel(order_ref, fac_ref, other_ref, left_ref, acts_ref, grad_ref, keep_ref, give_ref, fac_new, total):
    me = lax.axis_index("tensor")
    regroup(order_ref, fac_ref, fac_new.at[:, columns(me)], me * QUARTER)
    regroup(order_ref, other_ref, fac_new.at[:, columns(1 - me)], me * QUARTER)
    u = dot(fac_new[...], grad_ref[...], ((1,), (1,)))
    high = u.astype(BF)
    low = (u - high.astype(F32)).astype(BF)
    both = dot(jnp.concatenate([high, low], 0), acts_ref[...], ((1,), (0,)))
    total[...] = left_ref[...] + (both[:RANK] + both[RANK:])
    half = RANK // 2
    keep_ref[...] = total[rows_at(me, half), :]
    give_ref[...] = total[rows_at(1 - me, half), :]


def term_part(order, old_factor, other_factor, left, acts, grad_out):
    half = pltpu.VMEM((RANK // 2, ROWS), F32)
    return call(
        term_kernel,
        "term_part",
        [SCALARS] + [WHOLE] * 5,
        [half, half],
        [pltpu.VMEM((RANK, WIDTH), BF), pltpu.VMEM((RANK, ROWS), F32)],
        flops=4 * RANK * ROWS * TOK,
        bytes_accessed=5 * 10**6,
    )(order, old_factor, other_factor, in_vmem(left), in_vmem(acts), in_vmem(grad_out))


def send_kernel(order_ref, after_ref, err_ref, send_ref):
    other = 1 - lax.axis_index("tensor")

    @pl.loop(0, ROWS // BIG)
    def _(i):
        regroup(order_ref, err_ref, send_ref, other * QUARTER, rows_at(i, BIG))


def send_part(order, after, err):
    return call(
        send_kernel,
        "send_part",
        [SCALARS, pl.BlockSpec(memory_space=pl.ANY), WHOLE],
        [pltpu.VMEM((ROWS, HALF), BF)],
        flops=10**9,
        bytes_accessed=4 * 10**6,
    )(order, after, in_vmem(err))[0]


def add_grad(acts_ref, grad_ref, who, err_ref, out_ref):
    @pl.loop(0, ROWS // BIG)
    def _(i):
        rows = pl.ds(pl.multiple_of(i * BIG, BIG), BIG)
        grad = dot(acts_ref[:, rows], grad_ref[:, columns(who)], ((0,), (0,)))
        out_ref[rows, :] = (grad + err_ref[rows, :].astype(F32)).astype(BF)


def half_kernel(other, after_ref, acts_ref, grad_ref, err_ref, out_ref):
    me = lax.axis_index("tensor")
    add_grad(acts_ref, grad_ref, 1 - me if other else me, err_ref, out_ref)


def corrected_half(other, after, acts, grad_out, err):
    return call(
        functools.partial(half_kernel, other),
        "corrected_other" if other else "corrected_own",
        [pl.BlockSpec(memory_space=pl.ANY)] + [WHOLE] * 3,
        [pltpu.VMEM((ROWS, HALF), BF)],
        flops=2 * TOK * ROWS * HALF,
        bytes_accessed=8 * 10**6,
    )(after, in_vmem(acts), in_vmem(grad_out), in_vmem(err))[0]


def right_kernel(keep_ref, took_ref, own_ref, other_ref, basis_ref, basis_b_ref, right_ref):
    me = lax.axis_index("tensor")
    keep, took = keep_ref[...], took_ref[...]
    sums = jnp.concatenate([jnp.where(me == 0, keep, took), jnp.where(me == 0, took, keep)], 0)
    gram = dot(sums, sums, ((1,), (1,)), HI)
    row = lax.broadcasted_iota(jnp.int32, (RANK, RANK), 0)
    col = lax.broadcasted_iota(jnp.int32, (RANK, RANK), 1)
    work = jnp.concatenate([gram, (row == col).astype(F32)], 1)
    row2 = lax.broadcasted_iota(jnp.int32, (RANK, 2 * RANK), 0)
    for k in range(RANK - 1):
        column = jnp.broadcast_to(work[:, k : k + 1], work.shape)
        pivot_row = work[k : k + 1, :] * (1.0 / column[k : k + 1, :])
        work = jnp.where(row2 > k, work - column * pivot_row, work)
    pivots = jnp.sum(jnp.where(row == col, work[:, :RANK], 0.0), 1, keepdims=True)
    inverse = work[:, RANK:] * lax.rsqrt(pivots)
    basis = dot(inverse, sums, ((1,), (0,)), HI)
    basis_ref[...] = basis
    basis_b = basis.astype(BF)
    basis_b_ref[...] = basis_b
    right_ref[:, columns(me)] = dot(basis_b, own_ref[...], ((1,), (0,))).astype(BF)
    right_ref[:, columns(1 - me)] = dot(basis_b, other_ref[...], ((1,), (0,))).astype(BF)


def right_part(keep, took, own, other):
    return call(
        right_kernel,
        "right_part",
        [WHOLE] * 4,
        [pltpu.VMEM((RANK, ROWS), F32), pltpu.VMEM((RANK, ROWS), BF), pltpu.VMEM((RANK, WIDTH), BF)],
        flops=2 * RANK * ROWS * WIDTH,
        bytes_accessed=2 * ROWS * WIDTH,
    )(keep, took, in_vmem(own), in_vmem(other))


STEP = 384


def residue_kernel(scale, a_ref, b_ref, c_ref, d_ref, basis_b_ref, own_ref, other_ref, err_ref, far_ref, fac_ref, fac_b, stage, sems, fac_sem):
    total = (a_ref[...].astype(F32) + b_ref[...].astype(F32)) + (c_ref[...].astype(F32) + d_ref[...].astype(F32))
    factor = total * scale
    fac_ref[...] = factor
    fac_copy = pltpu.make_async_copy(fac_ref, far_ref, fac_sem)
    fac_copy.start()
    fac_b[...] = factor.astype(BF)
    me = lax.axis_index("tensor")

    def store(i):
        rows = pl.ds(pl.multiple_of(i * STEP, STEP), STEP)
        return pltpu.make_async_copy(stage.at[rows], err_ref.at[rows], sems.at[i])

    @pl.loop(0, ROWS // STEP)
    def _(i):
        rows = pl.ds(pl.multiple_of(i * STEP, STEP), STEP)
        for src, who in ((own_ref, me), (other_ref, 1 - me)):
            approx = dot(basis_b_ref[:, rows], fac_b[:, columns(who)], ((0,), (0,)))
            stage[rows, columns(who)] = (src[rows, :].astype(F32) - approx).astype(BF)
        store(i).start()

    @pl.loop(0, ROWS // STEP)
    def _(i):
        store(i).wait()

    fac_copy.wait()


def residue(terms, basis_b, own, other, scale):
    return call(
        functools.partial(residue_kernel, scale),
        "residue",
        [WHOLE] * 7,
        [pltpu.HBM((ROWS, WIDTH), BF), pltpu.HBM((RANK, WIDTH), F32)],
        [
            pltpu.VMEM((RANK, WIDTH), F32),
            pltpu.VMEM((RANK, WIDTH), BF),
            pltpu.VMEM((ROWS, WIDTH), BF),
            pltpu.SemaphoreType.DMA((ROWS // STEP,)),
            pltpu.SemaphoreType.DMA,
        ],
        mib=24,
        flops=2 * RANK * ROWS * WIDTH,
        bytes_accessed=2 * ROWS * WIDTH,
    )(*terms, basis_b, in_vmem(own), in_vmem(other))


def ring_pairs(axes, flip):
    pairs = []
    for index in range(64):
        for core in range(2):
            pairs.append((index * 2 + core, (index ^ (flip << (2 * axes[core]))) * 2 + core))
    return pairs


STAGES = ((0, 1), (1, 2), (2, 0))
SWAP = [(0, 1), (1, 0)]


def spread(x, axes):
    return [x] + [lax.ppermute(x, AXES, ring_pairs(axes, flip)) for flip in (2, 1, 3)]


def add4(terms):
    a, b, c, d = (t.astype(F32) for t in terms)
    return (a + b) + (c + d)


def add_kernel(a_ref, b_ref, c_ref, d_ref, work_ref, sum_ref, work_out_ref):
    sum_ref[...] = (a_ref[...] + b_ref[...]) + (c_ref[...] + d_ref[...])


def add_after(terms, work):
    return call(
        add_kernel,
        "add_terms",
        [WHOLE] * 4 + [pl.BlockSpec(memory_space=pl.ANY)],
        [pltpu.VMEM(terms[0].shape, F32), pltpu.VMEM(work.shape, work.dtype)],
        bytes_accessed=10**6,
        aliases={4: 1},
    )(*terms, in_vmem(work))


def body(acts, grad_out, old_error, old_factor, piece_order):
    other_factor = lax.ppermute(old_factor, "tensor", SWAP)
    left, own_err, err, acts, grad_out = load_part(piece_order, old_factor, old_error, acts, grad_out)
    keep, give = term_part(piece_order, old_factor, other_factor, left, acts, grad_out)
    part = keep + lax.ppermute(give, "tensor", SWAP)
    terms = spread(part, STAGES[0])
    part, send = add_after(terms, send_part(piece_order, part, err))
    other_err = lax.ppermute(send, "tensor", SWAP)
    terms = spread(part, STAGES[1])
    part, own = add_after(terms, corrected_half(False, part, acts, grad_out, own_err))
    terms = spread(part, STAGES[2])
    part, other = add_after(terms, corrected_half(True, part, acts, grad_out, other_err))
    basis_t, basis_b, right = right_part(part, lax.ppermute(part, "tensor", SWAP), own, other)
    for axes in STAGES[:-1]:
        right = add4(spread(right, axes)).astype(BF)
    terms = spread(right, STAGES[-1])
    new_error, new_factor = residue(terms, basis_b, own, other, 1.0 / lax.axis_size("dp"))
    return (new_error, basis_t.T, new_factor)


def solution(mesh):
    return jax.shard_map(
        body,
        mesh=mesh,
        in_specs=(P("dp", None), P("dp", "tensor"), P("dp", "tensor"), P(None, "tensor"), P()),
        out_specs=(P("dp", "tensor"), P(), P(None, "tensor")),
        check_vma=False,
    )
```

time: 422 us -> 82.4 us (0.20)
  waiting for transfers between devices: 276 us -> 20.4 us
  local copies, waits for them, and re-layouts: 49.3 us -> 0.72 us
  matrix products: 38.9 us -> 0 us
  other arithmetic: 31.2 us -> 0.17 us
  Pallas kernels: 0 us -> 29.1 us
  starting transfers between devices: 11.6 us -> 30.4 us
  between operations: 14.2 us -> 0.82 us
    psum x2 -> x0, waiting for transfers between devices: 269 us -> none  [the longest x1 145 us: body(): sums = lax.psum(left_term, ('dp', 'tensor'))]
    dot_general x5 -> x0, matrix products: 37.5 us -> none  [the longest x1 13.1 us: body(): lax.dot_general(acts, grad_out, (((0,), (0,)), ((), ())), preferred_eleme...]
    ppermute x0 -> x22, starting transfers between devices: none -> 30.4 us  [the longest x18 29.6 us: spread(): lax.ppermute(x, AXES, ring_pairs(axes, flip))]
    pallas_call x0 -> x10, Pallas kernels: none -> 29.1 us  [the longest x2 7.4 us: corrected_half(): call(functools.partial(half_kernel, other), 'corrected_other' if other el...]
    convert_element_type x1 -> x0, local copies, waits for them, and re-layouts: 22.1 us -> none  [body(): corrected = (grad + error.astype(jnp.float32)).astype(jnp.bfloat16)]
    ppermute x0 -> x22, waiting for transfers between devices: none -> 20.4 us  [the longest x18 18 us: spread(): lax.ppermute(x, AXES, ring_pairs(axes, flip))]
    unnamed x9 -> x5, local copies, waits for them, and re-layouts: 15.2 us -> 0.72 us
    convert_element_type x1 -> x2, other arithmetic: 11.7 us -> 0.15 us  [body(): right = add4(spread(right, axes)).astype(BF)]
  transfers between devices with their start and end apart: 4 -> 22, of which waited for: 3 -> 15; matrix products, arithmetic and copies ran while one was open for 9% -> 1% of each run, Pallas kernels for 0% -> 20%
where the time goes in v2:
time: 82.4 us; the launch traced here: 81.6 us
  starting transfers between devices  30.4 us (37%)
  Pallas kernels  29.1 us (35%)
  waiting for transfers between devices  20.4 us (25%)
    ppermute x18, starting transfers between devices, spread(): lax.ppermute(x, AXES, ring_pairs(axes, flip))  29.6 us
    ppermute x18, waiting for transfers between devices, spread(): lax.ppermute(x, AXES, ring_pairs(axes, flip))  18 us
    pallas_call x2, Pallas kernels, corrected_half(): call(functools.partial(half_kernel, other), 'corrected_other' if other el...  7.4 us
    pallas_call x1, Pallas kernels, load_part(): call(load_kernel, 'load_part', [FAR] * 5, [pltpu.VMEM((RANK, ROWS), F32),...  6.05 us
    pallas_call x1, Pallas kernels, right_part(): call(right_kernel, 'right_part', [WHOLE] * 4, [pltpu.VMEM((RANK, ROWS), F...  5.31 us
    pallas_call x1, Pallas kernels, residue(): call(functools.partial(residue_kernel, scale), 'residue', [WHOLE] * 7, [p...  5.25 us
    pallas_call x1, Pallas kernels, send_part(): call(send_kernel, 'send_part', [SCALARS, pl.BlockSpec(memory_space=pl.ANY...  3.13 us
    pallas_call x1, Pallas kernels, term_part(): call(term_kernel, 'term_part', [SCALARS] + [WHOLE] * 5, [half, half], [pl...  1.89 us
  transfers between devices with their start and end apart: 22, of which 15 were waited for; matrix products, arithmetic and copies ran while one was open for 1% of the time, Pallas kernels for 20%

profile of v2, /device:TPU:0, one launch (start us, length us, event | category | flops | bytes accessed | tf_op | source)
XLA Modules:
  0.0 81.6 jit_solution(11454914039646957936)
XLA Ops:
  0.7 0.1 collective-permute-start
  0.7 6.0 %load_part.1 = (f32[32,2304]{1,0:T(8,128)S(1)}, bf16[2304,1152]{1,0:T(8,128)(2,1)S(1)}, bf16[2304,2304]{1,0:T(8,128)(2,1)S(1)}, bf16[512,2304]{1,0:T(8,128)(2,1)S(1)}, bf16[512,2304]{1,0:T(8,128)(2,1)S(1)}) custom-call(s32[8]{0:T(128)} %order_ref.3, bf16[32,2304]{1,0:T(8,128)(2,1)} %fac_ref.1, bf16[2304,2304]{1,0:T(8,128)(2,1)} %far_err.1, ...), custom_call_target="tpu_custom_call" | custom-call | flops 339738624 | bytes 10616832 | tf_op jit(solution)/shard_map/load_part/pallas_call | solution.py:109
  6.8 0.0 collective-permute-done.other_ref
  6.8 1.9 %term_part.1 = (f32[16,2304]{1,0:T(8,128)S(1)}, f32[16,2304]{1,0:T(8,128)S(1)}) custom-call(s32[8]{0:T(128)S(1)} %copy-done.1, bf16[32,2304]{1,0:T(8,128)(2,1)S(1)} %copy-done, bf16[32,2304]{1,0:T(8,128)(2,1)S(1)} %collective-permute-done.other_ref, f32[32,2304]{1,0:T(8,128)S(1)} %get-tuple-element.21.left_ref, ...), custom_call_target="tpu_custom_call" | custom-call | flops 150994944 | bytes 5000000 | tf_op jit(solution)/shard_map/term_part/pallas_call | solution.py:146
  8.7 0.6 collective-permute-start.1
  9.3 1.0 %collective-permute-done.1 = f32[16,2304]{1,0:T(8,128)S(1)} collective-permute-done((f32[16,2304]{1,0:T(8,128)S(1)}, f32[16,2304]{1,0:T(8,128)S(1)}, u32[]{:S(2)}, u32[]{:S(2)}) %collective-permute-start.1) | collective-permute-done | bytes 147488 | tf_op jit(solution)/shard_map/ppermute | solution.py:324
  10.4 2.9 %collective-permute-start.4 = (f32[16,2304]{1,0:T(8,128)S(1)}, f32[16,2304]{1,0:T(8,128)S(1)}, u32[]{:S(2)}, u32[]{:S(2)}) collective-permute-start(f32[16,2304]{1,0:T(8,128)S(1)} %add.21.after_ref.a_ref), channel_id=1, source_target_pairs={{0,6},{1,25},{2,4},{3,27},{4,2},{5,29},{6,0},{7,31},{8,14},{9,17},... | collective-permute-start | bytes 442376 | tf_op jit(solution)/shard_map/ppermute | solution.py:297
  13.3 0.2 collective-permute-start.3
  13.5 1.6 %collective-permute-start.2 = (f32[16,2304]{1,0:T(8,128)S(1)}, f32[16,2304]{1,0:T(8,128)S(1)}, u32[]{:S(2)}, u32[]{:S(2)}) collective-permute-start(f32[16,2304]{1,0:T(8,128)S(1)} %add.21.after_ref.a_ref), channel_id=1, source_target_pairs={{0,4},{1,17},{2,6},{3,19},{4,0},{5,21},{6,2},{7,23},{8,12},{9,25},... | collective-permute-start | bytes 442376 | tf_op jit(solution)/shard_map/ppermute | solution.py:297
  15.1 3.1 %send_part.1.work_ref = bf16[2304,1152]{1,0:T(8,128)(2,1)S(1)} custom-call(s32[8]{0:T(128)S(1)} %copy-done.1, f32[16,2304]{1,0:T(8,128)S(1)} %add.21.after_ref.a_ref, bf16[2304,2304]{1,0:T(8,128)(2,1)S(1)} %get-tuple-element.26.err_ref), custom_call_target="tpu_custom_call" | custom-call | flops 1000000000 | bytes 4000000 | tf_op jit(solution)/shard_map/send_part/pallas_call | solution.py:166
  18.3 0.1 collective-permute-done.3.c_ref
  18.4 1.7 %collective-permute-done.2.b_ref = f32[16,2304]{1,0:T(8,128)S(1)} collective-permute-done((f32[16,2304]{1,0:T(8,128)S(1)}, f32[16,2304]{1,0:T(8,128)S(1)}, u32[]{:S(2)}, u32[]{:S(2)}) %collective-permute-start.2) | collective-permute-done | bytes 147488 | tf_op jit(solution)/shard_map/ppermute | solution.py:297
  20.2 0.1 collective-permute-start.11
  20.3 3.1 %collective-permute-start.7 = (f32[16,2304]{1,0:T(8,128)S(1)}, f32[16,2304]{1,0:T(8,128)S(1)}, u32[]{:S(2)}, u32[]{:S(2)}) collective-permute-start(f32[16,2304]{1,0:T(8,128)S(1)} %get-tuple-element.27.after_ref.a_ref), channel_id=1, source_target_pairs={{0,24},{1,97},{2,26},{3,99},{4,28},{5,101},{6,30},{7,103},{8,16},{... | collective-permute-start | bytes 442376 | tf_op jit(solution)/shard_map/ppermute | solution.py:297
  23.4 0.1 collective-permute-start.6
  23.5 1.6 %collective-permute-start.5 = (f32[16,2304]{1,0:T(8,128)S(1)}, f32[16,2304]{1,0:T(8,128)S(1)}, u32[]{:S(2)}, u32[]{:S(2)}) collective-permute-start(f32[16,2304]{1,0:T(8,128)S(1)} %get-tuple-element.27.after_ref.a_ref), channel_id=1, source_target_pairs={{0,16},{1,65},{2,18},{3,67},{4,20},{5,69},{6,22},{7,71},{8,24},{9,... | collective-permute-start | bytes 442376 | tf_op jit(solution)/shard_map/ppermute | solution.py:297
  25.1 3.7 %corrected_own.1.work_ref = bf16[2304,1152]{1,0:T(8,128)(2,1)S(1)} custom-call(f32[16,2304]{1,0:T(8,128)S(1)} %get-tuple-element.27.after_ref.a_ref, bf16[512,2304]{1,0:T(8,128)(2,1)S(1)} %get-tuple-element.22.acts_ref, bf16[512,2304]{1,0:T(8,128)(2,1)S(1)} %get-tuple-element.23.grad_ref, bf16[2304,1152]{1,0:T(8,128)(2,1)S(1)} %get-tuple-element.28.err_ref), custom_call_target="tpu_custom_call" | custom-call | flops 2717908992 | bytes 8000000 | tf_op jit(solution)/shard_map/corrected_own/pallas_call | solution.py:190
  28.8 0.0 collective-permute-done.7.d_ref
  28.8 0.0 collective-permute-done.6.c_ref
  28.8 1.4 %collective-permute-done.5.b_ref = f32[16,2304]{1,0:T(8,128)S(1)} collective-permute-done((f32[16,2304]{1,0:T(8,128)S(1)}, f32[16,2304]{1,0:T(8,128)S(1)}, u32[]{:S(2)}, u32[]{:S(2)}) %collective-permute-start.5) | collective-permute-done | bytes 147488 | tf_op jit(solution)/shard_map/ppermute | solution.py:297
  30.2 4.1 %collective-permute-start.10 = (f32[16,2304]{1,0:T(8,128)S(1)}, f32[16,2304]{1,0:T(8,128)S(1)}, u32[]{:S(2)}, u32[]{:S(2)}) collective-permute-start(f32[16,2304]{1,0:T(8,128)S(1)} %get-tuple-element.29.after_ref.a_ref), channel_id=1, source_target_pairs={{0,96},{1,7},{2,98},{3,5},{4,100},{5,3},{6,102},{7,1},{8,104},{9,1... | collective-permute-start | bytes 442376 | tf_op jit(solution)/shard_map/ppermute | solution.py:297
  34.3 0.0 collective-permute-start.9
  34.3 1.6 %collective-permute-start.8 = (f32[16,2304]{1,0:T(8,128)S(1)}, f32[16,2304]{1,0:T(8,128)S(1)}, u32[]{:S(2)}, u32[]{:S(2)}) collective-permute-start(f32[16,2304]{1,0:T(8,128)S(1)} %get-tuple-element.29.after_ref.a_ref), channel_id=1, source_target_pairs={{0,64},{1,5},{2,66},{3,7},{4,68},{5,1},{6,70},{7,3},{8,72},{9,13},... | collective-permute-start | bytes 442376 | tf_op jit(solution)/shard_map/ppermute | solution.py:297
  35.9 3.7 %corrected_other.1.work_ref = bf16[2304,1152]{1,0:T(8,128)(2,1)S(1)} custom-call(f32[16,2304]{1,0:T(8,128)S(1)} %get-tuple-element.29.after_ref.a_ref, bf16[512,2304]{1,0:T(8,128)(2,1)S(1)} %get-tuple-element.22.acts_ref, bf16[512,2304]{1,0:T(8,128)(2,1)S(1)} %get-tuple-element.23.grad_ref, bf16[2304,1152]{1,0:T(8,128)(2,1)S(1)} %collective-permute-done.11.err_ref), custom_call_target="tpu_custom_call" | custom-call | flops 2717908992 | bytes 8000000 | tf_op jit(solution)/shard_map/corrected_other/pallas_call | solution.py:190
  39.6 0.0 collective-permute-done.10.d_ref
  39.6 1.3 %collective-permute-done.8.b_ref = f32[16,2304]{1,0:T(8,128)S(1)} collective-permute-done((f32[16,2304]{1,0:T(8,128)S(1)}, f32[16,2304]{1,0:T(8,128)S(1)}, u32[]{:S(2)}, u32[]{:S(2)}) %collective-permute-start.8) | collective-permute-done | bytes 147488 | tf_op jit(solution)/shard_map/ppermute | solution.py:297
  41.0 0.1 collective-permute-start.12
  41.1 1.4 %collective-permute-done.12.took_ref = f32[16,2304]{1,0:T(8,128)S(1)} collective-permute-done((f32[16,2304]{1,0:T(8,128)S(1)}, f32[16,2304]{1,0:T(8,128)S(1)}, u32[]{:S(2)}, u32[]{:S(2)}) %collective-permute-start.12) | collective-permute-done | bytes 147488 | tf_op jit(solution)/shard_map/ppermute | solution.py:332
  42.5 5.3 %right_part.1 = (f32[32,2304]{1,0:T(8,128)S(1)}, bf16[32,2304]{1,0:T(8,128)(2,1)S(1)}, bf16[32,2304]{1,0:T(8,128)(2,1)S(1)}) custom-call(f32[16,2304]{1,0:T(8,128)S(1)} %get-tuple-element.31.keep_ref, f32[16,2304]{1,0:T(8,128)S(1)} %collective-permute-done.12.took_ref, bf16[2304,1152]{1,0:T(8,128)(2,1)S(1)} %get-tuple-element.32.own_ref, ...), custom_call_target="tpu_custom_call" | custom-call | flops 339738624 | bytes 10616832 | tf_op jit(solution)/shard_map/right_part/pallas_call | solution.py:224
  47.8 2.6 %collective-permute-start.15 = (bf16[32,2304]{1,0:T(8,128)(2,1)S(1)}, bf16[32,2304]{1,0:T(8,128)(2,1)S(1)}, u32[]{:S(2)}, u32[]{:S(2)}) collective-permute-start(bf16[32,2304]{1,0:T(8,128)(2,1)S(1)} %get-tuple-element.34), channel_id=1, source_target_pairs={{0,6},{1,25},{2,4},{3,27},{4,2},{5,29},{6,0},{7,31},{8,14},{9,17},... | collective-permute-start | bytes 442376 | tf_op jit(solution)/shard_map/ppermute | solution.py:297
  50.4 2.2 %collective-permute-start.13 = (bf16[32,2304]{1,0:T(8,128)(2,1)S(1)}, bf16[32,2304]{1,0:T(8,128)(2,1)S(1)}, u32[]{:S(2)}, u32[]{:S(2)}) collective-permute-start(bf16[32,2304]{1,0:T(8,128)(2,1)S(1)} %get-tuple-element.34), channel_id=1, source_target_pairs={{0,4},{1,17},{2,6},{3,19},{4,0},{5,21},{6,2},{7,23},{8,12},{9,25},... | collective-permute-start | bytes 442376 | tf_op jit(solution)/shard_map/ppermute | solution.py:297
  52.6 1.7 %collective-permute-done.15 = bf16[32,2304]{1,0:T(8,128)(2,1)S(1)} collective-permute-done((bf16[32,2304]{1,0:T(8,128)(2,1)S(1)}, bf16[32,2304]{1,0:T(8,128)(2,1)S(1)}, u32[]{:S(2)}, u32[]{:S(2)}) %collective-permute-start.15) | collective-permute-done | bytes 147488 | tf_op jit(solution)/shard_map/ppermute | solution.py:297
  54.2 1.3 %collective-permute-done.14 = bf16[32,2304]{1,0:T(8,128)(2,1)S(1)} collective-permute-done((bf16[32,2304]{1,0:T(8,128)(2,1)S(1)}, bf16[32,2304]{1,0:T(8,128)(2,1)S(1)}, u32[]{:S(2)}, u32[]{:S(2)}) %collective-permute-start.14) | collective-permute-done | bytes 147488 | tf_op jit(solution)/shard_map/ppermute | solution.py:297
  55.5 1.7 %collective-permute-done.13 = bf16[32,2304]{1,0:T(8,128)(2,1)S(1)} collective-permute-done((bf16[32,2304]{1,0:T(8,128)(2,1)S(1)}, bf16[32,2304]{1,0:T(8,128)(2,1)S(1)}, u32[]{:S(2)}, u32[]{:S(2)}) %collective-permute-start.13) | collective-permute-done | bytes 147488 | tf_op jit(solution)/shard_map/ppermute | solution.py:297
  57.3 0.1 add_convert_fusion.1
  57.3 2.7 %collective-permute-start.18 = (bf16[32,2304]{1,0:T(8,128)(2,1)S(1)}, bf16[32,2304]{1,0:T(8,128)(2,1)S(1)}, u32[]{:S(2)}, u32[]{:S(2)}) collective-permute-start(bf16[32,2304]{1,0:T(8,128)(2,1)S(1)} %add_convert_fusion.1), channel_id=1, source_target_pairs={{0,24},{1,97},{2,26},{3,99},{4,28},{5,101},{6,30},{7,103},{8,16},{... | collective-permute-start | bytes 442376 | tf_op jit(solution)/shard_map/ppermute | solution.py:297
  60.0 2.1 %collective-permute-start.16 = (bf16[32,2304]{1,0:T(8,128)(2,1)S(1)}, bf16[32,2304]{1,0:T(8,128)(2,1)S(1)}, u32[]{:S(2)}, u32[]{:S(2)}) collective-permute-start(bf16[32,2304]{1,0:T(8,128)(2,1)S(1)} %add_convert_fusion.1), channel_id=1, source_target_pairs={{0,16},{1,65},{2,18},{3,67},{4,20},{5,69},{6,22},{7,71},{8,24},{9,... | collective-permute-start | bytes 442376 | tf_op jit(solution)/shard_map/ppermute | solution.py:297
  62.1 1.7 %collective-permute-done.18 = bf16[32,2304]{1,0:T(8,128)(2,1)S(1)} collective-permute-done((bf16[32,2304]{1,0:T(8,128)(2,1)S(1)}, bf16[32,2304]{1,0:T(8,128)(2,1)S(1)}, u32[]{:S(2)}, u32[]{:S(2)}) %collective-permute-start.18) | collective-permute-done | bytes 147488 | tf_op jit(solution)/shard_map/ppermute | solution.py:297
  63.8 1.4 %collective-permute-done.17 = bf16[32,2304]{1,0:T(8,128)(2,1)S(1)} collective-permute-done((bf16[32,2304]{1,0:T(8,128)(2,1)S(1)}, bf16[32,2304]{1,0:T(8,128)(2,1)S(1)}, u32[]{:S(2)}, u32[]{:S(2)}) %collective-permute-start.17) | collective-permute-done | bytes 147488 | tf_op jit(solution)/shard_map/ppermute | solution.py:297
  65.2 1.6 %collective-permute-done.16 = bf16[32,2304]{1,0:T(8,128)(2,1)S(1)} collective-permute-done((bf16[32,2304]{1,0:T(8,128)(2,1)S(1)}, bf16[32,2304]{1,0:T(8,128)(2,1)S(1)}, u32[]{:S(2)}, u32[]{:S(2)}) %collective-permute-start.16) | collective-permute-done | bytes 147488 | tf_op jit(solution)/shard_map/ppermute | solution.py:297
  66.8 0.1 add_convert_fusion.a_ref
  66.9 2.8 %collective-permute-start.21 = (bf16[32,2304]{1,0:T(8,128)(2,1)S(1)}, bf16[32,2304]{1,0:T(8,128)(2,1)S(1)}, u32[]{:S(2)}, u32[]{:S(2)}) collective-permute-start(bf16[32,2304]{1,0:T(8,128)(2,1)S(1)} %add_convert_fusion.a_ref), channel_id=1, source_target_pairs={{0,96},{1,7},{2,98},{3,5},{4,100},{5,3},{6,102},{7,1},{8,104},{9,1... | collective-permute-start | bytes 442376 | tf_op jit(solution)/shard_map/ppermute | solution.py:297
  69.7 2.0 %collective-permute-start.19 = (bf16[32,2304]{1,0:T(8,128)(2,1)S(1)}, bf16[32,2304]{1,0:T(8,128)(2,1)S(1)}, u32[]{:S(2)}, u32[]{:S(2)}) collective-permute-start(bf16[32,2304]{1,0:T(8,128)(2,1)S(1)} %add_convert_fusion.a_ref), channel_id=1, source_target_pairs={{0,64},{1,5},{2,66},{3,7},{4,68},{5,1},{6,70},{7,3},{8,72},{9,13},... | collective-permute-start | bytes 442376 | tf_op jit(solution)/shard_map/ppermute | solution.py:297
  71.7 0.7 copy.14
  72.4 0.9 %collective-permute-done.21.d_ref = bf16[32,2304]{1,0:T(8,128)(2,1)S(1)} collective-permute-done((bf16[32,2304]{1,0:T(8,128)(2,1)S(1)}, bf16[32,2304]{1,0:T(8,128)(2,1)S(1)}, u32[]{:S(2)}, u32[]{:S(2)}) %collective-permute-start.21) | collective-permute-done | bytes 147488 | tf_op jit(solution)/shard_map/ppermute | solution.py:297
  73.3 1.5 %collective-permute-done.20.c_ref = bf16[32,2304]{1,0:T(8,128)(2,1)S(1)} collective-permute-done((bf16[32,2304]{1,0:T(8,128)(2,1)S(1)}, bf16[32,2304]{1,0:T(8,128)(2,1)S(1)}, u32[]{:S(2)}, u32[]{:S(2)}) %collective-permute-start.20) | collective-permute-done | bytes 147488 | tf_op jit(solution)/shard_map/ppermute | solution.py:297
  74.9 1.5 %collective-permute-done.19.b_ref = bf16[32,2304]{1,0:T(8,128)(2,1)S(1)} collective-permute-done((bf16[32,2304]{1,0:T(8,128)(2,1)S(1)}, bf16[32,2304]{1,0:T(8,128)(2,1)S(1)}, u32[]{:S(2)}, u32[]{:S(2)}) %collective-permute-start.19) | collective-permute-done | bytes 147488 | tf_op jit(solution)/shard_map/ppermute | solution.py:297
  76.4 5.2 %residue.1 = (bf16[2304,2304]{1,0:T(8,128)(2,1)}, f32[32,2304]{1,0:T(8,128)}) custom-call(bf16[32,2304]{1,0:T(8,128)(2,1)S(1)} %add_convert_fusion.a_ref, bf16[32,2304]{1,0:T(8,128)(2,1)S(1)} %collective-permute-done.19.b_ref, bf16[32,2304]{1,0:T(8,128)(2,1)S(1)} %collective-permute-done.20.c_ref, bf16[32,2304]{1,0:T(8,128)(2,1)S(1)} %collective-permute-done.21.d_ref, ...), custom_call_target="tpu_custom_call" | custom-call | flops 339738624 | bytes 10616832 | tf_op jit(solution)/shard_map/residue/pallas_call | solution.py:266
  (14 shorter events, 0.1 us)
Async XLA Ops:
  0.6 6.2 %copy-start = (bf16[32,2304]{1,0:T(8,128)(2,1)S(1)}, bf16[32,2304]{1,0:T(8,128)(2,1)}, u32[]{:S(2)}) copy-start(bf16[32,2304]{1,0:T(8,128)(2,1)} %fac_ref.1) | copy-start | bytes 442372
  0.6 6.2 %copy-start.1 = (s32[8]{0:T(128)S(1)}, s32[8]{0:T(128)}, u32[]{:S(2)}) copy-start(s32[8]{0:T(128)} %order_ref.3) | copy-start | bytes 100
  0.7 6.1 %collective-permute-start = (bf16[32,2304]{1,0:T(8,128)(2,1)}, bf16[32,2304]{1,0:T(8,128)(2,1)S(1)}, u32[]{:S(2)}, u32[]{:S(2)}) collective-permute-start(bf16[32,2304]{1,0:T(8,128)(2,1)} %fac_ref.1), channel_id=1, source_target_pairs={{0,1},{1,0},{2,3},{3,2},{4,5},{5,4},{6,7},{7,6},{8,9},{9,8},{10,11... | collective-permute-start | bytes 442376 | tf_op jit(solution)/shard_map/ppermute | solution.py:321
  8.7 1.6 %collective-permute-start.1 = (f32[16,2304]{1,0:T(8,128)S(1)}, f32[16,2304]{1,0:T(8,128)S(1)}, u32[]{:S(2)}, u32[]{:S(2)}) collective-permute-start(f32[16,2304]{1,0:T(8,128)S(1)} %get-tuple-element.25), channel_id=1, source_target_pairs={{0,1},{1,0},{2,3},{3,2},{4,5},{5,4},{6,7},{7,6},{8,9},{9,8},{10,11... | collective-permute-start | bytes 442376 | tf_op jit(solution)/shard_map/ppermute | solution.py:324
  10.4 7.9 %collective-permute-start.4 = (f32[16,2304]{1,0:T(8,128)S(1)}, f32[16,2304]{1,0:T(8,128)S(1)}, u32[]{:S(2)}, u32[]{:S(2)}) collective-permute-start(f32[16,2304]{1,0:T(8,128)S(1)} %add.21.after_ref.a_ref), channel_id=1, source_target_pairs={{0,6},{1,25},{2,4},{3,27},{4,2},{5,29},{6,0},{7,31},{8,14},{9,17},... | collective-permute-start | bytes 442376 | tf_op jit(solution)/shard_map/ppermute | solution.py:297
  13.3 5.1 %collective-permute-start.3 = (f32[16,2304]{1,0:T(8,128)S(1)}, f32[16,2304]{1,0:T(8,128)S(1)}, u32[]{:S(2)}, u32[]{:S(2)}) collective-permute-start(f32[16,2304]{1,0:T(8,128)S(1)} %add.21.after_ref.a_ref), channel_id=1, source_target_pairs={{0,2},{1,9},{2,0},{3,11},{4,6},{5,13},{6,4},{7,15},{8,10},{9,1},{1... | collective-permute-start | bytes 442376 | tf_op jit(solution)/shard_map/ppermute | solution.py:297
  13.5 6.6 %collective-permute-start.2 = (f32[16,2304]{1,0:T(8,128)S(1)}, f32[16,2304]{1,0:T(8,128)S(1)}, u32[]{:S(2)}, u32[]{:S(2)}) collective-permute-start(f32[16,2304]{1,0:T(8,128)S(1)} %add.21.after_ref.a_ref), channel_id=1, source_target_pairs={{0,4},{1,17},{2,6},{3,19},{4,0},{5,21},{6,2},{7,23},{8,12},{9,25},... | collective-permute-start | bytes 442376 | tf_op jit(solution)/shard_map/ppermute | solution.py:297
  20.2 15.7 %collective-permute-start.11 = (bf16[2304,1152]{1,0:T(8,128)(2,1)S(1)}, bf16[2304,1152]{1,0:T(8,128)(2,1)S(1)}, u32[]{:S(2)}, u32[]{:S(2)}) collective-permute-start(bf16[2304,1152]{1,0:T(8,128)(2,1)S(1)} %get-tuple-element.30), channel_id=1, source_target_pairs={{0,1},{1,0},{2,3},{3,2},{4,5},{5,4},{6,7},{7,6},{8,9},{9,8},{10,11... | collective-permute-start | bytes 15925256 | tf_op jit(solution)/shard_map/ppermute | solution.py:327
  20.3 8.5 %collective-permute-start.7 = (f32[16,2304]{1,0:T(8,128)S(1)}, f32[16,2304]{1,0:T(8,128)S(1)}, u32[]{:S(2)}, u32[]{:S(2)}) collective-permute-start(f32[16,2304]{1,0:T(8,128)S(1)} %get-tuple-element.27.after_ref.a_ref), channel_id=1, source_target_pairs={{0,24},{1,97},{2,26},{3,99},{4,28},{5,101},{6,30},{7,103},{8,16},{... | collective-permute-start | bytes 442376 | tf_op jit(solution)/shard_map/ppermute | solution.py:297
  23.4 5.4 %collective-permute-start.6 = (f32[16,2304]{1,0:T(8,128)S(1)}, f32[16,2304]{1,0:T(8,128)S(1)}, u32[]{:S(2)}, u32[]{:S(2)}) collective-permute-start(f32[16,2304]{1,0:T(8,128)S(1)} %get-tuple-element.27.after_ref.a_ref), channel_id=1, source_target_pairs={{0,8},{1,33},{2,10},{3,35},{4,12},{5,37},{6,14},{7,39},{8,0},{9,41... | collective-permute-start | bytes 442376 | tf_op jit(solution)/shard_map/ppermute | solution.py:297
  23.5 6.6 %collective-permute-start.5 = (f32[16,2304]{1,0:T(8,128)S(1)}, f32[16,2304]{1,0:T(8,128)S(1)}, u32[]{:S(2)}, u32[]{:S(2)}) collective-permute-start(f32[16,2304]{1,0:T(8,128)S(1)} %get-tuple-element.27.after_ref.a_ref), channel_id=1, source_target_pairs={{0,16},{1,65},{2,18},{3,67},{4,20},{5,69},{6,22},{7,71},{8,24},{9,... | collective-permute-start | bytes 442376 | tf_op jit(solution)/shard_map/ppermute | solution.py:297
  30.2 9.4 %collective-permute-start.10 = (f32[16,2304]{1,0:T(8,128)S(1)}, f32[16,2304]{1,0:T(8,128)S(1)}, u32[]{:S(2)}, u32[]{:S(2)}) collective-permute-start(f32[16,2304]{1,0:T(8,128)S(1)} %get-tuple-element.29.after_ref.a_ref), channel_id=1, source_target_pairs={{0,96},{1,7},{2,98},{3,5},{4,100},{5,3},{6,102},{7,1},{8,104},{9,1... | collective-permute-start | bytes 442376 | tf_op jit(solution)/shard_map/ppermute | solution.py:297
  34.3 5.3 %collective-permute-start.9 = (f32[16,2304]{1,0:T(8,128)S(1)}, f32[16,2304]{1,0:T(8,128)S(1)}, u32[]{:S(2)}, u32[]{:S(2)}) collective-permute-start(f32[16,2304]{1,0:T(8,128)S(1)} %get-tuple-element.29.after_ref.a_ref), channel_id=1, source_target_pairs={{0,32},{1,3},{2,34},{3,1},{4,36},{5,7},{6,38},{7,5},{8,40},{9,11},... | collective-permute-start | bytes 442376 | tf_op jit(solution)/shard_map/ppermute | solution.py:297
  34.3 6.6 %collective-permute-start.8 = (f32[16,2304]{1,0:T(8,128)S(1)}, f32[16,2304]{1,0:T(8,128)S(1)}, u32[]{:S(2)}, u32[]{:S(2)}) collective-permute-start(f32[16,2304]{1,0:T(8,128)S(1)} %get-tuple-element.29.after_ref.a_ref), channel_id=1, source_target_pairs={{0,64},{1,5},{2,66},{3,7},{4,68},{5,1},{6,70},{7,3},{8,72},{9,13},... | collective-permute-start | bytes 442376 | tf_op jit(solution)/shard_map/ppermute | solution.py:297
  41.0 1.5 %collective-permute-start.12 = (f32[16,2304]{1,0:T(8,128)S(1)}, f32[16,2304]{1,0:T(8,128)S(1)}, u32[]{:S(2)}, u32[]{:S(2)}) collective-permute-start(f32[16,2304]{1,0:T(8,128)S(1)} %get-tuple-element.31.keep_ref), channel_id=1, source_target_pairs={{0,1},{1,0},{2,3},{3,2},{4,5},{5,4},{6,7},{7,6},{8,9},{9,8},{10,11... | collective-permute-start | bytes 442376 | tf_op jit(solution)/shard_map/ppermute | solution.py:332
  47.8 6.4 %collective-permute-start.15 = (bf16[32,2304]{1,0:T(8,128)(2,1)S(1)}, bf16[32,2304]{1,0:T(8,128)(2,1)S(1)}, u32[]{:S(2)}, u32[]{:S(2)}) collective-permute-start(bf16[32,2304]{1,0:T(8,128)(2,1)S(1)} %get-tuple-element.34), channel_id=1, source_target_pairs={{0,6},{1,25},{2,4},{3,27},{4,2},{5,29},{6,0},{7,31},{8,14},{9,17},... | collective-permute-start | bytes 442376 | tf_op jit(solution)/shard_map/ppermute | solution.py:297
  50.4 5.1 %collective-permute-start.14 = (bf16[32,2304]{1,0:T(8,128)(2,1)S(1)}, bf16[32,2304]{1,0:T(8,128)(2,1)S(1)}, u32[]{:S(2)}, u32[]{:S(2)}) collective-permute-start(bf16[32,2304]{1,0:T(8,128)(2,1)S(1)} %get-tuple-element.34), channel_id=1, source_target_pairs={{0,2},{1,9},{2,0},{3,11},{4,6},{5,13},{6,4},{7,15},{8,10},{9,1},{1... | collective-permute-start | bytes 442376 | tf_op jit(solution)/shard_map/ppermute | solution.py:297
  50.4 6.9 %collective-permute-start.13 = (bf16[32,2304]{1,0:T(8,128)(2,1)S(1)}, bf16[32,2304]{1,0:T(8,128)(2,1)S(1)}, u32[]{:S(2)}, u32[]{:S(2)}) collective-permute-start(bf16[32,2304]{1,0:T(8,128)(2,1)S(1)} %get-tuple-element.34), channel_id=1, source_target_pairs={{0,4},{1,17},{2,6},{3,19},{4,0},{5,21},{6,2},{7,23},{8,12},{9,25},... | collective-permute-start | bytes 442376 | tf_op jit(solution)/shard_map/ppermute | solution.py:297
  57.3 6.4 %collective-permute-start.18 = (bf16[32,2304]{1,0:T(8,128)(2,1)S(1)}, bf16[32,2304]{1,0:T(8,128)(2,1)S(1)}, u32[]{:S(2)}, u32[]{:S(2)}) collective-permute-start(bf16[32,2304]{1,0:T(8,128)(2,1)S(1)} %add_convert_fusion.1), channel_id=1, source_target_pairs={{0,24},{1,97},{2,26},{3,99},{4,28},{5,101},{6,30},{7,103},{8,16},{... | collective-permute-start | bytes 442376 | tf_op jit(solution)/shard_map/ppermute | solution.py:297
  60.0 5.1 %collective-permute-start.17 = (bf16[32,2304]{1,0:T(8,128)(2,1)S(1)}, bf16[32,2304]{1,0:T(8,128)(2,1)S(1)}, u32[]{:S(2)}, u32[]{:S(2)}) collective-permute-start(bf16[32,2304]{1,0:T(8,128)(2,1)S(1)} %add_convert_fusion.1), channel_id=1, source_target_pairs={{0,8},{1,33},{2,10},{3,35},{4,12},{5,37},{6,14},{7,39},{8,0},{9,41... | collective-permute-start | bytes 442376 | tf_op jit(solution)/shard_map/ppermute | solution.py:297
  60.0 6.8 %collective-permute-start.16 = (bf16[32,2304]{1,0:T(8,128)(2,1)S(1)}, bf16[32,2304]{1,0:T(8,128)(2,1)S(1)}, u32[]{:S(2)}, u32[]{:S(2)}) collective-permute-start(bf16[32,2304]{1,0:T(8,128)(2,1)S(1)} %add_convert_fusion.1), channel_id=1, source_target_pairs={{0,16},{1,65},{2,18},{3,67},{4,20},{5,69},{6,22},{7,71},{8,24},{9,... | collective-permute-start | bytes 442376 | tf_op jit(solution)/shard_map/ppermute | solution.py:297
  66.9 6.4 %collective-permute-start.21 = (bf16[32,2304]{1,0:T(8,128)(2,1)S(1)}, bf16[32,2304]{1,0:T(8,128)(2,1)S(1)}, u32[]{:S(2)}, u32[]{:S(2)}) collective-permute-start(bf16[32,2304]{1,0:T(8,128)(2,1)S(1)} %add_convert_fusion.a_ref), channel_id=1, source_target_pairs={{0,96},{1,7},{2,98},{3,5},{4,100},{5,3},{6,102},{7,1},{8,104},{9,1... | collective-permute-start | bytes 442376 | tf_op jit(solution)/shard_map/ppermute | solution.py:297
  69.7 5.1 %collective-permute-start.20 = (bf16[32,2304]{1,0:T(8,128)(2,1)S(1)}, bf16[32,2304]{1,0:T(8,128)(2,1)S(1)}, u32[]{:S(2)}, u32[]{:S(2)}) collective-permute-start(bf16[32,2304]{1,0:T(8,128)(2,1)S(1)} %add_convert_fusion.a_ref), channel_id=1, source_target_pairs={{0,32},{1,3},{2,34},{3,1},{4,36},{5,7},{6,38},{7,5},{8,40},{9,11},... | collective-permute-start | bytes 442376 | tf_op jit(solution)/shard_map/ppermute | solution.py:297
  69.7 6.6 %collective-permute-start.19 = (bf16[32,2304]{1,0:T(8,128)(2,1)S(1)}, bf16[32,2304]{1,0:T(8,128)(2,1)S(1)}, u32[]{:S(2)}, u32[]{:S(2)}) collective-permute-start(bf16[32,2304]{1,0:T(8,128)(2,1)S(1)} %add_convert_fusion.a_ref), channel_id=1, source_target_pairs={{0,64},{1,5},{2,66},{3,7},{4,68},{5,1},{6,70},{7,3},{8,72},{9,13},... | collective-permute-start | bytes 442376 | tf_op jit(solution)/shard_map/ppermute | solution.py:297

commit v3 on v2

--- a/solution.py
+++ b/solution.py
@@ -197,27 +197,50 @@
     )(after, in_vmem(acts), in_vmem(grad_out), in_vmem(err))[0]
 
 
+def split3(x):
+    terms = []
+    for _ in range(3):
+        terms.append(x.astype(BF))
+        x = x - terms[-1].astype(F32)
+    return jnp.concatenate(terms, 0)
+
+
+def inverse_factor(gram):
+    row = lax.broadcasted_iota(jnp.int32, (RANK, RANK), 0)
+    col = lax.broadcasted_iota(jnp.int32, (RANK, RANK), 1)
+    work = jnp.concatenate([gram, (row == col).astype(F32)], 1)
+    wide = lax.broadcasted_iota(jnp.int32, work.shape, 0)
+    for k in range(0, RANK, 2):
+        first = jnp.broadcast_to(work[:, k : k + 1], work.shape)
+        second = jnp.broadcast_to(work[:, k + 1 : k + 2], work.shape)
+        row0 = work[k : k + 1, :]
+        inv0 = 1.0 / first[k : k + 1, :]
+        ratio = first[k + 1 : k + 2, :] * inv0
+        row1 = work[k + 1 : k + 2, :] - ratio * row0
+        pivot1 = second[k + 1 : k + 2, :] - ratio * first[k + 1 : k + 2, :]
+        second = second - first * ratio
+        below = work - first * (row0 * inv0) - second * (row1 * (1.0 / pivot1))
+        work = jnp.where(wide > k + 1, below, jnp.where(wide == k + 1, row1, work))
+    pivots = jnp.sum(jnp.where(row == col, work[:, :RANK], 0.0), 1, keepdims=True)
+    return work[:, RANK:] * lax.rsqrt(pivots)
+
+
 def right_kernel(keep_ref, took_ref, own_ref, other_ref, basis_ref, basis_b_ref, right_ref):
     me = lax.axis_index("tensor")
     keep, took = keep_ref[...], took_ref[...]
     sums = jnp.concatenate([jnp.where(me == 0, keep, took), jnp.where(me == 0, took, keep)], 0)
     gram = dot(sums, sums, ((1,), (1,)), HI)
-    row = lax.broadcasted_iota(jnp.int32, (RANK, RANK), 0)
-    col = lax.broadcasted_iota(jnp.int32, (RANK, RANK), 1)
-    work = jnp.concatenate([gram, (row == col).astype(F32)], 1)
-    row2 = lax.broadcasted_iota(jnp.int32, (RANK, 2 * RANK), 0)
-    for k in range(RANK - 1):
-        column = jnp.broadcast_to(work[:, k : k + 1], work.shape)
-        pivot_row = work[k : k + 1, :] * (1.0 / column[k : k + 1, :])
-        work = jnp.where(row2 > k, work - column * pivot_row, work)
-    pivots = jnp.sum(jnp.where(row == col, work[:, :RANK], 0.0), 1, keepdims=True)
-    inverse = work[:, RANK:] * lax.rsqrt(pivots)
+    terms = split3(sums)
+    halves = []
+    for ref in (own_ref, other_ref):
+        x = dot(terms, ref[...], ((1,), (0,)))
+        halves.append(x[:RANK] + (x[RANK : 2 * RANK] + x[2 * RANK :]))
+    inverse = inverse_factor(gram)
     basis = dot(inverse, sums, ((1,), (0,)), HI)
     basis_ref[...] = basis
-    basis_b = basis.astype(BF)
-    basis_b_ref[...] = basis_b
-    right_ref[:, columns(me)] = dot(basis_b, own_ref[...], ((1,), (0,))).astype(BF)
-    right_ref[:, columns(1 - me)] = dot(basis_b, other_ref[...], ((1,), (0,))).astype(BF)
+    basis_b_ref[...] = basis.astype(BF)
+    for half, who in zip(halves, (me, 1 - me)):
+        right_ref[:, columns(who)] = dot(inverse, half, ((1,), (0,)), HI).astype(BF)
 
 
 def right_part(keep, took, own, other):
@@ -231,7 +254,7 @@
     )(keep, took, in_vmem(own), in_vmem(other))
 
 
-STEP = 384
+STEP = 192
 
 
 def residue_kernel(scale, a_ref, b_ref, c_ref, d_ref, basis_b_ref, own_ref, other_ref, err_ref, far_ref, fac_ref, fac_b, stage, sems, fac_sem):
@@ -240,25 +263,22 @@
     fac_ref[...] = factor
     fac_copy = pltpu.make_async_copy(fac_ref, far_ref, fac_sem)
     fac_copy.start()
-    fac_b[...] = factor.astype(BF)
-    me = lax.axis_index("tensor")
+    me = lax.axis_index("tensor")
+    fac_b[:, :HALF] = fac_ref[:, columns(me)].astype(BF)
+    fac_b[:, HALF:] = fac_ref[:, columns(1 - me)].astype(BF)
 
     def store(i):
-        rows = pl.ds(pl.multiple_of(i * STEP, STEP), STEP)
+        rows = pl.ds(i * STEP, STEP)
         return pltpu.make_async_copy(stage.at[rows], err_ref.at[rows], sems.at[i])
 
-    @pl.loop(0, ROWS // STEP)
-    def _(i):
-        rows = pl.ds(pl.multiple_of(i * STEP, STEP), STEP)
-        for src, who in ((own_ref, me), (other_ref, 1 - me)):
-            approx = dot(basis_b_ref[:, rows], fac_b[:, columns(who)], ((0,), (0,)))
+    for i in range(ROWS // STEP):
+        rows = pl.ds(i * STEP, STEP)
+        for n, (src, who) in enumerate(((own_ref, me), (other_ref, 1 - me))):
+            approx = dot(basis_b_ref[:, rows], fac_b[:, n * HALF : (n + 1) * HALF], ((0,), (0,)))
             stage[rows, columns(who)] = (src[rows, :].astype(F32) - approx).astype(BF)
         store(i).start()
-
-    @pl.loop(0, ROWS // STEP)
-    def _(i):
+    for i in range(ROWS // STEP):
         store(i).wait()
-
     fac_copy.wait()
 
 

time: 82.4 us -> 79.7 us (0.967)
  Pallas kernels: 29.1 us -> 26.2 us
    pallas_call x1, Pallas kernels: 5.31 us -> 3 us  [right_part(): call(right_kernel, 'right_part', [WHOLE] * 4, [pltpu.VMEM((RANK, ROWS), F...]
  transfers between devices with their start and end apart: 22 -> 22, of which waited for: 15 -> 15; matrix products, arithmetic and copies ran while one was open for 1% -> 1% of each run, Pallas kernels for 20% -> 21%
where the time goes in v3:
time: 79.7 us; the launch traced here: 79 us
  starting transfers between devices  30.6 us (38%)
  Pallas kernels  26.2 us (33%)
  waiting for transfers between devices  20.3 us (25%)
  between operations  0.98 us (1%)
    ppermute x18, starting transfers between devices, spread(): lax.ppermute(x, AXES, ring_pairs(axes, flip))  29.8 us
    ppermute x18, waiting for transfers between devices, spread(): lax.ppermute(x, AXES, ring_pairs(axes, flip))  18 us
    pallas_call x2, Pallas kernels, corrected_half(): call(functools.partial(half_kernel, other), 'corrected_other' if other el...  7.4 us
    pallas_call x1, Pallas kernels, load_part(): call(load_kernel, 'load_part', [FAR] * 5, [pltpu.VMEM((RANK, ROWS), F32),...  6.09 us
    pallas_call x1, Pallas kernels, residue(): call(functools.partial(residue_kernel, scale), 'residue', [WHOLE] * 7, [p...  4.59 us
    pallas_call x1, Pallas kernels, send_part(): call(send_kernel, 'send_part', [SCALARS, pl.BlockSpec(memory_space=pl.ANY...  3.17 us
    pallas_call x1, Pallas kernels, right_part(): call(right_kernel, 'right_part', [WHOLE] * 4, [pltpu.VMEM((RANK, ROWS), F...  3 us
    pallas_call x1, Pallas kernels, term_part(): call(term_kernel, 'term_part', [SCALARS] + [WHOLE] * 5, [half, half], [pl...  1.89 us
  transfers between devices with their start and end apart: 22, of which 15 were waited for; matrix products, arithmetic and copies ran while one was open for 1% of the time, Pallas kernels for 21%

profile of v3, /device:TPU:0, one launch (start us, length us, event | category | flops | bytes accessed | tf_op | source)
XLA Modules:
  0.0 79.0 jit_solution(9120634567197427987)
XLA Ops:
  0.7 0.1 collective-permute-start
  0.7 6.1 %load_part.1 = (f32[32,2304]{1,0:T(8,128)S(1)}, bf16[2304,1152]{1,0:T(8,128)(2,1)S(1)}, bf16[2304,2304]{1,0:T(8,128)(2,1)S(1)}, bf16[512,2304]{1,0:T(8,128)(2,1)S(1)}, bf16[512,2304]{1,0:T(8,128)(2,1)S(1)}) custom-call(s32[8]{0:T(128)} %order_ref.3, bf16[32,2304]{1,0:T(8,128)(2,1)} %fac_ref.1, bf16[2304,2304]{1,0:T(8,128)(2,1)} %far_err.1, ...), custom_call_target="tpu_custom_call" | custom-call | flops 339738624 | bytes 10616832 | tf_op jit(solution)/shard_map/load_part/pallas_call | solution.py:109
  6.8 0.0 collective-permute-done.other_ref
  6.9 1.9 %term_part.1 = (f32[16,2304]{1,0:T(8,128)S(1)}, f32[16,2304]{1,0:T(8,128)S(1)}) custom-call(s32[8]{0:T(128)S(1)} %copy-done.1, bf16[32,2304]{1,0:T(8,128)(2,1)S(1)} %copy-done, bf16[32,2304]{1,0:T(8,128)(2,1)S(1)} %collective-permute-done.other_ref, f32[32,2304]{1,0:T(8,128)S(1)} %get-tuple-element.21.left_ref, ...), custom_call_target="tpu_custom_call" | custom-call | flops 150994944 | bytes 5000000 | tf_op jit(solution)/shard_map/term_part/pallas_call | solution.py:146
  8.8 0.6 collective-permute-start.1
  9.3 1.0 %collective-permute-done.1 = f32[16,2304]{1,0:T(8,128)S(1)} collective-permute-done((f32[16,2304]{1,0:T(8,128)S(1)}, f32[16,2304]{1,0:T(8,128)S(1)}, u32[]{:S(2)}, u32[]{:S(2)}) %collective-permute-start.1) | collective-permute-done | bytes 147488 | tf_op jit(solution)/shard_map/ppermute | solution.py:344
  10.4 2.9 %collective-permute-start.4 = (f32[16,2304]{1,0:T(8,128)S(1)}, f32[16,2304]{1,0:T(8,128)S(1)}, u32[]{:S(2)}, u32[]{:S(2)}) collective-permute-start(f32[16,2304]{1,0:T(8,128)S(1)} %add.21.after_ref.a_ref), channel_id=1, source_target_pairs={{0,6},{1,25},{2,4},{3,27},{4,2},{5,29},{6,0},{7,31},{8,14},{9,17},... | collective-permute-start | bytes 442376 | tf_op jit(solution)/shard_map/ppermute | solution.py:317
  13.3 0.2 collective-permute-start.3
  13.5 1.6 %collective-permute-start.2 = (f32[16,2304]{1,0:T(8,128)S(1)}, f32[16,2304]{1,0:T(8,128)S(1)}, u32[]{:S(2)}, u32[]{:S(2)}) collective-permute-start(f32[16,2304]{1,0:T(8,128)S(1)} %add.21.after_ref.a_ref), channel_id=1, source_target_pairs={{0,4},{1,17},{2,6},{3,19},{4,0},{5,21},{6,2},{7,23},{8,12},{9,25},... | collective-permute-start | bytes 442376 | tf_op jit(solution)/shard_map/ppermute | solution.py:317
  15.1 3.2 %send_part.1.work_ref = bf16[2304,1152]{1,0:T(8,128)(2,1)S(1)} custom-call(s32[8]{0:T(128)S(1)} %copy-done.1, f32[16,2304]{1,0:T(8,128)S(1)} %add.21.after_ref.a_ref, bf16[2304,2304]{1,0:T(8,128)(2,1)S(1)} %get-tuple-element.26.err_ref), custom_call_target="tpu_custom_call" | custom-call | flops 1000000000 | bytes 4000000 | tf_op jit(solution)/shard_map/send_part/pallas_call | solution.py:166
  18.3 0.0 collective-permute-done.4.d_ref
  18.3 0.1 collective-permute-done.3.c_ref
  18.4 1.7 %collective-permute-done.2.b_ref = f32[16,2304]{1,0:T(8,128)S(1)} collective-permute-done((f32[16,2304]{1,0:T(8,128)S(1)}, f32[16,2304]{1,0:T(8,128)S(1)}, u32[]{:S(2)}, u32[]{:S(2)}) %collective-permute-start.2) | collective-permute-done | bytes 147488 | tf_op jit(solution)/shard_map/ppermute | solution.py:317
  20.2 0.1 collective-permute-start.11
  20.3 3.1 %collective-permute-start.7 = (f32[16,2304]{1,0:T(8,128)S(1)}, f32[16,2304]{1,0:T(8,128)S(1)}, u32[]{:S(2)}, u32[]{:S(2)}) collective-permute-start(f32[16,2304]{1,0:T(8,128)S(1)} %get-tuple-element.27.after_ref.a_ref), channel_id=1, source_target_pairs={{0,24},{1,97},{2,26},{3,99},{4,28},{5,101},{6,30},{7,103},{8,16},{... | collective-permute-start | bytes 442376 | tf_op jit(solution)/shard_map/ppermute | solution.py:317
  23.4 0.1 collective-permute-start.6
  23.5 1.6 %collective-permute-start.5 = (f32[16,2304]{1,0:T(8,128)S(1)}, f32[16,2304]{1,0:T(8,128)S(1)}, u32[]{:S(2)}, u32[]{:S(2)}) collective-permute-start(f32[16,2304]{1,0:T(8,128)S(1)} %get-tuple-element.27.after_ref.a_ref), channel_id=1, source_target_pairs={{0,16},{1,65},{2,18},{3,67},{4,20},{5,69},{6,22},{7,71},{8,24},{9,... | collective-permute-start | bytes 442376 | tf_op jit(solution)/shard_map/ppermute | solution.py:317
  25.1 3.7 %corrected_own.1.work_ref = bf16[2304,1152]{1,0:T(8,128)(2,1)S(1)} custom-call(f32[16,2304]{1,0:T(8,128)S(1)} %get-tuple-element.27.after_ref.a_ref, bf16[512,2304]{1,0:T(8,128)(2,1)S(1)} %get-tuple-element.22.acts_ref, bf16[512,2304]{1,0:T(8,128)(2,1)S(1)} %get-tuple-element.23.grad_ref, bf16[2304,1152]{1,0:T(8,128)(2,1)S(1)} %get-tuple-element.28.err_ref), custom_call_target="tpu_custom_call" | custom-call | flops 2717908992 | bytes 8000000 | tf_op jit(solution)/shard_map/corrected_own/pallas_call | solution.py:190
  28.8 0.0 collective-permute-done.6.c_ref
  28.8 1.4 %collective-permute-done.5.b_ref = f32[16,2304]{1,0:T(8,128)S(1)} collective-permute-done((f32[16,2304]{1,0:T(8,128)S(1)}, f32[16,2304]{1,0:T(8,128)S(1)}, u32[]{:S(2)}, u32[]{:S(2)}) %collective-permute-start.5) | collective-permute-done | bytes 147488 | tf_op jit(solution)/shard_map/ppermute | solution.py:317
  30.2 4.1 %collective-permute-start.10 = (f32[16,2304]{1,0:T(8,128)S(1)}, f32[16,2304]{1,0:T(8,128)S(1)}, u32[]{:S(2)}, u32[]{:S(2)}) collective-permute-start(f32[16,2304]{1,0:T(8,128)S(1)} %get-tuple-element.29.after_ref.a_ref), channel_id=1, source_target_pairs={{0,96},{1,7},{2,98},{3,5},{4,100},{5,3},{6,102},{7,1},{8,104},{9,1... | collective-permute-start | bytes 442376 | tf_op jit(solution)/shard_map/ppermute | solution.py:317
  34.3 1.6 %collective-permute-start.8 = (f32[16,2304]{1,0:T(8,128)S(1)}, f32[16,2304]{1,0:T(8,128)S(1)}, u32[]{:S(2)}, u32[]{:S(2)}) collective-permute-start(f32[16,2304]{1,0:T(8,128)S(1)} %get-tuple-element.29.after_ref.a_ref), channel_id=1, source_target_pairs={{0,64},{1,5},{2,66},{3,7},{4,68},{5,1},{6,70},{7,3},{8,72},{9,13},... | collective-permute-start | bytes 442376 | tf_op jit(solution)/shard_map/ppermute | solution.py:317
  35.9 0.0 collective-permute-done.11.err_ref
  35.9 3.7 %corrected_other.1.work_ref = bf16[2304,1152]{1,0:T(8,128)(2,1)S(1)} custom-call(f32[16,2304]{1,0:T(8,128)S(1)} %get-tuple-element.29.after_ref.a_ref, bf16[512,2304]{1,0:T(8,128)(2,1)S(1)} %get-tuple-element.22.acts_ref, bf16[512,2304]{1,0:T(8,128)(2,1)S(1)} %get-tuple-element.23.grad_ref, bf16[2304,1152]{1,0:T(8,128)(2,1)S(1)} %collective-permute-done.11.err_ref), custom_call_target="tpu_custom_call" | custom-call | flops 2717908992 | bytes 8000000 | tf_op jit(solution)/shard_map/corrected_other/pallas_call | solution.py:190
  39.6 1.3 %collective-permute-done.8.b_ref = f32[16,2304]{1,0:T(8,128)S(1)} collective-permute-done((f32[16,2304]{1,0:T(8,128)S(1)}, f32[16,2304]{1,0:T(8,128)S(1)}, u32[]{:S(2)}, u32[]{:S(2)}) %collective-permute-start.8) | collective-permute-done | bytes 147488 | tf_op jit(solution)/shard_map/ppermute | solution.py:317
  41.0 0.1 collective-permute-start.12
  41.1 1.4 %collective-permute-done.12.took_ref = f32[16,2304]{1,0:T(8,128)S(1)} collective-permute-done((f32[16,2304]{1,0:T(8,128)S(1)}, f32[16,2304]{1,0:T(8,128)S(1)}, u32[]{:S(2)}, u32[]{:S(2)}) %collective-permute-start.12) | collective-permute-done | bytes 147488 | tf_op jit(solution)/shard_map/ppermute | solution.py:352
  42.4 3.0 %right_part.1 = (f32[32,2304]{1,0:T(8,128)S(1)}, bf16[32,2304]{1,0:T(8,128)(2,1)S(1)}, bf16[32,2304]{1,0:T(8,128)(2,1)S(1)}) custom-call(f32[16,2304]{1,0:T(8,128)S(1)} %get-tuple-element.31.keep_ref, f32[16,2304]{1,0:T(8,128)S(1)} %collective-permute-done.12.took_ref, bf16[2304,1152]{1,0:T(8,128)(2,1)S(1)} %get-tuple-element.32.own_ref, ...), custom_call_target="tpu_custom_call" | custom-call | flops 339738624 | bytes 10616832 | tf_op jit(solution)/shard_map/right_part/pallas_call | solution.py:247
  45.5 2.6 %collective-permute-start.15 = (bf16[32,2304]{1,0:T(8,128)(2,1)S(1)}, bf16[32,2304]{1,0:T(8,128)(2,1)S(1)}, u32[]{:S(2)}, u32[]{:S(2)}) collective-permute-start(bf16[32,2304]{1,0:T(8,128)(2,1)S(1)} %get-tuple-element.34), channel_id=1, source_target_pairs={{0,6},{1,25},{2,4},{3,27},{4,2},{5,29},{6,0},{7,31},{8,14},{9,17},... | collective-permute-start | bytes 442376 | tf_op jit(solution)/shard_map/ppermute | solution.py:317
  48.1 0.0 collective-permute-start.14
  48.1 2.2 %collective-permute-start.13 = (bf16[32,2304]{1,0:T(8,128)(2,1)S(1)}, bf16[32,2304]{1,0:T(8,128)(2,1)S(1)}, u32[]{:S(2)}, u32[]{:S(2)}) collective-permute-start(bf16[32,2304]{1,0:T(8,128)(2,1)S(1)} %get-tuple-element.34), channel_id=1, source_target_pairs={{0,4},{1,17},{2,6},{3,19},{4,0},{5,21},{6,2},{7,23},{8,12},{9,25},... | collective-permute-start | bytes 442376 | tf_op jit(solution)/shard_map/ppermute | solution.py:317
  50.2 1.7 %collective-permute-done.15 = bf16[32,2304]{1,0:T(8,128)(2,1)S(1)} collective-permute-done((bf16[32,2304]{1,0:T(8,128)(2,1)S(1)}, bf16[32,2304]{1,0:T(8,128)(2,1)S(1)}, u32[]{:S(2)}, u32[]{:S(2)}) %collective-permute-start.15) | collective-permute-done | bytes 147488 | tf_op jit(solution)/shard_map/ppermute | solution.py:317
  51.9 1.3 %collective-permute-done.14 = bf16[32,2304]{1,0:T(8,128)(2,1)S(1)} collective-permute-done((bf16[32,2304]{1,0:T(8,128)(2,1)S(1)}, bf16[32,2304]{1,0:T(8,128)(2,1)S(1)}, u32[]{:S(2)}, u32[]{:S(2)}) %collective-permute-start.14) | collective-permute-done | bytes 147488 | tf_op jit(solution)/shard_map/ppermute | solution.py:317
  53.2 1.7 %collective-permute-done.13 = bf16[32,2304]{1,0:T(8,128)(2,1)S(1)} collective-permute-done((bf16[32,2304]{1,0:T(8,128)(2,1)S(1)}, bf16[32,2304]{1,0:T(8,128)(2,1)S(1)}, u32[]{:S(2)}, u32[]{:S(2)}) %collective-permute-start.13) | collective-permute-done | bytes 147488 | tf_op jit(solution)/shard_map/ppermute | solution.py:317
  54.9 0.1 add_convert_fusion.1
  55.0 2.9 %collective-permute-start.18 = (bf16[32,2304]{1,0:T(8,128)(2,1)S(1)}, bf16[32,2304]{1,0:T(8,128)(2,1)S(1)}, u32[]{:S(2)}, u32[]{:S(2)}) collective-permute-start(bf16[32,2304]{1,0:T(8,128)(2,1)S(1)} %add_convert_fusion.1), channel_id=1, source_target_pairs={{0,24},{1,97},{2,26},{3,99},{4,28},{5,101},{6,30},{7,103},{8,16},{... | collective-permute-start | bytes 442376 | tf_op jit(solution)/shard_map/ppermute | solution.py:317
  57.9 2.1 %collective-permute-start.16 = (bf16[32,2304]{1,0:T(8,128)(2,1)S(1)}, bf16[32,2304]{1,0:T(8,128)(2,1)S(1)}, u32[]{:S(2)}, u32[]{:S(2)}) collective-permute-start(bf16[32,2304]{1,0:T(8,128)(2,1)S(1)} %add_convert_fusion.1), channel_id=1, source_target_pairs={{0,16},{1,65},{2,18},{3,67},{4,20},{5,69},{6,22},{7,71},{8,24},{9,... | collective-permute-start | bytes 442376 | tf_op jit(solution)/shard_map/ppermute | solution.py:317
  60.0 1.7 %collective-permute-done.18 = bf16[32,2304]{1,0:T(8,128)(2,1)S(1)} collective-permute-done((bf16[32,2304]{1,0:T(8,128)(2,1)S(1)}, bf16[32,2304]{1,0:T(8,128)(2,1)S(1)}, u32[]{:S(2)}, u32[]{:S(2)}) %collective-permute-start.18) | collective-permute-done | bytes 147488 | tf_op jit(solution)/shard_map/ppermute | solution.py:317
  61.6 1.4 %collective-permute-done.17 = bf16[32,2304]{1,0:T(8,128)(2,1)S(1)} collective-permute-done((bf16[32,2304]{1,0:T(8,128)(2,1)S(1)}, bf16[32,2304]{1,0:T(8,128)(2,1)S(1)}, u32[]{:S(2)}, u32[]{:S(2)}) %collective-permute-start.17) | collective-permute-done | bytes 147488 | tf_op jit(solution)/shard_map/ppermute | solution.py:317
  63.0 1.6 %collective-permute-done.16 = bf16[32,2304]{1,0:T(8,128)(2,1)S(1)} collective-permute-done((bf16[32,2304]{1,0:T(8,128)(2,1)S(1)}, bf16[32,2304]{1,0:T(8,128)(2,1)S(1)}, u32[]{:S(2)}, u32[]{:S(2)}) %collective-permute-start.16) | collective-permute-done | bytes 147488 | tf_op jit(solution)/shard_map/ppermute | solution.py:317
  64.7 0.1 add_convert_fusion.a_ref
  64.7 2.8 %collective-permute-start.21 = (bf16[32,2304]{1,0:T(8,128)(2,1)S(1)}, bf16[32,2304]{1,0:T(8,128)(2,1)S(1)}, u32[]{:S(2)}, u32[]{:S(2)}) collective-permute-start(bf16[32,2304]{1,0:T(8,128)(2,1)S(1)} %add_convert_fusion.a_ref), channel_id=1, source_target_pairs={{0,96},{1,7},{2,98},{3,5},{4,100},{5,3},{6,102},{7,1},{8,104},{9,1... | collective-permute-start | bytes 442376 | tf_op jit(solution)/shard_map/ppermute | solution.py:317
  67.6 1.9 %collective-permute-start.19 = (bf16[32,2304]{1,0:T(8,128)(2,1)S(1)}, bf16[32,2304]{1,0:T(8,128)(2,1)S(1)}, u32[]{:S(2)}, u32[]{:S(2)}) collective-permute-start(bf16[32,2304]{1,0:T(8,128)(2,1)S(1)} %add_convert_fusion.a_ref), channel_id=1, source_target_pairs={{0,64},{1,5},{2,66},{3,7},{4,68},{5,1},{6,70},{7,3},{8,72},{9,13},... | collective-permute-start | bytes 442376 | tf_op jit(solution)/shard_map/ppermute | solution.py:317
  69.5 0.7 copy.14
  70.2 0.9 %collective-permute-done.21.d_ref = bf16[32,2304]{1,0:T(8,128)(2,1)S(1)} collective-permute-done((bf16[32,2304]{1,0:T(8,128)(2,1)S(1)}, bf16[32,2304]{1,0:T(8,128)(2,1)S(1)}, u32[]{:S(2)}, u32[]{:S(2)}) %collective-permute-start.21) | collective-permute-done | bytes 147488 | tf_op jit(solution)/shard_map/ppermute | solution.py:317
  71.2 1.5 %collective-permute-done.20.c_ref = bf16[32,2304]{1,0:T(8,128)(2,1)S(1)} collective-permute-done((bf16[32,2304]{1,0:T(8,128)(2,1)S(1)}, bf16[32,2304]{1,0:T(8,128)(2,1)S(1)}, u32[]{:S(2)}, u32[]{:S(2)}) %collective-permute-start.20) | collective-permute-done | bytes 147488 | tf_op jit(solution)/shard_map/ppermute | solution.py:317
  72.7 1.5 %collective-permute-done.19.b_ref = bf16[32,2304]{1,0:T(8,128)(2,1)S(1)} collective-permute-done((bf16[32,2304]{1,0:T(8,128)(2,1)S(1)}, bf16[32,2304]{1,0:T(8,128)(2,1)S(1)}, u32[]{:S(2)}, u32[]{:S(2)}) %collective-permute-start.19) | collective-permute-done | bytes 147488 | tf_op jit(solution)/shard_map/ppermute | solution.py:317
  74.2 4.6 %residue.1 = (bf16[2304,2304]{1,0:T(8,128)(2,1)}, f32[32,2304]{1,0:T(8,128)}) custom-call(bf16[32,2304]{1,0:T(8,128)(2,1)S(1)} %add_convert_fusion.a_ref, bf16[32,2304]{1,0:T(8,128)(2,1)S(1)} %collective-permute-done.19.b_ref, bf16[32,2304]{1,0:T(8,128)(2,1)S(1)} %collective-permute-done.20.c_ref, bf16[32,2304]{1,0:T(8,128)(2,1)S(1)} %collective-permute-done.21.d_ref, ...), custom_call_target="tpu_custom_call" | custom-call | flops 339738624 | bytes 10616832 | tf_op jit(solution)/shard_map/residue/pallas_call | solution.py:286
  (14 shorter events, 0.1 us)
Async XLA Ops:
  0.6 6.2 %copy-start = (bf16[32,2304]{1,0:T(8,128)(2,1)S(1)}, bf16[32,2304]{1,0:T(8,128)(2,1)}, u32[]{:S(2)}) copy-start(bf16[32,2304]{1,0:T(8,128)(2,1)} %fac_ref.1) | copy-start | bytes 442372
  0.6 6.2 %copy-start.1 = (s32[8]{0:T(128)S(1)}, s32[8]{0:T(128)}, u32[]{:S(2)}) copy-start(s32[8]{0:T(128)} %order_ref.3) | copy-start | bytes 100
  0.7 6.2 %collective-permute-start = (bf16[32,2304]{1,0:T(8,128)(2,1)}, bf16[32,2304]{1,0:T(8,128)(2,1)S(1)}, u32[]{:S(2)}, u32[]{:S(2)}) collective-permute-start(bf16[32,2304]{1,0:T(8,128)(2,1)} %fac_ref.1), channel_id=1, source_target_pairs={{0,1},{1,0},{2,3},{3,2},{4,5},{5,4},{6,7},{7,6},{8,9},{9,8},{10,11... | collective-permute-start | bytes 442376 | tf_op jit(solution)/shard_map/ppermute | solution.py:341
  8.8 1.6 %collective-permute-start.1 = (f32[16,2304]{1,0:T(8,128)S(1)}, f32[16,2304]{1,0:T(8,128)S(1)}, u32[]{:S(2)}, u32[]{:S(2)}) collective-permute-start(f32[16,2304]{1,0:T(8,128)S(1)} %get-tuple-element.25), channel_id=1, source_target_pairs={{0,1},{1,0},{2,3},{3,2},{4,5},{5,4},{6,7},{7,6},{8,9},{9,8},{10,11... | collective-permute-start | bytes 442376 | tf_op jit(solution)/shard_map/ppermute | solution.py:344
  10.4 8.0 %collective-permute-start.4 = (f32[16,2304]{1,0:T(8,128)S(1)}, f32[16,2304]{1,0:T(8,128)S(1)}, u32[]{:S(2)}, u32[]{:S(2)}) collective-permute-start(f32[16,2304]{1,0:T(8,128)S(1)} %add.21.after_ref.a_ref), channel_id=1, source_target_pairs={{0,6},{1,25},{2,4},{3,27},{4,2},{5,29},{6,0},{7,31},{8,14},{9,17},... | collective-permute-start | bytes 442376 | tf_op jit(solution)/shard_map/ppermute | solution.py:317
  13.3 5.1 %collective-permute-start.3 = (f32[16,2304]{1,0:T(8,128)S(1)}, f32[16,2304]{1,0:T(8,128)S(1)}, u32[]{:S(2)}, u32[]{:S(2)}) collective-permute-start(f32[16,2304]{1,0:T(8,128)S(1)} %add.21.after_ref.a_ref), channel_id=1, source_target_pairs={{0,2},{1,9},{2,0},{3,11},{4,6},{5,13},{6,4},{7,15},{8,10},{9,1},{1... | collective-permute-start | bytes 442376 | tf_op jit(solution)/shard_map/ppermute | solution.py:317
  13.5 6.6 %collective-permute-start.2 = (f32[16,2304]{1,0:T(8,128)S(1)}, f32[16,2304]{1,0:T(8,128)S(1)}, u32[]{:S(2)}, u32[]{:S(2)}) collective-permute-start(f32[16,2304]{1,0:T(8,128)S(1)} %add.21.after_ref.a_ref), channel_id=1, source_target_pairs={{0,4},{1,17},{2,6},{3,19},{4,0},{5,21},{6,2},{7,23},{8,12},{9,25},... | collective-permute-start | bytes 442376 | tf_op jit(solution)/shard_map/ppermute | solution.py:317
  20.2 15.7 %collective-permute-start.11 = (bf16[2304,1152]{1,0:T(8,128)(2,1)S(1)}, bf16[2304,1152]{1,0:T(8,128)(2,1)S(1)}, u32[]{:S(2)}, u32[]{:S(2)}) collective-permute-start(bf16[2304,1152]{1,0:T(8,128)(2,1)S(1)} %get-tuple-element.30), channel_id=1, source_target_pairs={{0,1},{1,0},{2,3},{3,2},{4,5},{5,4},{6,7},{7,6},{8,9},{9,8},{10,11... | collective-permute-start | bytes 15925256 | tf_op jit(solution)/shard_map/ppermute | solution.py:347
  20.3 8.5 %collective-permute-start.7 = (f32[16,2304]{1,0:T(8,128)S(1)}, f32[16,2304]{1,0:T(8,128)S(1)}, u32[]{:S(2)}, u32[]{:S(2)}) collective-permute-start(f32[16,2304]{1,0:T(8,128)S(1)} %get-tuple-element.27.after_ref.a_ref), channel_id=1, source_target_pairs={{0,24},{1,97},{2,26},{3,99},{4,28},{5,101},{6,30},{7,103},{8,16},{... | collective-permute-start | bytes 442376 | tf_op jit(solution)/shard_map/ppermute | solution.py:317
  23.4 5.4 %collective-permute-start.6 = (f32[16,2304]{1,0:T(8,128)S(1)}, f32[16,2304]{1,0:T(8,128)S(1)}, u32[]{:S(2)}, u32[]{:S(2)}) collective-permute-start(f32[16,2304]{1,0:T(8,128)S(1)} %get-tuple-element.27.after_ref.a_ref), channel_id=1, source_target_pairs={{0,8},{1,33},{2,10},{3,35},{4,12},{5,37},{6,14},{7,39},{8,0},{9,41... | collective-permute-start | bytes 442376 | tf_op jit(solution)/shard_map/ppermute | solution.py:317
  23.5 6.6 %collective-permute-start.5 = (f32[16,2304]{1,0:T(8,128)S(1)}, f32[16,2304]{1,0:T(8,128)S(1)}, u32[]{:S(2)}, u32[]{:S(2)}) collective-permute-start(f32[16,2304]{1,0:T(8,128)S(1)} %get-tuple-element.27.after_ref.a_ref), channel_id=1, source_target_pairs={{0,16},{1,65},{2,18},{3,67},{4,20},{5,69},{6,22},{7,71},{8,24},{9,... | collective-permute-start | bytes 442376 | tf_op jit(solution)/shard_map/ppermute | solution.py:317
  30.2 9.4 %collective-permute-start.10 = (f32[16,2304]{1,0:T(8,128)S(1)}, f32[16,2304]{1,0:T(8,128)S(1)}, u32[]{:S(2)}, u32[]{:S(2)}) collective-permute-start(f32[16,2304]{1,0:T(8,128)S(1)} %get-tuple-element.29.after_ref.a_ref), channel_id=1, source_target_pairs={{0,96},{1,7},{2,98},{3,5},{4,100},{5,3},{6,102},{7,1},{8,104},{9,1... | collective-permute-start | bytes 442376 | tf_op jit(solution)/shard_map/ppermute | solution.py:317
  34.3 5.3 %collective-permute-start.9 = (f32[16,2304]{1,0:T(8,128)S(1)}, f32[16,2304]{1,0:T(8,128)S(1)}, u32[]{:S(2)}, u32[]{:S(2)}) collective-permute-start(f32[16,2304]{1,0:T(8,128)S(1)} %get-tuple-element.29.after_ref.a_ref), channel_id=1, source_target_pairs={{0,32},{1,3},{2,34},{3,1},{4,36},{5,7},{6,38},{7,5},{8,40},{9,11},... | collective-permute-start | bytes 442376 | tf_op jit(solution)/shard_map/ppermute | solution.py:317
  34.3 6.6 %collective-permute-start.8 = (f32[16,2304]{1,0:T(8,128)S(1)}, f32[16,2304]{1,0:T(8,128)S(1)}, u32[]{:S(2)}, u32[]{:S(2)}) collective-permute-start(f32[16,2304]{1,0:T(8,128)S(1)} %get-tuple-element.29.after_ref.a_ref), channel_id=1, source_target_pairs={{0,64},{1,5},{2,66},{3,7},{4,68},{5,1},{6,70},{7,3},{8,72},{9,13},... | collective-permute-start | bytes 442376 | tf_op jit(solution)/shard_map/ppermute | solution.py:317
  41.0 1.5 %collective-permute-start.12 = (f32[16,2304]{1,0:T(8,128)S(1)}, f32[16,2304]{1,0:T(8,128)S(1)}, u32[]{:S(2)}, u32[]{:S(2)}) collective-permute-start(f32[16,2304]{1,0:T(8,128)S(1)} %get-tuple-element.31.keep_ref), channel_id=1, source_target_pairs={{0,1},{1,0},{2,3},{3,2},{4,5},{5,4},{6,7},{7,6},{8,9},{9,8},{10,11... | collective-permute-start | bytes 442376 | tf_op jit(solution)/shard_map/ppermute | solution.py:352
  45.5 6.4 %collective-permute-start.15 = (bf16[32,2304]{1,0:T(8,128)(2,1)S(1)}, bf16[32,2304]{1,0:T(8,128)(2,1)S(1)}, u32[]{:S(2)}, u32[]{:S(2)}) collective-permute-start(bf16[32,2304]{1,0:T(8,128)(2,1)S(1)} %get-tuple-element.34), channel_id=1, source_target_pairs={{0,6},{1,25},{2,4},{3,27},{4,2},{5,29},{6,0},{7,31},{8,14},{9,17},... | collective-permute-start | bytes 442376 | tf_op jit(solution)/shard_map/ppermute | solution.py:317
  48.1 5.1 %collective-permute-start.14 = (bf16[32,2304]{1,0:T(8,128)(2,1)S(1)}, bf16[32,2304]{1,0:T(8,128)(2,1)S(1)}, u32[]{:S(2)}, u32[]{:S(2)}) collective-permute-start(bf16[32,2304]{1,0:T(8,128)(2,1)S(1)} %get-tuple-element.34), channel_id=1, source_target_pairs={{0,2},{1,9},{2,0},{3,11},{4,6},{5,13},{6,4},{7,15},{8,10},{9,1},{1... | collective-permute-start | bytes 442376 | tf_op jit(solution)/shard_map/ppermute | solution.py:317
  48.1 6.9 %collective-permute-start.13 = (bf16[32,2304]{1,0:T(8,128)(2,1)S(1)}, bf16[32,2304]{1,0:T(8,128)(2,1)S(1)}, u32[]{:S(2)}, u32[]{:S(2)}) collective-permute-start(bf16[32,2304]{1,0:T(8,128)(2,1)S(1)} %get-tuple-element.34), channel_id=1, source_target_pairs={{0,4},{1,17},{2,6},{3,19},{4,0},{5,21},{6,2},{7,23},{8,12},{9,25},... | collective-permute-start | bytes 442376 | tf_op jit(solution)/shard_map/ppermute | solution.py:317
  55.0 6.6 %collective-permute-start.18 = (bf16[32,2304]{1,0:T(8,128)(2,1)S(1)}, bf16[32,2304]{1,0:T(8,128)(2,1)S(1)}, u32[]{:S(2)}, u32[]{:S(2)}) collective-permute-start(bf16[32,2304]{1,0:T(8,128)(2,1)S(1)} %add_convert_fusion.1), channel_id=1, source_target_pairs={{0,24},{1,97},{2,26},{3,99},{4,28},{5,101},{6,30},{7,103},{8,16},{... | collective-permute-start | bytes 442376 | tf_op jit(solution)/shard_map/ppermute | solution.py:317
  57.9 5.1 %collective-permute-start.17 = (bf16[32,2304]{1,0:T(8,128)(2,1)S(1)}, bf16[32,2304]{1,0:T(8,128)(2,1)S(1)}, u32[]{:S(2)}, u32[]{:S(2)}) collective-permute-start(bf16[32,2304]{1,0:T(8,128)(2,1)S(1)} %add_convert_fusion.1), channel_id=1, source_target_pairs={{0,8},{1,33},{2,10},{3,35},{4,12},{5,37},{6,14},{7,39},{8,0},{9,41... | collective-permute-start | bytes 442376 | tf_op jit(solution)/shard_map/ppermute | solution.py:317
  57.9 6.8 %collective-permute-start.16 = (bf16[32,2304]{1,0:T(8,128)(2,1)S(1)}, bf16[32,2304]{1,0:T(8,128)(2,1)S(1)}, u32[]{:S(2)}, u32[]{:S(2)}) collective-permute-start(bf16[32,2304]{1,0:T(8,128)(2,1)S(1)} %add_convert_fusion.1), channel_id=1, source_target_pairs={{0,16},{1,65},{2,18},{3,67},{4,20},{5,69},{6,22},{7,71},{8,24},{9,... | collective-permute-start | bytes 442376 | tf_op jit(solution)/shard_map/ppermute | solution.py:317
  64.7 6.4 %collective-permute-start.21 = (bf16[32,2304]{1,0:T(8,128)(2,1)S(1)}, bf16[32,2304]{1,0:T(8,128)(2,1)S(1)}, u32[]{:S(2)}, u32[]{:S(2)}) collective-permute-start(bf16[32,2304]{1,0:T(8,128)(2,1)S(1)} %add_convert_fusion.a_ref), channel_id=1, source_target_pairs={{0,96},{1,7},{2,98},{3,5},{4,100},{5,3},{6,102},{7,1},{8,104},{9,1... | collective-permute-start | bytes 442376 | tf_op jit(solution)/shard_map/ppermute | solution.py:317
  67.6 5.1 %collective-permute-start.20 = (bf16[32,2304]{1,0:T(8,128)(2,1)S(1)}, bf16[32,2304]{1,0:T(8,128)(2,1)S(1)}, u32[]{:S(2)}, u32[]{:S(2)}) collective-permute-start(bf16[32,2304]{1,0:T(8,128)(2,1)S(1)} %add_convert_fusion.a_ref), channel_id=1, source_target_pairs={{0,32},{1,3},{2,34},{3,1},{4,36},{5,7},{6,38},{7,5},{8,40},{9,11},... | collective-permute-start | bytes 442376 | tf_op jit(solution)/shard_map/ppermute | solution.py:317
  67.6 6.6 %collective-permute-start.19 = (bf16[32,2304]{1,0:T(8,128)(2,1)S(1)}, bf16[32,2304]{1,0:T(8,128)(2,1)S(1)}, u32[]{:S(2)}, u32[]{:S(2)}) collective-permute-start(bf16[32,2304]{1,0:T(8,128)(2,1)S(1)} %add_convert_fusion.a_ref), channel_id=1, source_target_pairs={{0,64},{1,5},{2,66},{3,7},{4,68},{5,1},{6,70},{7,3},{8,72},{9,13},... | collective-permute-start | bytes 442376 | tf_op jit(solution)/shard_map/ppermute | solution.py:317

commit v4 on v3

--- a/solution.py
+++ b/solution.py
@@ -301,20 +301,31 @@
     )(*terms, basis_b, in_vmem(own), in_vmem(other))
 
 
-def ring_pairs(axes, flip):
+def ring_pairs(axes, flip, cross):
     pairs = []
     for index in range(64):
         for core in range(2):
-            pairs.append((index * 2 + core, (index ^ (flip << (2 * axes[core]))) * 2 + core))
+            there = index ^ (flip << (2 * axes[core]))
+            pairs.append((index * 2 + core, there * 2 + (core ^ cross)))
     return pairs
 
 
+FLIPS = (1, 3, 2)
 STAGES = ((0, 1), (1, 2), (2, 0))
 SWAP = [(0, 1), (1, 0)]
 
 
-def spread(x, axes):
-    return [x] + [lax.ppermute(x, AXES, ring_pairs(axes, flip)) for flip in (2, 1, 3)]
+def stages(crosses):
+    moved = 0
+    for axes, cross in zip(STAGES, crosses):
+        yield (axes[::-1] if moved else axes), cross
+        moved ^= cross
+
+
+def spread(x, stage):
+    axes, cross = stage
+    terms = [lax.ppermute(x, AXES, ring_pairs(axes, flip, cross)) for flip in FLIPS]
+    return [lax.ppermute(x, "tensor", SWAP) if cross else x] + terms
 
 
 def add4(terms):
@@ -342,17 +353,19 @@
     left, own_err, err, acts, grad_out = load_part(piece_order, old_factor, old_error, acts, grad_out)
     keep, give = term_part(piece_order, old_factor, other_factor, left, acts, grad_out)
     part = keep + lax.ppermute(give, "tensor", SWAP)
-    terms = spread(part, STAGES[0])
+    first, second, third = stages((1, 0, 1))
+    terms = spread(part, first)
     part, send = add_after(terms, send_part(piece_order, part, err))
     other_err = lax.ppermute(send, "tensor", SWAP)
-    terms = spread(part, STAGES[1])
+    terms = spread(part, second)
     part, own = add_after(terms, corrected_half(False, part, acts, grad_out, own_err))
-    terms = spread(part, STAGES[2])
+    terms = spread(part, third)
     part, other = add_after(terms, corrected_half(True, part, acts, grad_out, other_err))
     basis_t, basis_b, right = right_part(part, lax.ppermute(part, "tensor", SWAP), own, other)
-    for axes in STAGES[:-1]:
-        right = add4(spread(right, axes)).astype(BF)
-    terms = spread(right, STAGES[-1])
+    first, second, third = stages((1, 1, 0))
+    for stage in (first, second):
+        right = add4(spread(right, stage)).astype(BF)
+    terms = spread(right, third)
     new_error, new_factor = residue(terms, basis_b, own, other, 1.0 / lax.axis_size("dp"))
     return (new_error, basis_t.T, new_factor)
 

time: 79.7 us -> 73.6 us (0.923)
  waiting for transfers between devices: 20.3 us -> 16.3 us
  starting transfers between devices: 30.6 us -> 29.2 us
    ppermute x18 -> x22, waiting for transfers between devices: 18 us -> 14.2 us  [the longest x18 14.2 us: spread(): lax.ppermute(x, AXES, ring_pairs(axes, flip, cross))]
    ppermute x18 -> x22, starting transfers between devices: 29.8 us -> 27.4 us  [the longest x18 25.6 us: spread(): lax.ppermute(x, AXES, ring_pairs(axes, flip, cross))]
  transfers between devices with their start and end apart: 22 -> 26, of which waited for: 15 -> 12; matrix products, arithmetic and copies ran while one was open for 1% -> 1% of each run, Pallas kernels for 21% -> 23%
where the time goes in v4:
time: 73.6 us; the launch traced here: 73.5 us
  starting transfers between devices  29.2 us (40%)
  Pallas kernels  26.1 us (35%)
  waiting for transfers between devices  16.3 us (22%)
  between operations  1 us (1%)
    ppermute x18, starting transfers between devices, spread(): lax.ppermute(x, AXES, ring_pairs(axes, flip, cross))  25.6 us
    ppermute x18, waiting for transfers between devices, spread(): lax.ppermute(x, AXES, ring_pairs(axes, flip, cross))  14.2 us
    pallas_call x2, Pallas kernels, corrected_half(): call(functools.partial(half_kernel, other), 'corrected_other' if other el...  7.41 us
    pallas_call x1, Pallas kernels, load_part(): call(load_kernel, 'load_part', [FAR] * 5, [pltpu.VMEM((RANK, ROWS), F32),...  6.03 us
    pallas_call x1, Pallas kernels, residue(): call(functools.partial(residue_kernel, scale), 'residue', [WHOLE] * 7, [p...  4.6 us
    pallas_call x1, Pallas kernels, send_part(): call(send_kernel, 'send_part', [SCALARS, pl.BlockSpec(memory_space=pl.ANY...  3.09 us
    pallas_call x1, Pallas kernels, right_part(): call(right_kernel, 'right_part', [WHOLE] * 4, [pltpu.VMEM((RANK, ROWS), F...  3.01 us
    pallas_call x1, Pallas kernels, term_part(): call(term_kernel, 'term_part', [SCALARS] + [WHOLE] * 5, [half, half], [pl...  1.89 us
  transfers between devices with their start and end apart: 26, of which 12 were waited for; matrix products, arithmetic and copies ran while one was open for 1% of the time, Pallas kernels for 23%

profile of v4, /device:TPU:0, one launch (start us, length us, event | category | flops | bytes accessed | tf_op | source)
XLA Modules:
  0.0 73.5 jit_solution(4316932933967696327)
XLA Ops:
  0.7 0.1 collective-permute-start
  0.7 6.0 %load_part.1 = (f32[32,2304]{1,0:T(8,128)S(1)}, bf16[2304,1152]{1,0:T(8,128)(2,1)S(1)}, bf16[2304,2304]{1,0:T(8,128)(2,1)S(1)}, bf16[512,2304]{1,0:T(8,128)(2,1)S(1)}, bf16[512,2304]{1,0:T(8,128)(2,1)S(1)}) custom-call(s32[8]{0:T(128)} %order_ref.3, bf16[32,2304]{1,0:T(8,128)(2,1)} %fac_ref.1, bf16[2304,2304]{1,0:T(8,128)(2,1)} %far_err.1, ...), custom_call_target="tpu_custom_call" | custom-call | flops 339738624 | bytes 10616832 | tf_op jit(solution)/shard_map/load_part/pallas_call | solution.py:109
  6.8 1.9 %term_part.1 = (f32[16,2304]{1,0:T(8,128)S(1)}, f32[16,2304]{1,0:T(8,128)S(1)}) custom-call(s32[8]{0:T(128)S(1)} %copy-done.1, bf16[32,2304]{1,0:T(8,128)(2,1)S(1)} %copy-done, bf16[32,2304]{1,0:T(8,128)(2,1)S(1)} %collective-permute-done.other_ref, f32[32,2304]{1,0:T(8,128)S(1)} %get-tuple-element.21.left_ref, ...), custom_call_target="tpu_custom_call" | custom-call | flops 150994944 | bytes 5000000 | tf_op jit(solution)/shard_map/term_part/pallas_call | solution.py:146
  8.7 0.6 collective-permute-start.1
  9.3 1.0 %collective-permute-done.1 = f32[16,2304]{1,0:T(8,128)S(1)} collective-permute-done((f32[16,2304]{1,0:T(8,128)S(1)}, f32[16,2304]{1,0:T(8,128)S(1)}, u32[]{:S(2)}, u32[]{:S(2)}) %collective-permute-start.1) | collective-permute-done | bytes 147488 | tf_op jit(solution)/shard_map/ppermute | solution.py:355
  10.4 3.1 %collective-permute-start.5 = (f32[16,2304]{1,0:T(8,128)S(1)}, f32[16,2304]{1,0:T(8,128)S(1)}, u32[]{:S(2)}, u32[]{:S(2)}) collective-permute-start(f32[16,2304]{1,0:T(8,128)S(1)} %add.21.after_ref), channel_id=1, source_target_pairs={{0,5},{1,16},{2,7},{3,18},{4,1},{5,20},{6,3},{7,22},{8,13},{9,24},... | collective-permute-start | bytes 442376 | tf_op jit(solution)/shard_map/ppermute | solution.py:327
  13.5 2.7 %collective-permute-start.4 = (f32[16,2304]{1,0:T(8,128)S(1)}, f32[16,2304]{1,0:T(8,128)S(1)}, u32[]{:S(2)}, u32[]{:S(2)}) collective-permute-start(f32[16,2304]{1,0:T(8,128)S(1)} %add.21.after_ref), channel_id=1, source_target_pairs={{0,7},{1,24},{2,5},{3,26},{4,3},{5,28},{6,1},{7,30},{8,15},{9,16},... | collective-permute-start | bytes 442376 | tf_op jit(solution)/shard_map/ppermute | solution.py:327
  16.2 0.6 collective-permute-start.3
  16.8 0.1 collective-permute-start.2
  17.0 3.1 %send_part.1.work_ref = bf16[2304,1152]{1,0:T(8,128)(2,1)S(1)} custom-call(s32[8]{0:T(128)S(1)} %copy-done.1, f32[16,2304]{1,0:T(8,128)S(1)} %add.21.after_ref, bf16[2304,2304]{1,0:T(8,128)(2,1)S(1)} %get-tuple-element.26.err_ref), custom_call_target="tpu_custom_call" | custom-call | flops 1000000000 | bytes 4000000 | tf_op jit(solution)/shard_map/send_part/pallas_call | solution.py:166
  20.1 0.0 collective-permute-done.4.c_ref
  20.1 0.7 collective-permute-done.3.b_ref
  20.8 0.0 collective-permute-done.2.a_ref
  20.8 0.5 collective-permute-start.13
  21.3 3.9 %collective-permute-start.8 = (f32[16,2304]{1,0:T(8,128)S(1)}, f32[16,2304]{1,0:T(8,128)S(1)}, u32[]{:S(2)}, u32[]{:S(2)}) collective-permute-start(f32[16,2304]{1,0:T(8,128)S(1)} %get-tuple-element.27.after_ref.a_ref), channel_id=1, source_target_pairs={{0,64},{1,17},{2,66},{3,19},{4,68},{5,21},{6,70},{7,23},{8,72},{9,... | collective-permute-start | bytes 442376 | tf_op jit(solution)/shard_map/ppermute | solution.py:327
  25.2 0.7 collective-permute-start.7
  25.9 0.3 collective-permute-start.6
  26.2 3.7 %corrected_own.1.work_ref = bf16[2304,1152]{1,0:T(8,128)(2,1)S(1)} custom-call(f32[16,2304]{1,0:T(8,128)S(1)} %get-tuple-element.27.after_ref.a_ref, bf16[512,2304]{1,0:T(8,128)(2,1)S(1)} %get-tuple-element.22.acts_ref, bf16[512,2304]{1,0:T(8,128)(2,1)S(1)} %get-tuple-element.23.grad_ref, bf16[2304,1152]{1,0:T(8,128)(2,1)S(1)} %get-tuple-element.28.err_ref), custom_call_target="tpu_custom_call" | custom-call | flops 2717908992 | bytes 8000000 | tf_op jit(solution)/shard_map/corrected_own/pallas_call | solution.py:190
  29.9 1.6 %collective-permute-done.7.c_ref = f32[16,2304]{1,0:T(8,128)S(1)} collective-permute-done((f32[16,2304]{1,0:T(8,128)S(1)}, f32[16,2304]{1,0:T(8,128)S(1)}, u32[]{:S(2)}, u32[]{:S(2)}) %collective-permute-start.7) | collective-permute-done | bytes 147488 | tf_op jit(solution)/shard_map/ppermute | solution.py:327
  31.6 0.1 collective-permute-start.12
  31.7 2.9 %collective-permute-start.11 = (f32[16,2304]{1,0:T(8,128)S(1)}, f32[16,2304]{1,0:T(8,128)S(1)}, u32[]{:S(2)}, u32[]{:S(2)}) collective-permute-start(f32[16,2304]{1,0:T(8,128)S(1)} %get-tuple-element.29.after_ref), channel_id=1, source_target_pairs={{0,7},{1,96},{2,5},{3,98},{4,3},{5,100},{6,1},{7,102},{8,15},{9,10... | collective-permute-start | bytes 442376 | tf_op jit(solution)/shard_map/ppermute | solution.py:327
  34.6 0.9 %collective-permute-start.9 = (f32[16,2304]{1,0:T(8,128)S(1)}, f32[16,2304]{1,0:T(8,128)S(1)}, u32[]{:S(2)}, u32[]{:S(2)}) collective-permute-start(f32[16,2304]{1,0:T(8,128)S(1)} %get-tuple-element.29.after_ref), channel_id=1, source_target_pairs={{0,1},{1,0},{2,3},{3,2},{4,5},{5,4},{6,7},{7,6},{8,9},{9,8},{10,11... | collective-permute-start | bytes 442376 | tf_op jit(solution)/shard_map/ppermute | solution.py:328
  35.5 3.7 %corrected_other.1.work_ref = bf16[2304,1152]{1,0:T(8,128)(2,1)S(1)} custom-call(f32[16,2304]{1,0:T(8,128)S(1)} %get-tuple-element.29.after_ref, bf16[512,2304]{1,0:T(8,128)(2,1)S(1)} %get-tuple-element.22.acts_ref, bf16[512,2304]{1,0:T(8,128)(2,1)S(1)} %get-tuple-element.23.grad_ref, bf16[2304,1152]{1,0:T(8,128)(2,1)S(1)} %collective-permute-done.13.err_ref), custom_call_target="tpu_custom_call" | custom-call | flops 2717908992 | bytes 8000000 | tf_op jit(solution)/shard_map/corrected_other/pallas_call | solution.py:190
  39.4 0.6 collective-permute-start.14
  39.9 1.1 %collective-permute-done.14.took_ref = f32[16,2304]{1,0:T(8,128)S(1)} collective-permute-done((f32[16,2304]{1,0:T(8,128)S(1)}, f32[16,2304]{1,0:T(8,128)S(1)}, u32[]{:S(2)}, u32[]{:S(2)}) %collective-permute-start.14) | collective-permute-done | bytes 147488 | tf_op jit(solution)/shard_map/ppermute | solution.py:364
  41.0 3.0 %right_part.1 = (f32[32,2304]{1,0:T(8,128)S(1)}, bf16[32,2304]{1,0:T(8,128)(2,1)S(1)}, bf16[32,2304]{1,0:T(8,128)(2,1)S(1)}) custom-call(f32[16,2304]{1,0:T(8,128)S(1)} %get-tuple-element.31.keep_ref, f32[16,2304]{1,0:T(8,128)S(1)} %collective-permute-done.14.took_ref, bf16[2304,1152]{1,0:T(8,128)(2,1)S(1)} %get-tuple-element.32.own_ref, ...), custom_call_target="tpu_custom_call" | custom-call | flops 339738624 | bytes 10616832 | tf_op jit(solution)/shard_map/right_part/pallas_call | solution.py:247
  44.0 1.7 %collective-permute-start.18 = (bf16[32,2304]{1,0:T(8,128)(2,1)S(1)}, bf16[32,2304]{1,0:T(8,128)(2,1)S(1)}, u32[]{:S(2)}, u32[]{:S(2)}) collective-permute-start(bf16[32,2304]{1,0:T(8,128)(2,1)S(1)} %get-tuple-element.34), channel_id=1, source_target_pairs={{0,5},{1,16},{2,7},{3,18},{4,1},{5,20},{6,3},{7,22},{8,13},{9,24},... | collective-permute-start | bytes 442376 | tf_op jit(solution)/shard_map/ppermute | solution.py:327
  45.7 1.3 %collective-permute-start.17 = (bf16[32,2304]{1,0:T(8,128)(2,1)S(1)}, bf16[32,2304]{1,0:T(8,128)(2,1)S(1)}, u32[]{:S(2)}, u32[]{:S(2)}) collective-permute-start(bf16[32,2304]{1,0:T(8,128)(2,1)S(1)} %get-tuple-element.34), channel_id=1, source_target_pairs={{0,7},{1,24},{2,5},{3,26},{4,3},{5,28},{6,1},{7,30},{8,15},{9,16},... | collective-permute-start | bytes 442376 | tf_op jit(solution)/shard_map/ppermute | solution.py:327
  47.0 0.7 collective-permute-start.16
  47.7 0.4 collective-permute-start.15
  48.0 2.1 %collective-permute-done.18 = bf16[32,2304]{1,0:T(8,128)(2,1)S(1)} collective-permute-done((bf16[32,2304]{1,0:T(8,128)(2,1)S(1)}, bf16[32,2304]{1,0:T(8,128)(2,1)S(1)}, u32[]{:S(2)}, u32[]{:S(2)}) %collective-permute-start.18) | collective-permute-done | bytes 147488 | tf_op jit(solution)/shard_map/ppermute | solution.py:327
  50.2 1.6 %collective-permute-done.17 = bf16[32,2304]{1,0:T(8,128)(2,1)S(1)} collective-permute-done((bf16[32,2304]{1,0:T(8,128)(2,1)S(1)}, bf16[32,2304]{1,0:T(8,128)(2,1)S(1)}, u32[]{:S(2)}, u32[]{:S(2)}) %collective-permute-start.17) | collective-permute-done | bytes 147488 | tf_op jit(solution)/shard_map/ppermute | solution.py:327
  51.7 0.1 add_convert_fusion.1
  51.8 1.6 %collective-permute-start.22 = (bf16[32,2304]{1,0:T(8,128)(2,1)S(1)}, bf16[32,2304]{1,0:T(8,128)(2,1)S(1)}, u32[]{:S(2)}, u32[]{:S(2)}) collective-permute-start(bf16[32,2304]{1,0:T(8,128)(2,1)S(1)} %add_convert_fusion.1), channel_id=1, source_target_pairs={{0,65},{1,16},{2,67},{3,18},{4,69},{5,20},{6,71},{7,22},{8,73},{9,... | collective-permute-start | bytes 442376 | tf_op jit(solution)/shard_map/ppermute | solution.py:327
  53.5 1.6 %collective-permute-start.21 = (bf16[32,2304]{1,0:T(8,128)(2,1)S(1)}, bf16[32,2304]{1,0:T(8,128)(2,1)S(1)}, u32[]{:S(2)}, u32[]{:S(2)}) collective-permute-start(bf16[32,2304]{1,0:T(8,128)(2,1)S(1)} %add_convert_fusion.1), channel_id=1, source_target_pairs={{0,97},{1,24},{2,99},{3,26},{4,101},{5,28},{6,103},{7,30},{8,105},... | collective-permute-start | bytes 442376 | tf_op jit(solution)/shard_map/ppermute | solution.py:327
  55.0 0.4 collective-permute-start.20
  55.4 0.4 collective-permute-start.19
  55.8 2.2 %collective-permute-done.22 = bf16[32,2304]{1,0:T(8,128)(2,1)S(1)} collective-permute-done((bf16[32,2304]{1,0:T(8,128)(2,1)S(1)}, bf16[32,2304]{1,0:T(8,128)(2,1)S(1)}, u32[]{:S(2)}, u32[]{:S(2)}) %collective-permute-start.22) | collective-permute-done | bytes 147488 | tf_op jit(solution)/shard_map/ppermute | solution.py:327
  58.0 1.6 %collective-permute-done.21 = bf16[32,2304]{1,0:T(8,128)(2,1)S(1)} collective-permute-done((bf16[32,2304]{1,0:T(8,128)(2,1)S(1)}, bf16[32,2304]{1,0:T(8,128)(2,1)S(1)}, u32[]{:S(2)}, u32[]{:S(2)}) %collective-permute-start.21) | collective-permute-done | bytes 147488 | tf_op jit(solution)/shard_map/ppermute | solution.py:327
  59.5 0.1 collective-permute-done.20
  59.6 0.1 add_convert_fusion.a_ref
  59.7 2.1 %collective-permute-start.25 = (bf16[32,2304]{1,0:T(8,128)(2,1)S(1)}, bf16[32,2304]{1,0:T(8,128)(2,1)S(1)}, u32[]{:S(2)}, u32[]{:S(2)}) collective-permute-start(bf16[32,2304]{1,0:T(8,128)(2,1)S(1)} %add_convert_fusion.a_ref), channel_id=1, source_target_pairs={{0,64},{1,5},{2,66},{3,7},{4,68},{5,1},{6,70},{7,3},{8,72},{9,13},... | collective-permute-start | bytes 442376 | tf_op jit(solution)/shard_map/ppermute | solution.py:327
  61.8 1.8 %collective-permute-start.24 = (bf16[32,2304]{1,0:T(8,128)(2,1)S(1)}, bf16[32,2304]{1,0:T(8,128)(2,1)S(1)}, u32[]{:S(2)}, u32[]{:S(2)}) collective-permute-start(bf16[32,2304]{1,0:T(8,128)(2,1)S(1)} %add_convert_fusion.a_ref), channel_id=1, source_target_pairs={{0,96},{1,7},{2,98},{3,5},{4,100},{5,3},{6,102},{7,1},{8,104},{9,1... | collective-permute-start | bytes 442376 | tf_op jit(solution)/shard_map/ppermute | solution.py:327
  63.6 0.7 copy.14
  64.3 2.1 %collective-permute-done.25.d_ref = bf16[32,2304]{1,0:T(8,128)(2,1)S(1)} collective-permute-done((bf16[32,2304]{1,0:T(8,128)(2,1)S(1)}, bf16[32,2304]{1,0:T(8,128)(2,1)S(1)}, u32[]{:S(2)}, u32[]{:S(2)}) %collective-permute-start.25) | collective-permute-done | bytes 147488 | tf_op jit(solution)/shard_map/ppermute | solution.py:327
  66.4 1.8 %collective-permute-done.24.c_ref = bf16[32,2304]{1,0:T(8,128)(2,1)S(1)} collective-permute-done((bf16[32,2304]{1,0:T(8,128)(2,1)S(1)}, bf16[32,2304]{1,0:T(8,128)(2,1)S(1)}, u32[]{:S(2)}, u32[]{:S(2)}) %collective-permute-start.24) | collective-permute-done | bytes 147488 | tf_op jit(solution)/shard_map/ppermute | solution.py:327
  68.2 0.6 collective-permute-done.23.b_ref
  68.7 4.6 %residue.1 = (bf16[2304,2304]{1,0:T(8,128)(2,1)}, f32[32,2304]{1,0:T(8,128)}) custom-call(bf16[32,2304]{1,0:T(8,128)(2,1)S(1)} %add_convert_fusion.a_ref, bf16[32,2304]{1,0:T(8,128)(2,1)S(1)} %collective-permute-done.23.b_ref, bf16[32,2304]{1,0:T(8,128)(2,1)S(1)} %collective-permute-done.24.c_ref, bf16[32,2304]{1,0:T(8,128)(2,1)S(1)} %collective-permute-done.25.d_ref, ...), custom_call_target="tpu_custom_call" | custom-call | flops 339738624 | bytes 10616832 | tf_op jit(solution)/shard_map/residue/pallas_call | solution.py:286
  (22 shorter events, 0.2 us)
Async XLA Ops:
  0.6 6.2 %copy-start = (bf16[32,2304]{1,0:T(8,128)(2,1)S(1)}, bf16[32,2304]{1,0:T(8,128)(2,1)}, u32[]{:S(2)}) copy-start(bf16[32,2304]{1,0:T(8,128)(2,1)} %fac_ref.1) | copy-start | bytes 442372
  0.6 6.2 %copy-start.1 = (s32[8]{0:T(128)S(1)}, s32[8]{0:T(128)}, u32[]{:S(2)}) copy-start(s32[8]{0:T(128)} %order_ref.3) | copy-start | bytes 100
  0.7 6.1 %collective-permute-start = (bf16[32,2304]{1,0:T(8,128)(2,1)}, bf16[32,2304]{1,0:T(8,128)(2,1)S(1)}, u32[]{:S(2)}, u32[]{:S(2)}) collective-permute-start(bf16[32,2304]{1,0:T(8,128)(2,1)} %fac_ref.1), channel_id=1, source_target_pairs={{0,1},{1,0},{2,3},{3,2},{4,5},{5,4},{6,7},{7,6},{8,9},{9,8},{10,11... | collective-permute-start | bytes 442376 | tf_op jit(solution)/shard_map/ppermute | solution.py:352
  8.7 1.6 %collective-permute-start.1 = (f32[16,2304]{1,0:T(8,128)S(1)}, f32[16,2304]{1,0:T(8,128)S(1)}, u32[]{:S(2)}, u32[]{:S(2)}) collective-permute-start(f32[16,2304]{1,0:T(8,128)S(1)} %get-tuple-element.25), channel_id=1, source_target_pairs={{0,1},{1,0},{2,3},{3,2},{4,5},{5,4},{6,7},{7,6},{8,9},{9,8},{10,11... | collective-permute-start | bytes 442376 | tf_op jit(solution)/shard_map/ppermute | solution.py:355
  10.4 9.7 %collective-permute-start.5 = (f32[16,2304]{1,0:T(8,128)S(1)}, f32[16,2304]{1,0:T(8,128)S(1)}, u32[]{:S(2)}, u32[]{:S(2)}) collective-permute-start(f32[16,2304]{1,0:T(8,128)S(1)} %add.21.after_ref), channel_id=1, source_target_pairs={{0,5},{1,16},{2,7},{3,18},{4,1},{5,20},{6,3},{7,22},{8,13},{9,24},... | collective-permute-start | bytes 442376 | tf_op jit(solution)/shard_map/ppermute | solution.py:327
  13.5 6.6 %collective-permute-start.4 = (f32[16,2304]{1,0:T(8,128)S(1)}, f32[16,2304]{1,0:T(8,128)S(1)}, u32[]{:S(2)}, u32[]{:S(2)}) collective-permute-start(f32[16,2304]{1,0:T(8,128)S(1)} %add.21.after_ref), channel_id=1, source_target_pairs={{0,7},{1,24},{2,5},{3,26},{4,3},{5,28},{6,1},{7,30},{8,15},{9,16},... | collective-permute-start | bytes 442376 | tf_op jit(solution)/shard_map/ppermute | solution.py:327
  16.2 4.6 %collective-permute-start.3 = (f32[16,2304]{1,0:T(8,128)S(1)}, f32[16,2304]{1,0:T(8,128)S(1)}, u32[]{:S(2)}, u32[]{:S(2)}) collective-permute-start(f32[16,2304]{1,0:T(8,128)S(1)} %add.21.after_ref), channel_id=1, source_target_pairs={{0,3},{1,8},{2,1},{3,10},{4,7},{5,12},{6,5},{7,14},{8,11},{9,0},{1... | collective-permute-start | bytes 442376 | tf_op jit(solution)/shard_map/ppermute | solution.py:327
  16.8 3.9 %collective-permute-start.2 = (f32[16,2304]{1,0:T(8,128)S(1)}, f32[16,2304]{1,0:T(8,128)S(1)}, u32[]{:S(2)}, u32[]{:S(2)}) collective-permute-start(f32[16,2304]{1,0:T(8,128)S(1)} %add.21.after_ref), channel_id=1, source_target_pairs={{0,1},{1,0},{2,3},{3,2},{4,5},{5,4},{6,7},{7,6},{8,9},{9,8},{10,11... | collective-permute-start | bytes 442376 | tf_op jit(solution)/shard_map/ppermute | solution.py:328
  20.8 14.7 %collective-permute-start.13 = (bf16[2304,1152]{1,0:T(8,128)(2,1)S(1)}, bf16[2304,1152]{1,0:T(8,128)(2,1)S(1)}, u32[]{:S(2)}, u32[]{:S(2)}) collective-permute-start(bf16[2304,1152]{1,0:T(8,128)(2,1)S(1)} %get-tuple-element.30), channel_id=1, source_target_pairs={{0,1},{1,0},{2,3},{3,2},{4,5},{5,4},{6,7},{7,6},{8,9},{9,8},{10,11... | collective-permute-start | bytes 15925256 | tf_op jit(solution)/shard_map/ppermute | solution.py:359
  21.3 8.6 %collective-permute-start.8 = (f32[16,2304]{1,0:T(8,128)S(1)}, f32[16,2304]{1,0:T(8,128)S(1)}, u32[]{:S(2)}, u32[]{:S(2)}) collective-permute-start(f32[16,2304]{1,0:T(8,128)S(1)} %get-tuple-element.27.after_ref.a_ref), channel_id=1, source_target_pairs={{0,64},{1,17},{2,66},{3,19},{4,68},{5,21},{6,70},{7,23},{8,72},{9,... | collective-permute-start | bytes 442376 | tf_op jit(solution)/shard_map/ppermute | solution.py:327
  25.2 6.4 %collective-permute-start.7 = (f32[16,2304]{1,0:T(8,128)S(1)}, f32[16,2304]{1,0:T(8,128)S(1)}, u32[]{:S(2)}, u32[]{:S(2)}) collective-permute-start(f32[16,2304]{1,0:T(8,128)S(1)} %get-tuple-element.27.after_ref.a_ref), channel_id=1, source_target_pairs={{0,96},{1,25},{2,98},{3,27},{4,100},{5,29},{6,102},{7,31},{8,104},... | collective-permute-start | bytes 442376 | tf_op jit(solution)/shard_map/ppermute | solution.py:327
  25.9 5.6 %collective-permute-start.6 = (f32[16,2304]{1,0:T(8,128)S(1)}, f32[16,2304]{1,0:T(8,128)S(1)}, u32[]{:S(2)}, u32[]{:S(2)}) collective-permute-start(f32[16,2304]{1,0:T(8,128)S(1)} %get-tuple-element.27.after_ref.a_ref), channel_id=1, source_target_pairs={{0,32},{1,9},{2,34},{3,11},{4,36},{5,13},{6,38},{7,15},{8,40},{9,1... | collective-permute-start | bytes 442376 | tf_op jit(solution)/shard_map/ppermute | solution.py:327
  31.6 7.7 %collective-permute-start.12 = (f32[16,2304]{1,0:T(8,128)S(1)}, f32[16,2304]{1,0:T(8,128)S(1)}, u32[]{:S(2)}, u32[]{:S(2)}) collective-permute-start(f32[16,2304]{1,0:T(8,128)S(1)} %get-tuple-element.29.after_ref), channel_id=1, source_target_pairs={{0,5},{1,64},{2,7},{3,66},{4,1},{5,68},{6,3},{7,70},{8,13},{9,72},... | collective-permute-start | bytes 442376 | tf_op jit(solution)/shard_map/ppermute | solution.py:327
  31.7 7.6 %collective-permute-start.11 = (f32[16,2304]{1,0:T(8,128)S(1)}, f32[16,2304]{1,0:T(8,128)S(1)}, u32[]{:S(2)}, u32[]{:S(2)}) collective-permute-start(f32[16,2304]{1,0:T(8,128)S(1)} %get-tuple-element.29.after_ref), channel_id=1, source_target_pairs={{0,7},{1,96},{2,5},{3,98},{4,3},{5,100},{6,1},{7,102},{8,15},{9,10... | collective-permute-start | bytes 442376 | tf_op jit(solution)/shard_map/ppermute | solution.py:327
  34.6 4.7 %collective-permute-start.10 = (f32[16,2304]{1,0:T(8,128)S(1)}, f32[16,2304]{1,0:T(8,128)S(1)}, u32[]{:S(2)}, u32[]{:S(2)}) collective-permute-start(f32[16,2304]{1,0:T(8,128)S(1)} %get-tuple-element.29.after_ref), channel_id=1, source_target_pairs={{0,3},{1,32},{2,1},{3,34},{4,7},{5,36},{6,5},{7,38},{8,11},{9,40},... | collective-permute-start | bytes 442376 | tf_op jit(solution)/shard_map/ppermute | solution.py:327
  34.6 4.7 %collective-permute-start.9 = (f32[16,2304]{1,0:T(8,128)S(1)}, f32[16,2304]{1,0:T(8,128)S(1)}, u32[]{:S(2)}, u32[]{:S(2)}) collective-permute-start(f32[16,2304]{1,0:T(8,128)S(1)} %get-tuple-element.29.after_ref), channel_id=1, source_target_pairs={{0,1},{1,0},{2,3},{3,2},{4,5},{5,4},{6,7},{7,6},{8,9},{9,8},{10,11... | collective-permute-start | bytes 442376 | tf_op jit(solution)/shard_map/ppermute | solution.py:328
  39.4 1.6 %collective-permute-start.14 = (f32[16,2304]{1,0:T(8,128)S(1)}, f32[16,2304]{1,0:T(8,128)S(1)}, u32[]{:S(2)}, u32[]{:S(2)}) collective-permute-start(f32[16,2304]{1,0:T(8,128)S(1)} %get-tuple-element.31.keep_ref), channel_id=1, source_target_pairs={{0,1},{1,0},{2,3},{3,2},{4,5},{5,4},{6,7},{7,6},{8,9},{9,8},{10,11... | collective-permute-start | bytes 442376 | tf_op jit(solution)/shard_map/ppermute | solution.py:364
  44.0 6.2 %collective-permute-start.18 = (bf16[32,2304]{1,0:T(8,128)(2,1)S(1)}, bf16[32,2304]{1,0:T(8,128)(2,1)S(1)}, u32[]{:S(2)}, u32[]{:S(2)}) collective-permute-start(bf16[32,2304]{1,0:T(8,128)(2,1)S(1)} %get-tuple-element.34), channel_id=1, source_target_pairs={{0,5},{1,16},{2,7},{3,18},{4,1},{5,20},{6,3},{7,22},{8,13},{9,24},... | collective-permute-start | bytes 442376 | tf_op jit(solution)/shard_map/ppermute | solution.py:327
  45.7 6.0 %collective-permute-start.17 = (bf16[32,2304]{1,0:T(8,128)(2,1)S(1)}, bf16[32,2304]{1,0:T(8,128)(2,1)S(1)}, u32[]{:S(2)}, u32[]{:S(2)}) collective-permute-start(bf16[32,2304]{1,0:T(8,128)(2,1)S(1)} %get-tuple-element.34), channel_id=1, source_target_pairs={{0,7},{1,24},{2,5},{3,26},{4,3},{5,28},{6,1},{7,30},{8,15},{9,16},... | collective-permute-start | bytes 442376 | tf_op jit(solution)/shard_map/ppermute | solution.py:327
  47.0 4.7 %collective-permute-start.16 = (bf16[32,2304]{1,0:T(8,128)(2,1)S(1)}, bf16[32,2304]{1,0:T(8,128)(2,1)S(1)}, u32[]{:S(2)}, u32[]{:S(2)}) collective-permute-start(bf16[32,2304]{1,0:T(8,128)(2,1)S(1)} %get-tuple-element.34), channel_id=1, source_target_pairs={{0,3},{1,8},{2,1},{3,10},{4,7},{5,12},{6,5},{7,14},{8,11},{9,0},{1... | collective-permute-start | bytes 442376 | tf_op jit(solution)/shard_map/ppermute | solution.py:327
  47.7 4.1 %collective-permute-start.15 = (bf16[32,2304]{1,0:T(8,128)(2,1)S(1)}, bf16[32,2304]{1,0:T(8,128)(2,1)S(1)}, u32[]{:S(2)}, u32[]{:S(2)}) collective-permute-start(bf16[32,2304]{1,0:T(8,128)(2,1)S(1)} %get-tuple-element.34), channel_id=1, source_target_pairs={{0,1},{1,0},{2,3},{3,2},{4,5},{5,4},{6,7},{7,6},{8,9},{9,8},{10,11... | collective-permute-start | bytes 442376 | tf_op jit(solution)/shard_map/ppermute | solution.py:328
  51.8 6.2 %collective-permute-start.22 = (bf16[32,2304]{1,0:T(8,128)(2,1)S(1)}, bf16[32,2304]{1,0:T(8,128)(2,1)S(1)}, u32[]{:S(2)}, u32[]{:S(2)}) collective-permute-start(bf16[32,2304]{1,0:T(8,128)(2,1)S(1)} %add_convert_fusion.1), channel_id=1, source_target_pairs={{0,65},{1,16},{2,67},{3,18},{4,69},{5,20},{6,71},{7,22},{8,73},{9,... | collective-permute-start | bytes 442376 | tf_op jit(solution)/shard_map/ppermute | solution.py:327
  53.5 6.1 %collective-permute-start.21 = (bf16[32,2304]{1,0:T(8,128)(2,1)S(1)}, bf16[32,2304]{1,0:T(8,128)(2,1)S(1)}, u32[]{:S(2)}, u32[]{:S(2)}) collective-permute-start(bf16[32,2304]{1,0:T(8,128)(2,1)S(1)} %add_convert_fusion.1), channel_id=1, source_target_pairs={{0,97},{1,24},{2,99},{3,26},{4,101},{5,28},{6,103},{7,30},{8,105},... | collective-permute-start | bytes 442376 | tf_op jit(solution)/shard_map/ppermute | solution.py:327
  55.0 4.6 %collective-permute-start.20 = (bf16[32,2304]{1,0:T(8,128)(2,1)S(1)}, bf16[32,2304]{1,0:T(8,128)(2,1)S(1)}, u32[]{:S(2)}, u32[]{:S(2)}) collective-permute-start(bf16[32,2304]{1,0:T(8,128)(2,1)S(1)} %add_convert_fusion.1), channel_id=1, source_target_pairs={{0,33},{1,8},{2,35},{3,10},{4,37},{5,12},{6,39},{7,14},{8,41},{9,0... | collective-permute-start | bytes 442376 | tf_op jit(solution)/shard_map/ppermute | solution.py:327
  55.4 4.2 %collective-permute-start.19 = (bf16[32,2304]{1,0:T(8,128)(2,1)S(1)}, bf16[32,2304]{1,0:T(8,128)(2,1)S(1)}, u32[]{:S(2)}, u32[]{:S(2)}) collective-permute-start(bf16[32,2304]{1,0:T(8,128)(2,1)S(1)} %add_convert_fusion.1), channel_id=1, source_target_pairs={{0,1},{1,0},{2,3},{3,2},{4,5},{5,4},{6,7},{7,6},{8,9},{9,8},{10,11... | collective-permute-start | bytes 442376 | tf_op jit(solution)/shard_map/ppermute | solution.py:328
  59.7 6.7 %collective-permute-start.25 = (bf16[32,2304]{1,0:T(8,128)(2,1)S(1)}, bf16[32,2304]{1,0:T(8,128)(2,1)S(1)}, u32[]{:S(2)}, u32[]{:S(2)}) collective-permute-start(bf16[32,2304]{1,0:T(8,128)(2,1)S(1)} %add_convert_fusion.a_ref), channel_id=1, source_target_pairs={{0,64},{1,5},{2,66},{3,7},{4,68},{5,1},{6,70},{7,3},{8,72},{9,13},... | collective-permute-start | bytes 442376 | tf_op jit(solution)/shard_map/ppermute | solution.py:327
  61.8 6.4 %collective-permute-start.24 = (bf16[32,2304]{1,0:T(8,128)(2,1)S(1)}, bf16[32,2304]{1,0:T(8,128)(2,1)S(1)}, u32[]{:S(2)}, u32[]{:S(2)}) collective-permute-start(bf16[32,2304]{1,0:T(8,128)(2,1)S(1)} %add_convert_fusion.a_ref), channel_id=1, source_target_pairs={{0,96},{1,7},{2,98},{3,5},{4,100},{5,3},{6,102},{7,1},{8,104},{9,1... | collective-permute-start | bytes 442376 | tf_op jit(solution)/shard_map/ppermute | solution.py:327
  63.6 5.1 %collective-permute-start.23 = (bf16[32,2304]{1,0:T(8,128)(2,1)S(1)}, bf16[32,2304]{1,0:T(8,128)(2,1)S(1)}, u32[]{:S(2)}, u32[]{:S(2)}) collective-permute-start(bf16[32,2304]{1,0:T(8,128)(2,1)S(1)} %add_convert_fusion.a_ref), channel_id=1, source_target_pairs={{0,32},{1,3},{2,34},{3,1},{4,36},{5,7},{6,38},{7,5},{8,40},{9,11},... | collective-permute-start | bytes 442376 | tf_op jit(solution)/shard_map/ppermute | solution.py:327

commit v5 on v4

--- a/solution.py
+++ b/solution.py
@@ -225,22 +225,39 @@
     return work[:, RANK:] * lax.rsqrt(pivots)
 
 
-def right_kernel(keep_ref, took_ref, own_ref, other_ref, basis_ref, basis_b_ref, right_ref):
+def dot3(terms, b):
+    n = terms.shape[0] // 3
+    x = dot(terms, b, ((1,), (0,)))
+    return x[:n] + (x[n : 2 * n] + x[2 * n :])
+
+
+def dot6(a, b):
+    n = a.shape[0]
+    terms = split3(a)
+    parts = []
+    for drop in range(3):
+        part = b.astype(BF)
+        b = b - part.astype(F32)
+        x = dot(terms[: (3 - drop) * n], part, ((1,), (0,)))
+        parts.append([x[i * n : (i + 1) * n] for i in range(3 - drop)])
+    (x11, x21, x31), (x12, x22), (x13,) = parts
+    return x11 + ((x21 + x12) + (x31 + (x22 + x13)))
+
+
+def right_kernel(keep_ref, took_ref, own_ref, other_ref, inverse_ref, sums_ref, right_ref):
     me = lax.axis_index("tensor")
     keep, took = keep_ref[...], took_ref[...]
     sums = jnp.concatenate([jnp.where(me == 0, keep, took), jnp.where(me == 0, took, keep)], 0)
-    gram = dot(sums, sums, ((1,), (1,)), HI)
+    sums_ref[...] = sums
     terms = split3(sums)
-    halves = []
-    for ref in (own_ref, other_ref):
-        x = dot(terms, ref[...], ((1,), (0,)))
-        halves.append(x[:RANK] + (x[RANK : 2 * RANK] + x[2 * RANK :]))
+    pairs = dot(terms, terms, ((1,), (1,)))
+    blocks = [[pairs[i * RANK : (i + 1) * RANK, j * RANK : (j + 1) * RANK] for j in range(3)] for i in range(3)]
+    gram = blocks[0][0] + ((blocks[0][1] + blocks[1][0]) + (blocks[1][1] + (blocks[0][2] + blocks[2][0])))
+    halves = [dot3(terms, ref[...]) for ref in (own_ref, other_ref)]
     inverse = inverse_factor(gram)
-    basis = dot(inverse, sums, ((1,), (0,)), HI)
-    basis_ref[...] = basis
-    basis_b_ref[...] = basis.astype(BF)
+    inverse_ref[...] = inverse
     for half, who in zip(halves, (me, 1 - me)):
-        right_ref[:, columns(who)] = dot(inverse, half, ((1,), (0,)), HI).astype(BF)
+        right_ref[:, columns(who)] = dot6(inverse, half).astype(BF)
 
 
 def right_part(keep, took, own, other):
@@ -248,10 +265,27 @@
         right_kernel,
         "right_part",
         [WHOLE] * 4,
-        [pltpu.VMEM((RANK, ROWS), F32), pltpu.VMEM((RANK, ROWS), BF), pltpu.VMEM((RANK, WIDTH), BF)],
+        [pltpu.VMEM((RANK, RANK), F32), pltpu.VMEM((RANK, ROWS), F32), pltpu.VMEM((RANK, WIDTH), BF)],
         flops=2 * RANK * ROWS * WIDTH,
         bytes_accessed=2 * ROWS * WIDTH,
     )(keep, took, in_vmem(own), in_vmem(other))
+
+
+def basis_kernel(inverse_ref, sums_ref, basis_ref, basis_b_ref):
+    basis = dot(inverse_ref[...], sums_ref[...], ((1,), (0,)), HI)
+    basis_ref[...] = basis
+    basis_b_ref[...] = basis.astype(BF)
+
+
+def basis_part(inverse, sums):
+    return call(
+        basis_kernel,
+        "basis_part",
+        [WHOLE] * 2,
+        [pltpu.VMEM((RANK, ROWS), F32), pltpu.VMEM((RANK, ROWS), BF)],
+        flops=12 * RANK * RANK * ROWS,
+        bytes_accessed=10**6,
+    )(in_vmem(inverse), in_vmem(sums))
 
 
 STEP = 192
@@ -361,7 +395,8 @@
     part, own = add_after(terms, corrected_half(False, part, acts, grad_out, own_err))
     terms = spread(part, third)
     part, other = add_after(terms, corrected_half(True, part, acts, grad_out, other_err))
-    basis_t, basis_b, right = right_part(part, lax.ppermute(part, "tensor", SWAP), own, other)
+    inverse, sums, right = right_part(part, lax.ppermute(part, "tensor", SWAP), own, other)
+    basis_t, basis_b = basis_part(inverse, sums)
     first, second, third = stages((1, 1, 0))
     for stage in (first, second):
         right = add4(spread(right, stage)).astype(BF)

time: 73.6 us -> 73.2 us (level)
    pallas_call x1 -> x2, Pallas kernels: 3.01 us -> 3.11 us  [the longest x1 2.74 us: right_part(): call(right_kernel, 'right_part', [WHOLE] * 4, [pltpu.VMEM((RANK, RANK), F...]
where the time goes in v5:
time: 73.2 us; the launch traced here: 73 us
  starting transfers between devices  28.9 us (39%)
  Pallas kernels  26.3 us (36%)
  waiting for transfers between devices  15.9 us (22%)
  between operations  1 us (1%)
    ppermute x18, starting transfers between devices, spread(): lax.ppermute(x, AXES, ring_pairs(axes, flip, cross))  25.5 us
    ppermute x18, waiting for transfers between devices, spread(): lax.ppermute(x, AXES, ring_pairs(axes, flip, cross))  13.8 us
    pallas_call x2, Pallas kernels, corrected_half(): call(functools.partial(half_kernel, other), 'corrected_other' if other el...  7.4 us
    pallas_call x1, Pallas kernels, load_part(): call(load_kernel, 'load_part', [FAR] * 5, [pltpu.VMEM((RANK, ROWS), F32),...  6.07 us
    pallas_call x1, Pallas kernels, residue(): call(functools.partial(residue_kernel, scale), 'residue', [WHOLE] * 7, [p...  4.59 us
    pallas_call x1, Pallas kernels, send_part(): call(send_kernel, 'send_part', [SCALARS, pl.BlockSpec(memory_space=pl.ANY...  3.14 us
    pallas_call x1, Pallas kernels, right_part(): call(right_kernel, 'right_part', [WHOLE] * 4, [pltpu.VMEM((RANK, RANK), F...  2.74 us
    pallas_call x1, Pallas kernels, term_part(): call(term_kernel, 'term_part', [SCALARS] + [WHOLE] * 5, [half, half], [pl...  1.89 us
  transfers between devices with their start and end apart: 26, of which 12 were waited for; matrix products, arithmetic and copies ran while one was open for 1% of the time, Pallas kernels for 23%

profile of v5, /device:TPU:0, one launch (start us, length us, event | category | flops | bytes accessed | tf_op | source)
XLA Modules:
  0.0 73.0 jit_solution(14934040390193194343)
XLA Ops:
  0.7 0.1 collective-permute-start
  0.7 6.1 %load_part.1 = (f32[32,2304]{1,0:T(8,128)S(1)}, bf16[2304,1152]{1,0:T(8,128)(2,1)S(1)}, bf16[2304,2304]{1,0:T(8,128)(2,1)S(1)}, bf16[512,2304]{1,0:T(8,128)(2,1)S(1)}, bf16[512,2304]{1,0:T(8,128)(2,1)S(1)}) custom-call(s32[8]{0:T(128)} %order_ref.3, bf16[32,2304]{1,0:T(8,128)(2,1)} %fac_ref.1, bf16[2304,2304]{1,0:T(8,128)(2,1)} %far_err.1, ...), custom_call_target="tpu_custom_call" | custom-call | flops 339738624 | bytes 10616832 | tf_op jit(solution)/shard_map/load_part/pallas_call | solution.py:109
  6.8 0.0 collective-permute-done.other_ref
  6.8 1.9 %term_part.1 = (f32[16,2304]{1,0:T(8,128)S(1)}, f32[16,2304]{1,0:T(8,128)S(1)}) custom-call(s32[8]{0:T(128)S(1)} %copy-done.1, bf16[32,2304]{1,0:T(8,128)(2,1)S(1)} %copy-done, bf16[32,2304]{1,0:T(8,128)(2,1)S(1)} %collective-permute-done.other_ref, f32[32,2304]{1,0:T(8,128)S(1)} %get-tuple-element.23.left_ref, ...), custom_call_target="tpu_custom_call" | custom-call | flops 150994944 | bytes 5000000 | tf_op jit(solution)/shard_map/term_part/pallas_call | solution.py:146
  8.7 0.6 collective-permute-start.1
  9.3 1.0 %collective-permute-done.1 = f32[16,2304]{1,0:T(8,128)S(1)} collective-permute-done((f32[16,2304]{1,0:T(8,128)S(1)}, f32[16,2304]{1,0:T(8,128)S(1)}, u32[]{:S(2)}, u32[]{:S(2)}) %collective-permute-start.1) | collective-permute-done | bytes 147488 | tf_op jit(solution)/shard_map/ppermute | solution.py:389
  10.3 3.1 %collective-permute-start.5 = (f32[16,2304]{1,0:T(8,128)S(1)}, f32[16,2304]{1,0:T(8,128)S(1)}, u32[]{:S(2)}, u32[]{:S(2)}) collective-permute-start(f32[16,2304]{1,0:T(8,128)S(1)} %add.21.after_ref), channel_id=1, source_target_pairs={{0,5},{1,16},{2,7},{3,18},{4,1},{5,20},{6,3},{7,22},{8,13},{9,24},... | collective-permute-start | bytes 442376 | tf_op jit(solution)/shard_map/ppermute | solution.py:361
  13.5 2.7 %collective-permute-start.4 = (f32[16,2304]{1,0:T(8,128)S(1)}, f32[16,2304]{1,0:T(8,128)S(1)}, u32[]{:S(2)}, u32[]{:S(2)}) collective-permute-start(f32[16,2304]{1,0:T(8,128)S(1)} %add.21.after_ref), channel_id=1, source_target_pairs={{0,7},{1,24},{2,5},{3,26},{4,3},{5,28},{6,1},{7,30},{8,15},{9,16},... | collective-permute-start | bytes 442376 | tf_op jit(solution)/shard_map/ppermute | solution.py:361
  16.2 0.6 collective-permute-start.3
  16.8 0.1 collective-permute-start.2
  17.0 3.1 %send_part.1.work_ref = bf16[2304,1152]{1,0:T(8,128)(2,1)S(1)} custom-call(s32[8]{0:T(128)S(1)} %copy-done.1, f32[16,2304]{1,0:T(8,128)S(1)} %add.21.after_ref, bf16[2304,2304]{1,0:T(8,128)(2,1)S(1)} %get-tuple-element.28.err_ref), custom_call_target="tpu_custom_call" | custom-call | flops 1000000000 | bytes 4000000 | tf_op jit(solution)/shard_map/send_part/pallas_call | solution.py:166
  20.1 0.6 collective-permute-done.3.b_ref
  20.8 0.5 collective-permute-start.13
  21.3 3.9 %collective-permute-start.8 = (f32[16,2304]{1,0:T(8,128)S(1)}, f32[16,2304]{1,0:T(8,128)S(1)}, u32[]{:S(2)}, u32[]{:S(2)}) collective-permute-start(f32[16,2304]{1,0:T(8,128)S(1)} %get-tuple-element.29.after_ref.a_ref), channel_id=1, source_target_pairs={{0,64},{1,17},{2,66},{3,19},{4,68},{5,21},{6,70},{7,23},{8,72},{9,... | collective-permute-start | bytes 442376 | tf_op jit(solution)/shard_map/ppermute | solution.py:361
  25.2 0.7 collective-permute-start.7
  25.9 0.3 collective-permute-start.6
  26.2 3.7 %corrected_own.1.work_ref = bf16[2304,1152]{1,0:T(8,128)(2,1)S(1)} custom-call(f32[16,2304]{1,0:T(8,128)S(1)} %get-tuple-element.29.after_ref.a_ref, bf16[512,2304]{1,0:T(8,128)(2,1)S(1)} %get-tuple-element.24.acts_ref, bf16[512,2304]{1,0:T(8,128)(2,1)S(1)} %get-tuple-element.25.grad_ref, bf16[2304,1152]{1,0:T(8,128)(2,1)S(1)} %get-tuple-element.30.err_ref), custom_call_target="tpu_custom_call" | custom-call | flops 2717908992 | bytes 8000000 | tf_op jit(solution)/shard_map/corrected_own/pallas_call | solution.py:190
  29.9 1.6 %collective-permute-done.7.c_ref = f32[16,2304]{1,0:T(8,128)S(1)} collective-permute-done((f32[16,2304]{1,0:T(8,128)S(1)}, f32[16,2304]{1,0:T(8,128)S(1)}, u32[]{:S(2)}, u32[]{:S(2)}) %collective-permute-start.7) | collective-permute-done | bytes 147488 | tf_op jit(solution)/shard_map/ppermute | solution.py:361
  31.6 0.1 collective-permute-start.12
  31.7 2.9 %collective-permute-start.11 = (f32[16,2304]{1,0:T(8,128)S(1)}, f32[16,2304]{1,0:T(8,128)S(1)}, u32[]{:S(2)}, u32[]{:S(2)}) collective-permute-start(f32[16,2304]{1,0:T(8,128)S(1)} %get-tuple-element.31.after_ref), channel_id=1, source_target_pairs={{0,7},{1,96},{2,5},{3,98},{4,3},{5,100},{6,1},{7,102},{8,15},{9,10... | collective-permute-start | bytes 442376 | tf_op jit(solution)/shard_map/ppermute | solution.py:361
  34.6 0.9 %collective-permute-start.9 = (f32[16,2304]{1,0:T(8,128)S(1)}, f32[16,2304]{1,0:T(8,128)S(1)}, u32[]{:S(2)}, u32[]{:S(2)}) collective-permute-start(f32[16,2304]{1,0:T(8,128)S(1)} %get-tuple-element.31.after_ref), channel_id=1, source_target_pairs={{0,1},{1,0},{2,3},{3,2},{4,5},{5,4},{6,7},{7,6},{8,9},{9,8},{10,11... | collective-permute-start | bytes 442376 | tf_op jit(solution)/shard_map/ppermute | solution.py:362
  35.5 3.7 %corrected_other.1.work_ref = bf16[2304,1152]{1,0:T(8,128)(2,1)S(1)} custom-call(f32[16,2304]{1,0:T(8,128)S(1)} %get-tuple-element.31.after_ref, bf16[512,2304]{1,0:T(8,128)(2,1)S(1)} %get-tuple-element.24.acts_ref, bf16[512,2304]{1,0:T(8,128)(2,1)S(1)} %get-tuple-element.25.grad_ref, bf16[2304,1152]{1,0:T(8,128)(2,1)S(1)} %collective-permute-done.13.err_ref), custom_call_target="tpu_custom_call" | custom-call | flops 2717908992 | bytes 8000000 | tf_op jit(solution)/shard_map/corrected_other/pallas_call | solution.py:190
  39.3 0.4 collective-permute-start.14
  39.7 1.1 %collective-permute-done.14.took_ref = f32[16,2304]{1,0:T(8,128)S(1)} collective-permute-done((f32[16,2304]{1,0:T(8,128)S(1)}, f32[16,2304]{1,0:T(8,128)S(1)}, u32[]{:S(2)}, u32[]{:S(2)}) %collective-permute-start.14) | collective-permute-done | bytes 147488 | tf_op jit(solution)/shard_map/ppermute | solution.py:398
  40.8 2.7 %right_part.1 = (f32[32,32]{1,0:T(8,128)S(1)}, f32[32,2304]{1,0:T(8,128)S(1)}, bf16[32,2304]{1,0:T(8,128)(2,1)S(1)}) custom-call(f32[16,2304]{1,0:T(8,128)S(1)} %get-tuple-element.33.keep_ref, f32[16,2304]{1,0:T(8,128)S(1)} %collective-permute-done.14.took_ref, bf16[2304,1152]{1,0:T(8,128)(2,1)S(1)} %get-tuple-element.34.own_ref, ...), custom_call_target="tpu_custom_call" | custom-call | flops 339738624 | bytes 10616832 | tf_op jit(solution)/shard_map/right_part/pallas_call | solution.py:264
  43.5 1.7 %collective-permute-start.18 = (bf16[32,2304]{1,0:T(8,128)(2,1)S(1)}, bf16[32,2304]{1,0:T(8,128)(2,1)S(1)}, u32[]{:S(2)}, u32[]{:S(2)}) collective-permute-start(bf16[32,2304]{1,0:T(8,128)(2,1)S(1)} %get-tuple-element.36), channel_id=1, source_target_pairs={{0,5},{1,16},{2,7},{3,18},{4,1},{5,20},{6,3},{7,22},{8,13},{9,24},... | collective-permute-start | bytes 442376 | tf_op jit(solution)/shard_map/ppermute | solution.py:361
  45.2 1.3 %collective-permute-start.17 = (bf16[32,2304]{1,0:T(8,128)(2,1)S(1)}, bf16[32,2304]{1,0:T(8,128)(2,1)S(1)}, u32[]{:S(2)}, u32[]{:S(2)}) collective-permute-start(bf16[32,2304]{1,0:T(8,128)(2,1)S(1)} %get-tuple-element.36), channel_id=1, source_target_pairs={{0,7},{1,24},{2,5},{3,26},{4,3},{5,28},{6,1},{7,30},{8,15},{9,16},... | collective-permute-start | bytes 442376 | tf_op jit(solution)/shard_map/ppermute | solution.py:361
  46.5 0.7 collective-permute-start.16
  47.2 0.4 collective-permute-start.15
  47.6 2.1 %collective-permute-done.18 = bf16[32,2304]{1,0:T(8,128)(2,1)S(1)} collective-permute-done((bf16[32,2304]{1,0:T(8,128)(2,1)S(1)}, bf16[32,2304]{1,0:T(8,128)(2,1)S(1)}, u32[]{:S(2)}, u32[]{:S(2)}) %collective-permute-start.18) | collective-permute-done | bytes 147488 | tf_op jit(solution)/shard_map/ppermute | solution.py:361
  49.7 1.6 %collective-permute-done.17 = bf16[32,2304]{1,0:T(8,128)(2,1)S(1)} collective-permute-done((bf16[32,2304]{1,0:T(8,128)(2,1)S(1)}, bf16[32,2304]{1,0:T(8,128)(2,1)S(1)}, u32[]{:S(2)}, u32[]{:S(2)}) %collective-permute-start.17) | collective-permute-done | bytes 147488 | tf_op jit(solution)/shard_map/ppermute | solution.py:361
  51.3 0.1 add_convert_fusion.1
  51.3 1.7 %collective-permute-start.22 = (bf16[32,2304]{1,0:T(8,128)(2,1)S(1)}, bf16[32,2304]{1,0:T(8,128)(2,1)S(1)}, u32[]{:S(2)}, u32[]{:S(2)}) collective-permute-start(bf16[32,2304]{1,0:T(8,128)(2,1)S(1)} %add_convert_fusion.1), channel_id=1, source_target_pairs={{0,65},{1,16},{2,67},{3,18},{4,69},{5,20},{6,71},{7,22},{8,73},{9,... | collective-permute-start | bytes 442376 | tf_op jit(solution)/shard_map/ppermute | solution.py:361
  53.0 1.6 %collective-permute-start.21 = (bf16[32,2304]{1,0:T(8,128)(2,1)S(1)}, bf16[32,2304]{1,0:T(8,128)(2,1)S(1)}, u32[]{:S(2)}, u32[]{:S(2)}) collective-permute-start(bf16[32,2304]{1,0:T(8,128)(2,1)S(1)} %add_convert_fusion.1), channel_id=1, source_target_pairs={{0,97},{1,24},{2,99},{3,26},{4,101},{5,28},{6,103},{7,30},{8,105},... | collective-permute-start | bytes 442376 | tf_op jit(solution)/shard_map/ppermute | solution.py:361
  54.6 0.4 collective-permute-start.20
  55.0 0.4 collective-permute-start.19
  55.3 2.2 %collective-permute-done.22 = bf16[32,2304]{1,0:T(8,128)(2,1)S(1)} collective-permute-done((bf16[32,2304]{1,0:T(8,128)(2,1)S(1)}, bf16[32,2304]{1,0:T(8,128)(2,1)S(1)}, u32[]{:S(2)}, u32[]{:S(2)}) %collective-permute-start.22) | collective-permute-done | bytes 147488 | tf_op jit(solution)/shard_map/ppermute | solution.py:361
  57.5 1.6 %collective-permute-done.21 = bf16[32,2304]{1,0:T(8,128)(2,1)S(1)} collective-permute-done((bf16[32,2304]{1,0:T(8,128)(2,1)S(1)}, bf16[32,2304]{1,0:T(8,128)(2,1)S(1)}, u32[]{:S(2)}, u32[]{:S(2)}) %collective-permute-start.21) | collective-permute-done | bytes 147488 | tf_op jit(solution)/shard_map/ppermute | solution.py:361
  59.1 0.1 collective-permute-done.20
  59.2 0.1 add_convert_fusion.a_ref
  59.2 2.1 %collective-permute-start.25 = (bf16[32,2304]{1,0:T(8,128)(2,1)S(1)}, bf16[32,2304]{1,0:T(8,128)(2,1)S(1)}, u32[]{:S(2)}, u32[]{:S(2)}) collective-permute-start(bf16[32,2304]{1,0:T(8,128)(2,1)S(1)} %add_convert_fusion.a_ref), channel_id=1, source_target_pairs={{0,64},{1,5},{2,66},{3,7},{4,68},{5,1},{6,70},{7,3},{8,72},{9,13},... | collective-permute-start | bytes 442376 | tf_op jit(solution)/shard_map/ppermute | solution.py:361
  61.4 1.7 %collective-permute-start.24 = (bf16[32,2304]{1,0:T(8,128)(2,1)S(1)}, bf16[32,2304]{1,0:T(8,128)(2,1)S(1)}, u32[]{:S(2)}, u32[]{:S(2)}) collective-permute-start(bf16[32,2304]{1,0:T(8,128)(2,1)S(1)} %add_convert_fusion.a_ref), channel_id=1, source_target_pairs={{0,96},{1,7},{2,98},{3,5},{4,100},{5,3},{6,102},{7,1},{8,104},{9,1... | collective-permute-start | bytes 442376 | tf_op jit(solution)/shard_map/ppermute | solution.py:361
  63.1 0.4 basis_part.1
  63.5 0.7 copy.14
  64.2 1.8 %collective-permute-done.25.d_ref = bf16[32,2304]{1,0:T(8,128)(2,1)S(1)} collective-permute-done((bf16[32,2304]{1,0:T(8,128)(2,1)S(1)}, bf16[32,2304]{1,0:T(8,128)(2,1)S(1)}, u32[]{:S(2)}, u32[]{:S(2)}) %collective-permute-start.25) | collective-permute-done | bytes 147488 | tf_op jit(solution)/shard_map/ppermute | solution.py:361
  66.0 1.8 %collective-permute-done.24.c_ref = bf16[32,2304]{1,0:T(8,128)(2,1)S(1)} collective-permute-done((bf16[32,2304]{1,0:T(8,128)(2,1)S(1)}, bf16[32,2304]{1,0:T(8,128)(2,1)S(1)}, u32[]{:S(2)}, u32[]{:S(2)}) %collective-permute-start.24) | collective-permute-done | bytes 147488 | tf_op jit(solution)/shard_map/ppermute | solution.py:361
  67.7 0.5 collective-permute-done.23.b_ref
  68.3 4.6 %residue.1 = (bf16[2304,2304]{1,0:T(8,128)(2,1)}, f32[32,2304]{1,0:T(8,128)}) custom-call(bf16[32,2304]{1,0:T(8,128)(2,1)S(1)} %add_convert_fusion.a_ref, bf16[32,2304]{1,0:T(8,128)(2,1)S(1)} %collective-permute-done.23.b_ref, bf16[32,2304]{1,0:T(8,128)(2,1)S(1)} %collective-permute-done.24.c_ref, bf16[32,2304]{1,0:T(8,128)(2,1)S(1)} %collective-permute-done.25.d_ref, ...), custom_call_target="tpu_custom_call" | custom-call | flops 339738624 | bytes 10616832 | tf_op jit(solution)/shard_map/residue/pallas_call | solution.py:320
  (23 shorter events, 0.2 us)
Async XLA Ops:
  0.6 6.2 %copy-start = (bf16[32,2304]{1,0:T(8,128)(2,1)S(1)}, bf16[32,2304]{1,0:T(8,128)(2,1)}, u32[]{:S(2)}) copy-start(bf16[32,2304]{1,0:T(8,128)(2,1)} %fac_ref.1) | copy-start | bytes 442372
  0.6 6.2 %copy-start.1 = (s32[8]{0:T(128)S(1)}, s32[8]{0:T(128)}, u32[]{:S(2)}) copy-start(s32[8]{0:T(128)} %order_ref.3) | copy-start | bytes 100
  0.7 6.2 %collective-permute-start = (bf16[32,2304]{1,0:T(8,128)(2,1)}, bf16[32,2304]{1,0:T(8,128)(2,1)S(1)}, u32[]{:S(2)}, u32[]{:S(2)}) collective-permute-start(bf16[32,2304]{1,0:T(8,128)(2,1)} %fac_ref.1), channel_id=1, source_target_pairs={{0,1},{1,0},{2,3},{3,2},{4,5},{5,4},{6,7},{7,6},{8,9},{9,8},{10,11... | collective-permute-start | bytes 442376 | tf_op jit(solution)/shard_map/ppermute | solution.py:386
  8.7 1.6 %collective-permute-start.1 = (f32[16,2304]{1,0:T(8,128)S(1)}, f32[16,2304]{1,0:T(8,128)S(1)}, u32[]{:S(2)}, u32[]{:S(2)}) collective-permute-start(f32[16,2304]{1,0:T(8,128)S(1)} %get-tuple-element.27), channel_id=1, source_target_pairs={{0,1},{1,0},{2,3},{3,2},{4,5},{5,4},{6,7},{7,6},{8,9},{9,8},{10,11... | collective-permute-start | bytes 442376 | tf_op jit(solution)/shard_map/ppermute | solution.py:389
  10.3 9.8 %collective-permute-start.5 = (f32[16,2304]{1,0:T(8,128)S(1)}, f32[16,2304]{1,0:T(8,128)S(1)}, u32[]{:S(2)}, u32[]{:S(2)}) collective-permute-start(f32[16,2304]{1,0:T(8,128)S(1)} %add.21.after_ref), channel_id=1, source_target_pairs={{0,5},{1,16},{2,7},{3,18},{4,1},{5,20},{6,3},{7,22},{8,13},{9,24},... | collective-permute-start | bytes 442376 | tf_op jit(solution)/shard_map/ppermute | solution.py:361
  13.5 6.6 %collective-permute-start.4 = (f32[16,2304]{1,0:T(8,128)S(1)}, f32[16,2304]{1,0:T(8,128)S(1)}, u32[]{:S(2)}, u32[]{:S(2)}) collective-permute-start(f32[16,2304]{1,0:T(8,128)S(1)} %add.21.after_ref), channel_id=1, source_target_pairs={{0,7},{1,24},{2,5},{3,26},{4,3},{5,28},{6,1},{7,30},{8,15},{9,16},... | collective-permute-start | bytes 442376 | tf_op jit(solution)/shard_map/ppermute | solution.py:361
  16.2 4.6 %collective-permute-start.3 = (f32[16,2304]{1,0:T(8,128)S(1)}, f32[16,2304]{1,0:T(8,128)S(1)}, u32[]{:S(2)}, u32[]{:S(2)}) collective-permute-start(f32[16,2304]{1,0:T(8,128)S(1)} %add.21.after_ref), channel_id=1, source_target_pairs={{0,3},{1,8},{2,1},{3,10},{4,7},{5,12},{6,5},{7,14},{8,11},{9,0},{1... | collective-permute-start | bytes 442376 | tf_op jit(solution)/shard_map/ppermute | solution.py:361
  16.8 3.9 %collective-permute-start.2 = (f32[16,2304]{1,0:T(8,128)S(1)}, f32[16,2304]{1,0:T(8,128)S(1)}, u32[]{:S(2)}, u32[]{:S(2)}) collective-permute-start(f32[16,2304]{1,0:T(8,128)S(1)} %add.21.after_ref), channel_id=1, source_target_pairs={{0,1},{1,0},{2,3},{3,2},{4,5},{5,4},{6,7},{7,6},{8,9},{9,8},{10,11... | collective-permute-start | bytes 442376 | tf_op jit(solution)/shard_map/ppermute | solution.py:362
  20.8 14.8 %collective-permute-start.13 = (bf16[2304,1152]{1,0:T(8,128)(2,1)S(1)}, bf16[2304,1152]{1,0:T(8,128)(2,1)S(1)}, u32[]{:S(2)}, u32[]{:S(2)}) collective-permute-start(bf16[2304,1152]{1,0:T(8,128)(2,1)S(1)} %get-tuple-element.32), channel_id=1, source_target_pairs={{0,1},{1,0},{2,3},{3,2},{4,5},{5,4},{6,7},{7,6},{8,9},{9,8},{10,11... | collective-permute-start | bytes 15925256 | tf_op jit(solution)/shard_map/ppermute | solution.py:393
  21.3 8.6 %collective-permute-start.8 = (f32[16,2304]{1,0:T(8,128)S(1)}, f32[16,2304]{1,0:T(8,128)S(1)}, u32[]{:S(2)}, u32[]{:S(2)}) collective-permute-start(f32[16,2304]{1,0:T(8,128)S(1)} %get-tuple-element.29.after_ref.a_ref), channel_id=1, source_target_pairs={{0,64},{1,17},{2,66},{3,19},{4,68},{5,21},{6,70},{7,23},{8,72},{9,... | collective-permute-start | bytes 442376 | tf_op jit(solution)/shard_map/ppermute | solution.py:361
  25.2 6.4 %collective-permute-start.7 = (f32[16,2304]{1,0:T(8,128)S(1)}, f32[16,2304]{1,0:T(8,128)S(1)}, u32[]{:S(2)}, u32[]{:S(2)}) collective-permute-start(f32[16,2304]{1,0:T(8,128)S(1)} %get-tuple-element.29.after_ref.a_ref), channel_id=1, source_target_pairs={{0,96},{1,25},{2,98},{3,27},{4,100},{5,29},{6,102},{7,31},{8,104},... | collective-permute-start | bytes 442376 | tf_op jit(solution)/shard_map/ppermute | solution.py:361
  25.9 5.7 %collective-permute-start.6 = (f32[16,2304]{1,0:T(8,128)S(1)}, f32[16,2304]{1,0:T(8,128)S(1)}, u32[]{:S(2)}, u32[]{:S(2)}) collective-permute-start(f32[16,2304]{1,0:T(8,128)S(1)} %get-tuple-element.29.after_ref.a_ref), channel_id=1, source_target_pairs={{0,32},{1,9},{2,34},{3,11},{4,36},{5,13},{6,38},{7,15},{8,40},{9,1... | collective-permute-start | bytes 442376 | tf_op jit(solution)/shard_map/ppermute | solution.py:361
  31.6 7.7 %collective-permute-start.12 = (f32[16,2304]{1,0:T(8,128)S(1)}, f32[16,2304]{1,0:T(8,128)S(1)}, u32[]{:S(2)}, u32[]{:S(2)}) collective-permute-start(f32[16,2304]{1,0:T(8,128)S(1)} %get-tuple-element.31.after_ref), channel_id=1, source_target_pairs={{0,5},{1,64},{2,7},{3,66},{4,1},{5,68},{6,3},{7,70},{8,13},{9,72},... | collective-permute-start | bytes 442376 | tf_op jit(solution)/shard_map/ppermute | solution.py:361
  31.7 7.6 %collective-permute-start.11 = (f32[16,2304]{1,0:T(8,128)S(1)}, f32[16,2304]{1,0:T(8,128)S(1)}, u32[]{:S(2)}, u32[]{:S(2)}) collective-permute-start(f32[16,2304]{1,0:T(8,128)S(1)} %get-tuple-element.31.after_ref), channel_id=1, source_target_pairs={{0,7},{1,96},{2,5},{3,98},{4,3},{5,100},{6,1},{7,102},{8,15},{9,10... | collective-permute-start | bytes 442376 | tf_op jit(solution)/shard_map/ppermute | solution.py:361
  34.6 4.7 %collective-permute-start.10 = (f32[16,2304]{1,0:T(8,128)S(1)}, f32[16,2304]{1,0:T(8,128)S(1)}, u32[]{:S(2)}, u32[]{:S(2)}) collective-permute-start(f32[16,2304]{1,0:T(8,128)S(1)} %get-tuple-element.31.after_ref), channel_id=1, source_target_pairs={{0,3},{1,32},{2,1},{3,34},{4,7},{5,36},{6,5},{7,38},{8,11},{9,40},... | collective-permute-start | bytes 442376 | tf_op jit(solution)/shard_map/ppermute | solution.py:361
  34.6 4.7 %collective-permute-start.9 = (f32[16,2304]{1,0:T(8,128)S(1)}, f32[16,2304]{1,0:T(8,128)S(1)}, u32[]{:S(2)}, u32[]{:S(2)}) collective-permute-start(f32[16,2304]{1,0:T(8,128)S(1)} %get-tuple-element.31.after_ref), channel_id=1, source_target_pairs={{0,1},{1,0},{2,3},{3,2},{4,5},{5,4},{6,7},{7,6},{8,9},{9,8},{10,11... | collective-permute-start | bytes 442376 | tf_op jit(solution)/shard_map/ppermute | solution.py:362
  39.3 1.5 %collective-permute-start.14 = (f32[16,2304]{1,0:T(8,128)S(1)}, f32[16,2304]{1,0:T(8,128)S(1)}, u32[]{:S(2)}, u32[]{:S(2)}) collective-permute-start(f32[16,2304]{1,0:T(8,128)S(1)} %get-tuple-element.33.keep_ref), channel_id=1, source_target_pairs={{0,1},{1,0},{2,3},{3,2},{4,5},{5,4},{6,7},{7,6},{8,9},{9,8},{10,11... | collective-permute-start | bytes 442376 | tf_op jit(solution)/shard_map/ppermute | solution.py:398
  43.5 6.2 %collective-permute-start.18 = (bf16[32,2304]{1,0:T(8,128)(2,1)S(1)}, bf16[32,2304]{1,0:T(8,128)(2,1)S(1)}, u32[]{:S(2)}, u32[]{:S(2)}) collective-permute-start(bf16[32,2304]{1,0:T(8,128)(2,1)S(1)} %get-tuple-element.36), channel_id=1, source_target_pairs={{0,5},{1,16},{2,7},{3,18},{4,1},{5,20},{6,3},{7,22},{8,13},{9,24},... | collective-permute-start | bytes 442376 | tf_op jit(solution)/shard_map/ppermute | solution.py:361
  45.2 6.0 %collective-permute-start.17 = (bf16[32,2304]{1,0:T(8,128)(2,1)S(1)}, bf16[32,2304]{1,0:T(8,128)(2,1)S(1)}, u32[]{:S(2)}, u32[]{:S(2)}) collective-permute-start(bf16[32,2304]{1,0:T(8,128)(2,1)S(1)} %get-tuple-element.36), channel_id=1, source_target_pairs={{0,7},{1,24},{2,5},{3,26},{4,3},{5,28},{6,1},{7,30},{8,15},{9,16},... | collective-permute-start | bytes 442376 | tf_op jit(solution)/shard_map/ppermute | solution.py:361
  46.5 4.7 %collective-permute-start.16 = (bf16[32,2304]{1,0:T(8,128)(2,1)S(1)}, bf16[32,2304]{1,0:T(8,128)(2,1)S(1)}, u32[]{:S(2)}, u32[]{:S(2)}) collective-permute-start(bf16[32,2304]{1,0:T(8,128)(2,1)S(1)} %get-tuple-element.36), channel_id=1, source_target_pairs={{0,3},{1,8},{2,1},{3,10},{4,7},{5,12},{6,5},{7,14},{8,11},{9,0},{1... | collective-permute-start | bytes 442376 | tf_op jit(solution)/shard_map/ppermute | solution.py:361
  47.2 4.1 %collective-permute-start.15 = (bf16[32,2304]{1,0:T(8,128)(2,1)S(1)}, bf16[32,2304]{1,0:T(8,128)(2,1)S(1)}, u32[]{:S(2)}, u32[]{:S(2)}) collective-permute-start(bf16[32,2304]{1,0:T(8,128)(2,1)S(1)} %get-tuple-element.36), channel_id=1, source_target_pairs={{0,1},{1,0},{2,3},{3,2},{4,5},{5,4},{6,7},{7,6},{8,9},{9,8},{10,11... | collective-permute-start | bytes 442376 | tf_op jit(solution)/shard_map/ppermute | solution.py:362
  51.3 6.2 %collective-permute-start.22 = (bf16[32,2304]{1,0:T(8,128)(2,1)S(1)}, bf16[32,2304]{1,0:T(8,128)(2,1)S(1)}, u32[]{:S(2)}, u32[]{:S(2)}) collective-permute-start(bf16[32,2304]{1,0:T(8,128)(2,1)S(1)} %add_convert_fusion.1), channel_id=1, source_target_pairs={{0,65},{1,16},{2,67},{3,18},{4,69},{5,20},{6,71},{7,22},{8,73},{9,... | collective-permute-start | bytes 442376 | tf_op jit(solution)/shard_map/ppermute | solution.py:361
  53.0 6.0 %collective-permute-start.21 = (bf16[32,2304]{1,0:T(8,128)(2,1)S(1)}, bf16[32,2304]{1,0:T(8,128)(2,1)S(1)}, u32[]{:S(2)}, u32[]{:S(2)}) collective-permute-start(bf16[32,2304]{1,0:T(8,128)(2,1)S(1)} %add_convert_fusion.1), channel_id=1, source_target_pairs={{0,97},{1,24},{2,99},{3,26},{4,101},{5,28},{6,103},{7,30},{8,105},... | collective-permute-start | bytes 442376 | tf_op jit(solution)/shard_map/ppermute | solution.py:361
  54.6 4.6 %collective-permute-start.20 = (bf16[32,2304]{1,0:T(8,128)(2,1)S(1)}, bf16[32,2304]{1,0:T(8,128)(2,1)S(1)}, u32[]{:S(2)}, u32[]{:S(2)}) collective-permute-start(bf16[32,2304]{1,0:T(8,128)(2,1)S(1)} %add_convert_fusion.1), channel_id=1, source_target_pairs={{0,33},{1,8},{2,35},{3,10},{4,37},{5,12},{6,39},{7,14},{8,41},{9,0... | collective-permute-start | bytes 442376 | tf_op jit(solution)/shard_map/ppermute | solution.py:361
  55.0 4.2 %collective-permute-start.19 = (bf16[32,2304]{1,0:T(8,128)(2,1)S(1)}, bf16[32,2304]{1,0:T(8,128)(2,1)S(1)}, u32[]{:S(2)}, u32[]{:S(2)}) collective-permute-start(bf16[32,2304]{1,0:T(8,128)(2,1)S(1)} %add_convert_fusion.1), channel_id=1, source_target_pairs={{0,1},{1,0},{2,3},{3,2},{4,5},{5,4},{6,7},{7,6},{8,9},{9,8},{10,11... | collective-permute-start | bytes 442376 | tf_op jit(solution)/shard_map/ppermute | solution.py:362
  59.2 6.7 %collective-permute-start.25 = (bf16[32,2304]{1,0:T(8,128)(2,1)S(1)}, bf16[32,2304]{1,0:T(8,128)(2,1)S(1)}, u32[]{:S(2)}, u32[]{:S(2)}) collective-permute-start(bf16[32,2304]{1,0:T(8,128)(2,1)S(1)} %add_convert_fusion.a_ref), channel_id=1, source_target_pairs={{0,64},{1,5},{2,66},{3,7},{4,68},{5,1},{6,70},{7,3},{8,72},{9,13},... | collective-permute-start | bytes 442376 | tf_op jit(solution)/shard_map/ppermute | solution.py:361
  61.4 6.4 %collective-permute-start.24 = (bf16[32,2304]{1,0:T(8,128)(2,1)S(1)}, bf16[32,2304]{1,0:T(8,128)(2,1)S(1)}, u32[]{:S(2)}, u32[]{:S(2)}) collective-permute-start(bf16[32,2304]{1,0:T(8,128)(2,1)S(1)} %add_convert_fusion.a_ref), channel_id=1, source_target_pairs={{0,96},{1,7},{2,98},{3,5},{4,100},{5,3},{6,102},{7,1},{8,104},{9,1... | collective-permute-start | bytes 442376 | tf_op jit(solution)/shard_map/ppermute | solution.py:361
  63.1 5.1 %collective-permute-start.23 = (bf16[32,2304]{1,0:T(8,128)(2,1)S(1)}, bf16[32,2304]{1,0:T(8,128)(2,1)S(1)}, u32[]{:S(2)}, u32[]{:S(2)}) collective-permute-start(bf16[32,2304]{1,0:T(8,128)(2,1)S(1)} %add_convert_fusion.a_ref), channel_id=1, source_target_pairs={{0,32},{1,3},{2,34},{3,1},{4,36},{5,7},{6,38},{7,5},{8,40},{9,11},... | collective-permute-start | bytes 442376 | tf_op jit(solution)/shard_map/ppermute | solution.py:361

commit v6 on v5

--- a/solution.py
+++ b/solution.py
@@ -359,7 +359,7 @@
 def spread(x, stage):
     axes, cross = stage
     terms = [lax.ppermute(x, AXES, ring_pairs(axes, flip, cross)) for flip in FLIPS]
-    return [lax.ppermute(x, "tensor", SWAP) if cross else x] + terms
+    return terms + [lax.ppermute(x, "tensor", SWAP) if cross else x]
 
 
 def add4(terms):

time: 73.2 us -> 74.1 us (1.012)
  waiting for transfers between devices: 15.9 us -> 17.2 us
    ppermute x18, waiting for transfers between devices: 13.8 us -> 15.1 us  [spread(): lax.ppermute(x, AXES, ring_pairs(axes, flip, cross))]
  transfers between devices with their start and end apart: 26 -> 26, of which waited for: 12 -> 11; matrix products, arithmetic and copies ran while one was open for 1% -> 1% of each run, Pallas kernels for 23% -> 23%
where the time goes in v6:
time: 74.1 us; the launch traced here: 73.7 us
  starting transfers between devices  28.4 us (38%)
  Pallas kernels  26.2 us (35%)
  waiting for transfers between devices  17.2 us (23%)
  between operations  1 us (1%)
    ppermute x18, starting transfers between devices, spread(): lax.ppermute(x, AXES, ring_pairs(axes, flip, cross))  25.9 us
    ppermute x18, waiting for transfers between devices, spread(): lax.ppermute(x, AXES, ring_pairs(axes, flip, cross))  15.1 us
    pallas_call x2, Pallas kernels, corrected_half(): call(functools.partial(half_kernel, other), 'corrected_other' if other el...  7.4 us
    pallas_call x1, Pallas kernels, load_part(): call(load_kernel, 'load_part', [FAR] * 5, [pltpu.VMEM((RANK, ROWS), F32),...  6.04 us
    pallas_call x1, Pallas kernels, residue(): call(functools.partial(residue_kernel, scale), 'residue', [WHOLE] * 7, [p...  4.6 us
    pallas_call x1, Pallas kernels, send_part(): call(send_kernel, 'send_part', [SCALARS, pl.BlockSpec(memory_space=pl.ANY...  3.11 us
    pallas_call x1, Pallas kernels, right_part(): call(right_kernel, 'right_part', [WHOLE] * 4, [pltpu.VMEM((RANK, RANK), F...  2.74 us
    pallas_call x1, Pallas kernels, term_part(): call(term_kernel, 'term_part', [SCALARS] + [WHOLE] * 5, [half, half], [pl...  1.89 us
  transfers between devices with their start and end apart: 26, of which 11 were waited for; matrix products, arithmetic and copies ran while one was open for 1% of the time, Pallas kernels for 23%

profile of v6, /device:TPU:0, one launch (start us, length us, event | category | flops | bytes accessed | tf_op | source)
XLA Modules:
  0.0 73.7 jit_solution(10959514987380653417)
XLA Ops:
  0.7 0.1 collective-permute-start
  0.7 6.0 %load_part.1 = (f32[32,2304]{1,0:T(8,128)S(1)}, bf16[2304,1152]{1,0:T(8,128)(2,1)S(1)}, bf16[2304,2304]{1,0:T(8,128)(2,1)S(1)}, bf16[512,2304]{1,0:T(8,128)(2,1)S(1)}, bf16[512,2304]{1,0:T(8,128)(2,1)S(1)}) custom-call(s32[8]{0:T(128)} %order_ref.3, bf16[32,2304]{1,0:T(8,128)(2,1)} %fac_ref.1, bf16[2304,2304]{1,0:T(8,128)(2,1)} %far_err.1, ...), custom_call_target="tpu_custom_call" | custom-call | flops 339738624 | bytes 10616832 | tf_op jit(solution)/shard_map/load_part/pallas_call | solution.py:109
  6.8 1.9 %term_part.1 = (f32[16,2304]{1,0:T(8,128)S(1)}, f32[16,2304]{1,0:T(8,128)S(1)}) custom-call(s32[8]{0:T(128)S(1)} %copy-done.1, bf16[32,2304]{1,0:T(8,128)(2,1)S(1)} %copy-done, bf16[32,2304]{1,0:T(8,128)(2,1)S(1)} %collective-permute-done.other_ref, f32[32,2304]{1,0:T(8,128)S(1)} %get-tuple-element.23.left_ref, ...), custom_call_target="tpu_custom_call" | custom-call | flops 150994944 | bytes 5000000 | tf_op jit(solution)/shard_map/term_part/pallas_call | solution.py:146
  8.7 0.6 collective-permute-start.1
  9.3 1.0 %collective-permute-done.1 = f32[16,2304]{1,0:T(8,128)S(1)} collective-permute-done((f32[16,2304]{1,0:T(8,128)S(1)}, f32[16,2304]{1,0:T(8,128)S(1)}, u32[]{:S(2)}, u32[]{:S(2)}) %collective-permute-start.1) | collective-permute-done | bytes 147488 | tf_op jit(solution)/shard_map/ppermute | solution.py:389
  10.3 0.4 collective-permute-start.5
  10.8 2.9 %collective-permute-start.4 = (f32[16,2304]{1,0:T(8,128)S(1)}, f32[16,2304]{1,0:T(8,128)S(1)}, u32[]{:S(2)}, u32[]{:S(2)}) collective-permute-start(f32[16,2304]{1,0:T(8,128)S(1)} %add.21.after_ref), channel_id=1, source_target_pairs={{0,5},{1,16},{2,7},{3,18},{4,1},{5,20},{6,3},{7,22},{8,13},{9,24},... | collective-permute-start | bytes 442376 | tf_op jit(solution)/shard_map/ppermute | solution.py:361
  13.6 2.9 %collective-permute-start.3 = (f32[16,2304]{1,0:T(8,128)S(1)}, f32[16,2304]{1,0:T(8,128)S(1)}, u32[]{:S(2)}, u32[]{:S(2)}) collective-permute-start(f32[16,2304]{1,0:T(8,128)S(1)} %add.21.after_ref), channel_id=1, source_target_pairs={{0,7},{1,24},{2,5},{3,26},{4,3},{5,28},{6,1},{7,30},{8,15},{9,16},... | collective-permute-start | bytes 442376 | tf_op jit(solution)/shard_map/ppermute | solution.py:361
  16.5 0.4 collective-permute-start.2
  16.9 3.1 %send_part.1.work_ref = bf16[2304,1152]{1,0:T(8,128)(2,1)S(1)} custom-call(s32[8]{0:T(128)S(1)} %copy-done.1, f32[16,2304]{1,0:T(8,128)S(1)} %add.21.after_ref, bf16[2304,2304]{1,0:T(8,128)(2,1)S(1)} %get-tuple-element.28.err_ref), custom_call_target="tpu_custom_call" | custom-call | flops 1000000000 | bytes 4000000 | tf_op jit(solution)/shard_map/send_part/pallas_call | solution.py:166
  20.1 1.0 %collective-permute-done.2.a_ref = f32[16,2304]{1,0:T(8,128)S(1)} collective-permute-done((f32[16,2304]{1,0:T(8,128)S(1)}, f32[16,2304]{1,0:T(8,128)S(1)}, u32[]{:S(2)}, u32[]{:S(2)}) %collective-permute-start.2) | collective-permute-done | bytes 147488 | tf_op jit(solution)/shard_map/ppermute | solution.py:361
  21.1 0.3 collective-permute-start.13
  21.4 3.9 %collective-permute-start.8 = (f32[16,2304]{1,0:T(8,128)S(1)}, f32[16,2304]{1,0:T(8,128)S(1)}, u32[]{:S(2)}, u32[]{:S(2)}) collective-permute-start(f32[16,2304]{1,0:T(8,128)S(1)} %get-tuple-element.29.after_ref.d_ref), channel_id=1, source_target_pairs={{0,64},{1,17},{2,66},{3,19},{4,68},{5,21},{6,70},{7,23},{8,72},{9,... | collective-permute-start | bytes 442376 | tf_op jit(solution)/shard_map/ppermute | solution.py:361
  25.3 0.7 collective-permute-start.7
  26.0 0.3 collective-permute-start.6
  26.3 3.7 %corrected_own.1.work_ref = bf16[2304,1152]{1,0:T(8,128)(2,1)S(1)} custom-call(f32[16,2304]{1,0:T(8,128)S(1)} %get-tuple-element.29.after_ref.d_ref, bf16[512,2304]{1,0:T(8,128)(2,1)S(1)} %get-tuple-element.24.acts_ref, bf16[512,2304]{1,0:T(8,128)(2,1)S(1)} %get-tuple-element.25.grad_ref, bf16[2304,1152]{1,0:T(8,128)(2,1)S(1)} %get-tuple-element.30.err_ref), custom_call_target="tpu_custom_call" | custom-call | flops 2717908992 | bytes 8000000 | tf_op jit(solution)/shard_map/corrected_own/pallas_call | solution.py:190
  30.0 1.6 %collective-permute-done.7.b_ref = f32[16,2304]{1,0:T(8,128)S(1)} collective-permute-done((f32[16,2304]{1,0:T(8,128)S(1)}, f32[16,2304]{1,0:T(8,128)S(1)}, u32[]{:S(2)}, u32[]{:S(2)}) %collective-permute-start.7) | collective-permute-done | bytes 147488 | tf_op jit(solution)/shard_map/ppermute | solution.py:361
  31.7 0.1 collective-permute-start.12
  31.8 1.0 %collective-permute-start.11 = (f32[16,2304]{1,0:T(8,128)S(1)}, f32[16,2304]{1,0:T(8,128)S(1)}, u32[]{:S(2)}, u32[]{:S(2)}) collective-permute-start(f32[16,2304]{1,0:T(8,128)S(1)} %get-tuple-element.31.after_ref), channel_id=1, source_target_pairs={{0,5},{1,64},{2,7},{3,66},{4,1},{5,68},{6,3},{7,70},{8,13},{9,72},... | collective-permute-start | bytes 442376 | tf_op jit(solution)/shard_map/ppermute | solution.py:361
  32.8 2.2 %collective-permute-start.10 = (f32[16,2304]{1,0:T(8,128)S(1)}, f32[16,2304]{1,0:T(8,128)S(1)}, u32[]{:S(2)}, u32[]{:S(2)}) collective-permute-start(f32[16,2304]{1,0:T(8,128)S(1)} %get-tuple-element.31.after_ref), channel_id=1, source_target_pairs={{0,7},{1,96},{2,5},{3,98},{4,3},{5,100},{6,1},{7,102},{8,15},{9,10... | collective-permute-start | bytes 442376 | tf_op jit(solution)/shard_map/ppermute | solution.py:361
  35.0 0.9 %collective-permute-start.9 = (f32[16,2304]{1,0:T(8,128)S(1)}, f32[16,2304]{1,0:T(8,128)S(1)}, u32[]{:S(2)}, u32[]{:S(2)}) collective-permute-start(f32[16,2304]{1,0:T(8,128)S(1)} %get-tuple-element.31.after_ref), channel_id=1, source_target_pairs={{0,3},{1,32},{2,1},{3,34},{4,7},{5,36},{6,5},{7,38},{8,11},{9,40},... | collective-permute-start | bytes 442376 | tf_op jit(solution)/shard_map/ppermute | solution.py:361
  35.9 3.7 %corrected_other.1.work_ref = bf16[2304,1152]{1,0:T(8,128)(2,1)S(1)} custom-call(f32[16,2304]{1,0:T(8,128)S(1)} %get-tuple-element.31.after_ref, bf16[512,2304]{1,0:T(8,128)(2,1)S(1)} %get-tuple-element.24.acts_ref, bf16[512,2304]{1,0:T(8,128)(2,1)S(1)} %get-tuple-element.25.grad_ref, bf16[2304,1152]{1,0:T(8,128)(2,1)S(1)} %collective-permute-done.13.err_ref), custom_call_target="tpu_custom_call" | custom-call | flops 2717908992 | bytes 8000000 | tf_op jit(solution)/shard_map/corrected_other/pallas_call | solution.py:190
  39.7 0.4 collective-permute-start.14
  40.1 1.1 %collective-permute-done.14.took_ref = f32[16,2304]{1,0:T(8,128)S(1)} collective-permute-done((f32[16,2304]{1,0:T(8,128)S(1)}, f32[16,2304]{1,0:T(8,128)S(1)}, u32[]{:S(2)}, u32[]{:S(2)}) %collective-permute-start.14) | collective-permute-done | bytes 147488 | tf_op jit(solution)/shard_map/ppermute | solution.py:398
  41.2 2.7 %right_part.1 = (f32[32,32]{1,0:T(8,128)S(1)}, f32[32,2304]{1,0:T(8,128)S(1)}, bf16[32,2304]{1,0:T(8,128)(2,1)S(1)}) custom-call(f32[16,2304]{1,0:T(8,128)S(1)} %get-tuple-element.33.keep_ref, f32[16,2304]{1,0:T(8,128)S(1)} %collective-permute-done.14.took_ref, bf16[2304,1152]{1,0:T(8,128)(2,1)S(1)} %get-tuple-element.34.own_ref, ...), custom_call_target="tpu_custom_call" | custom-call | flops 339738624 | bytes 10616832 | tf_op jit(solution)/shard_map/right_part/pallas_call | solution.py:264
  43.9 0.4 collective-permute-start.18
  44.3 2.3 %collective-permute-start.17 = (bf16[32,2304]{1,0:T(8,128)(2,1)S(1)}, bf16[32,2304]{1,0:T(8,128)(2,1)S(1)}, u32[]{:S(2)}, u32[]{:S(2)}) collective-permute-start(bf16[32,2304]{1,0:T(8,128)(2,1)S(1)} %get-tuple-element.36), channel_id=1, source_target_pairs={{0,5},{1,16},{2,7},{3,18},{4,1},{5,20},{6,3},{7,22},{8,13},{9,24},... | collective-permute-start | bytes 442376 | tf_op jit(solution)/shard_map/ppermute | solution.py:361
  46.6 0.8 %collective-permute-start.16 = (bf16[32,2304]{1,0:T(8,128)(2,1)S(1)}, bf16[32,2304]{1,0:T(8,128)(2,1)S(1)}, u32[]{:S(2)}, u32[]{:S(2)}) collective-permute-start(bf16[32,2304]{1,0:T(8,128)(2,1)S(1)} %get-tuple-element.36), channel_id=1, source_target_pairs={{0,7},{1,24},{2,5},{3,26},{4,3},{5,28},{6,1},{7,30},{8,15},{9,16},... | collective-permute-start | bytes 442376 | tf_op jit(solution)/shard_map/ppermute | solution.py:361
  47.4 0.5 collective-permute-start.15
  48.0 2.4 %collective-permute-done.17 = bf16[32,2304]{1,0:T(8,128)(2,1)S(1)} collective-permute-done((bf16[32,2304]{1,0:T(8,128)(2,1)S(1)}, bf16[32,2304]{1,0:T(8,128)(2,1)S(1)}, u32[]{:S(2)}, u32[]{:S(2)}) %collective-permute-start.17) | collective-permute-done | bytes 147488 | tf_op jit(solution)/shard_map/ppermute | solution.py:361
  50.3 2.0 %collective-permute-done.16 = bf16[32,2304]{1,0:T(8,128)(2,1)S(1)} collective-permute-done((bf16[32,2304]{1,0:T(8,128)(2,1)S(1)}, bf16[32,2304]{1,0:T(8,128)(2,1)S(1)}, u32[]{:S(2)}, u32[]{:S(2)}) %collective-permute-start.16) | collective-permute-done | bytes 147488 | tf_op jit(solution)/shard_map/ppermute | solution.py:361
  52.4 0.1 add_convert_fusion.1
  52.5 0.3 collective-permute-start.22
  52.7 1.5 %collective-permute-start.21 = (bf16[32,2304]{1,0:T(8,128)(2,1)S(1)}, bf16[32,2304]{1,0:T(8,128)(2,1)S(1)}, u32[]{:S(2)}, u32[]{:S(2)}) collective-permute-start(bf16[32,2304]{1,0:T(8,128)(2,1)S(1)} %add_convert_fusion.1), channel_id=1, source_target_pairs={{0,65},{1,16},{2,67},{3,18},{4,69},{5,20},{6,71},{7,22},{8,73},{9,... | collective-permute-start | bytes 442376 | tf_op jit(solution)/shard_map/ppermute | solution.py:361
  54.3 1.3 %collective-permute-start.20 = (bf16[32,2304]{1,0:T(8,128)(2,1)S(1)}, bf16[32,2304]{1,0:T(8,128)(2,1)S(1)}, u32[]{:S(2)}, u32[]{:S(2)}) collective-permute-start(bf16[32,2304]{1,0:T(8,128)(2,1)S(1)} %add_convert_fusion.1), channel_id=1, source_target_pairs={{0,97},{1,24},{2,99},{3,26},{4,101},{5,28},{6,103},{7,30},{8,105},... | collective-permute-start | bytes 442376 | tf_op jit(solution)/shard_map/ppermute | solution.py:361
  55.6 0.6 collective-permute-start.19
  56.2 2.7 %collective-permute-done.21 = bf16[32,2304]{1,0:T(8,128)(2,1)S(1)} collective-permute-done((bf16[32,2304]{1,0:T(8,128)(2,1)S(1)}, bf16[32,2304]{1,0:T(8,128)(2,1)S(1)}, u32[]{:S(2)}, u32[]{:S(2)}) %collective-permute-start.21) | collective-permute-done | bytes 147488 | tf_op jit(solution)/shard_map/ppermute | solution.py:361
  58.8 1.5 %collective-permute-done.20 = bf16[32,2304]{1,0:T(8,128)(2,1)S(1)} collective-permute-done((bf16[32,2304]{1,0:T(8,128)(2,1)S(1)}, bf16[32,2304]{1,0:T(8,128)(2,1)S(1)}, u32[]{:S(2)}, u32[]{:S(2)}) %collective-permute-start.20) | collective-permute-done | bytes 147488 | tf_op jit(solution)/shard_map/ppermute | solution.py:361
  60.4 0.1 add_convert_fusion.d_ref
  60.5 1.7 %collective-permute-start.25 = (bf16[32,2304]{1,0:T(8,128)(2,1)S(1)}, bf16[32,2304]{1,0:T(8,128)(2,1)S(1)}, u32[]{:S(2)}, u32[]{:S(2)}) collective-permute-start(bf16[32,2304]{1,0:T(8,128)(2,1)S(1)} %add_convert_fusion.d_ref), channel_id=1, source_target_pairs={{0,64},{1,5},{2,66},{3,7},{4,68},{5,1},{6,70},{7,3},{8,72},{9,13},... | collective-permute-start | bytes 442376 | tf_op jit(solution)/shard_map/ppermute | solution.py:361
  62.2 1.6 %collective-permute-start.24 = (bf16[32,2304]{1,0:T(8,128)(2,1)S(1)}, bf16[32,2304]{1,0:T(8,128)(2,1)S(1)}, u32[]{:S(2)}, u32[]{:S(2)}) collective-permute-start(bf16[32,2304]{1,0:T(8,128)(2,1)S(1)} %add_convert_fusion.d_ref), channel_id=1, source_target_pairs={{0,96},{1,7},{2,98},{3,5},{4,100},{5,3},{6,102},{7,1},{8,104},{9,1... | collective-permute-start | bytes 442376 | tf_op jit(solution)/shard_map/ppermute | solution.py:361
  63.8 0.3 collective-permute-start.23
  64.0 0.4 basis_part.1
  64.4 0.7 copy.14
  65.1 2.1 %collective-permute-done.25.c_ref = bf16[32,2304]{1,0:T(8,128)(2,1)S(1)} collective-permute-done((bf16[32,2304]{1,0:T(8,128)(2,1)S(1)}, bf16[32,2304]{1,0:T(8,128)(2,1)S(1)}, u32[]{:S(2)}, u32[]{:S(2)}) %collective-permute-start.25) | collective-permute-done | bytes 147488 | tf_op jit(solution)/shard_map/ppermute | solution.py:361
  67.2 1.6 %collective-permute-done.24.b_ref = bf16[32,2304]{1,0:T(8,128)(2,1)S(1)} collective-permute-done((bf16[32,2304]{1,0:T(8,128)(2,1)S(1)}, bf16[32,2304]{1,0:T(8,128)(2,1)S(1)}, u32[]{:S(2)}, u32[]{:S(2)}) %collective-permute-start.24) | collective-permute-done | bytes 147488 | tf_op jit(solution)/shard_map/ppermute | solution.py:361
  68.8 0.1 collective-permute-done.23.a_ref
  68.9 4.6 %residue.1 = (bf16[2304,2304]{1,0:T(8,128)(2,1)}, f32[32,2304]{1,0:T(8,128)}) custom-call(bf16[32,2304]{1,0:T(8,128)(2,1)S(1)} %collective-permute-done.23.a_ref, bf16[32,2304]{1,0:T(8,128)(2,1)S(1)} %collective-permute-done.24.b_ref, bf16[32,2304]{1,0:T(8,128)(2,1)S(1)} %collective-permute-done.25.c_ref, bf16[32,2304]{1,0:T(8,128)(2,1)S(1)} %add_convert_fusion.d_ref, ...), custom_call_target="tpu_custom_call" | custom-call | flops 339738624 | bytes 10616832 | tf_op jit(solution)/shard_map/residue/pallas_call | solution.py:320
  (23 shorter events, 0.2 us)
Async XLA Ops:
  0.6 6.2 %copy-start = (bf16[32,2304]{1,0:T(8,128)(2,1)S(1)}, bf16[32,2304]{1,0:T(8,128)(2,1)}, u32[]{:S(2)}) copy-start(bf16[32,2304]{1,0:T(8,128)(2,1)} %fac_ref.1) | copy-start | bytes 442372
  0.6 6.2 %copy-start.1 = (s32[8]{0:T(128)S(1)}, s32[8]{0:T(128)}, u32[]{:S(2)}) copy-start(s32[8]{0:T(128)} %order_ref.3) | copy-start | bytes 100
  0.7 6.1 %collective-permute-start = (bf16[32,2304]{1,0:T(8,128)(2,1)}, bf16[32,2304]{1,0:T(8,128)(2,1)S(1)}, u32[]{:S(2)}, u32[]{:S(2)}) collective-permute-start(bf16[32,2304]{1,0:T(8,128)(2,1)} %fac_ref.1), channel_id=1, source_target_pairs={{0,1},{1,0},{2,3},{3,2},{4,5},{5,4},{6,7},{7,6},{8,9},{9,8},{10,11... | collective-permute-start | bytes 442376 | tf_op jit(solution)/shard_map/ppermute | solution.py:386
  8.7 1.6 %collective-permute-start.1 = (f32[16,2304]{1,0:T(8,128)S(1)}, f32[16,2304]{1,0:T(8,128)S(1)}, u32[]{:S(2)}, u32[]{:S(2)}) collective-permute-start(f32[16,2304]{1,0:T(8,128)S(1)} %get-tuple-element.27), channel_id=1, source_target_pairs={{0,1},{1,0},{2,3},{3,2},{4,5},{5,4},{6,7},{7,6},{8,9},{9,8},{10,11... | collective-permute-start | bytes 442376 | tf_op jit(solution)/shard_map/ppermute | solution.py:389
  10.3 9.7 %collective-permute-start.5 = (f32[16,2304]{1,0:T(8,128)S(1)}, f32[16,2304]{1,0:T(8,128)S(1)}, u32[]{:S(2)}, u32[]{:S(2)}) collective-permute-start(f32[16,2304]{1,0:T(8,128)S(1)} %add.21.after_ref), channel_id=1, source_target_pairs={{0,1},{1,0},{2,3},{3,2},{4,5},{5,4},{6,7},{7,6},{8,9},{9,8},{10,11... | collective-permute-start | bytes 442376 | tf_op jit(solution)/shard_map/ppermute | solution.py:362
  10.8 9.3 %collective-permute-start.4 = (f32[16,2304]{1,0:T(8,128)S(1)}, f32[16,2304]{1,0:T(8,128)S(1)}, u32[]{:S(2)}, u32[]{:S(2)}) collective-permute-start(f32[16,2304]{1,0:T(8,128)S(1)} %add.21.after_ref), channel_id=1, source_target_pairs={{0,5},{1,16},{2,7},{3,18},{4,1},{5,20},{6,3},{7,22},{8,13},{9,24},... | collective-permute-start | bytes 442376 | tf_op jit(solution)/shard_map/ppermute | solution.py:361
  13.6 6.5 %collective-permute-start.3 = (f32[16,2304]{1,0:T(8,128)S(1)}, f32[16,2304]{1,0:T(8,128)S(1)}, u32[]{:S(2)}, u32[]{:S(2)}) collective-permute-start(f32[16,2304]{1,0:T(8,128)S(1)} %add.21.after_ref), channel_id=1, source_target_pairs={{0,7},{1,24},{2,5},{3,26},{4,3},{5,28},{6,1},{7,30},{8,15},{9,16},... | collective-permute-start | bytes 442376 | tf_op jit(solution)/shard_map/ppermute | solution.py:361
  16.5 4.6 %collective-permute-start.2 = (f32[16,2304]{1,0:T(8,128)S(1)}, f32[16,2304]{1,0:T(8,128)S(1)}, u32[]{:S(2)}, u32[]{:S(2)}) collective-permute-start(f32[16,2304]{1,0:T(8,128)S(1)} %add.21.after_ref), channel_id=1, source_target_pairs={{0,3},{1,8},{2,1},{3,10},{4,7},{5,12},{6,5},{7,14},{8,11},{9,0},{1... | collective-permute-start | bytes 442376 | tf_op jit(solution)/shard_map/ppermute | solution.py:361
  21.1 14.8 %collective-permute-start.13 = (bf16[2304,1152]{1,0:T(8,128)(2,1)S(1)}, bf16[2304,1152]{1,0:T(8,128)(2,1)S(1)}, u32[]{:S(2)}, u32[]{:S(2)}) collective-permute-start(bf16[2304,1152]{1,0:T(8,128)(2,1)S(1)} %get-tuple-element.32), channel_id=1, source_target_pairs={{0,1},{1,0},{2,3},{3,2},{4,5},{5,4},{6,7},{7,6},{8,9},{9,8},{10,11... | collective-permute-start | bytes 15925256 | tf_op jit(solution)/shard_map/ppermute | solution.py:393
  21.4 8.6 %collective-permute-start.8 = (f32[16,2304]{1,0:T(8,128)S(1)}, f32[16,2304]{1,0:T(8,128)S(1)}, u32[]{:S(2)}, u32[]{:S(2)}) collective-permute-start(f32[16,2304]{1,0:T(8,128)S(1)} %get-tuple-element.29.after_ref.d_ref), channel_id=1, source_target_pairs={{0,64},{1,17},{2,66},{3,19},{4,68},{5,21},{6,70},{7,23},{8,72},{9,... | collective-permute-start | bytes 442376 | tf_op jit(solution)/shard_map/ppermute | solution.py:361
  25.3 6.4 %collective-permute-start.7 = (f32[16,2304]{1,0:T(8,128)S(1)}, f32[16,2304]{1,0:T(8,128)S(1)}, u32[]{:S(2)}, u32[]{:S(2)}) collective-permute-start(f32[16,2304]{1,0:T(8,128)S(1)} %get-tuple-element.29.after_ref.d_ref), channel_id=1, source_target_pairs={{0,96},{1,25},{2,98},{3,27},{4,100},{5,29},{6,102},{7,31},{8,104},... | collective-permute-start | bytes 442376 | tf_op jit(solution)/shard_map/ppermute | solution.py:361
  26.0 5.6 %collective-permute-start.6 = (f32[16,2304]{1,0:T(8,128)S(1)}, f32[16,2304]{1,0:T(8,128)S(1)}, u32[]{:S(2)}, u32[]{:S(2)}) collective-permute-start(f32[16,2304]{1,0:T(8,128)S(1)} %get-tuple-element.29.after_ref.d_ref), channel_id=1, source_target_pairs={{0,32},{1,9},{2,34},{3,11},{4,36},{5,13},{6,38},{7,15},{8,40},{9,1... | collective-permute-start | bytes 442376 | tf_op jit(solution)/shard_map/ppermute | solution.py:361
  31.7 7.9 %collective-permute-start.12 = (f32[16,2304]{1,0:T(8,128)S(1)}, f32[16,2304]{1,0:T(8,128)S(1)}, u32[]{:S(2)}, u32[]{:S(2)}) collective-permute-start(f32[16,2304]{1,0:T(8,128)S(1)} %get-tuple-element.31.after_ref), channel_id=1, source_target_pairs={{0,1},{1,0},{2,3},{3,2},{4,5},{5,4},{6,7},{7,6},{8,9},{9,8},{10,11... | collective-permute-start | bytes 442376 | tf_op jit(solution)/shard_map/ppermute | solution.py:362
  31.8 7.8 %collective-permute-start.11 = (f32[16,2304]{1,0:T(8,128)S(1)}, f32[16,2304]{1,0:T(8,128)S(1)}, u32[]{:S(2)}, u32[]{:S(2)}) collective-permute-start(f32[16,2304]{1,0:T(8,128)S(1)} %get-tuple-element.31.after_ref), channel_id=1, source_target_pairs={{0,5},{1,64},{2,7},{3,66},{4,1},{5,68},{6,3},{7,70},{8,13},{9,72},... | collective-permute-start | bytes 442376 | tf_op jit(solution)/shard_map/ppermute | solution.py:361
  32.8 6.9 %collective-permute-start.10 = (f32[16,2304]{1,0:T(8,128)S(1)}, f32[16,2304]{1,0:T(8,128)S(1)}, u32[]{:S(2)}, u32[]{:S(2)}) collective-permute-start(f32[16,2304]{1,0:T(8,128)S(1)} %get-tuple-element.31.after_ref), channel_id=1, source_target_pairs={{0,7},{1,96},{2,5},{3,98},{4,3},{5,100},{6,1},{7,102},{8,15},{9,10... | collective-permute-start | bytes 442376 | tf_op jit(solution)/shard_map/ppermute | solution.py:361
  35.0 4.6 %collective-permute-start.9 = (f32[16,2304]{1,0:T(8,128)S(1)}, f32[16,2304]{1,0:T(8,128)S(1)}, u32[]{:S(2)}, u32[]{:S(2)}) collective-permute-start(f32[16,2304]{1,0:T(8,128)S(1)} %get-tuple-element.31.after_ref), channel_id=1, source_target_pairs={{0,3},{1,32},{2,1},{3,34},{4,7},{5,36},{6,5},{7,38},{8,11},{9,40},... | collective-permute-start | bytes 442376 | tf_op jit(solution)/shard_map/ppermute | solution.py:361
  39.7 1.5 %collective-permute-start.14 = (f32[16,2304]{1,0:T(8,128)S(1)}, f32[16,2304]{1,0:T(8,128)S(1)}, u32[]{:S(2)}, u32[]{:S(2)}) collective-permute-start(f32[16,2304]{1,0:T(8,128)S(1)} %get-tuple-element.33.keep_ref), channel_id=1, source_target_pairs={{0,1},{1,0},{2,3},{3,2},{4,5},{5,4},{6,7},{7,6},{8,9},{9,8},{10,11... | collective-permute-start | bytes 442376 | tf_op jit(solution)/shard_map/ppermute | solution.py:398
  43.9 4.1 %collective-permute-start.18 = (bf16[32,2304]{1,0:T(8,128)(2,1)S(1)}, bf16[32,2304]{1,0:T(8,128)(2,1)S(1)}, u32[]{:S(2)}, u32[]{:S(2)}) collective-permute-start(bf16[32,2304]{1,0:T(8,128)(2,1)S(1)} %get-tuple-element.36), channel_id=1, source_target_pairs={{0,1},{1,0},{2,3},{3,2},{4,5},{5,4},{6,7},{7,6},{8,9},{9,8},{10,11... | collective-permute-start | bytes 442376 | tf_op jit(solution)/shard_map/ppermute | solution.py:362
  44.3 6.1 %collective-permute-start.17 = (bf16[32,2304]{1,0:T(8,128)(2,1)S(1)}, bf16[32,2304]{1,0:T(8,128)(2,1)S(1)}, u32[]{:S(2)}, u32[]{:S(2)}) collective-permute-start(bf16[32,2304]{1,0:T(8,128)(2,1)S(1)} %get-tuple-element.36), channel_id=1, source_target_pairs={{0,5},{1,16},{2,7},{3,18},{4,1},{5,20},{6,3},{7,22},{8,13},{9,24},... | collective-permute-start | bytes 442376 | tf_op jit(solution)/shard_map/ppermute | solution.py:361
  46.6 5.8 %collective-permute-start.16 = (bf16[32,2304]{1,0:T(8,128)(2,1)S(1)}, bf16[32,2304]{1,0:T(8,128)(2,1)S(1)}, u32[]{:S(2)}, u32[]{:S(2)}) collective-permute-start(bf16[32,2304]{1,0:T(8,128)(2,1)S(1)} %get-tuple-element.36), channel_id=1, source_target_pairs={{0,7},{1,24},{2,5},{3,26},{4,3},{5,28},{6,1},{7,30},{8,15},{9,16},... | collective-permute-start | bytes 442376 | tf_op jit(solution)/shard_map/ppermute | solution.py:361
  47.4 5.0 %collective-permute-start.15 = (bf16[32,2304]{1,0:T(8,128)(2,1)S(1)}, bf16[32,2304]{1,0:T(8,128)(2,1)S(1)}, u32[]{:S(2)}, u32[]{:S(2)}) collective-permute-start(bf16[32,2304]{1,0:T(8,128)(2,1)S(1)} %get-tuple-element.36), channel_id=1, source_target_pairs={{0,3},{1,8},{2,1},{3,10},{4,7},{5,12},{6,5},{7,14},{8,11},{9,0},{1... | collective-permute-start | bytes 442376 | tf_op jit(solution)/shard_map/ppermute | solution.py:361
  52.5 3.7 %collective-permute-start.22 = (bf16[32,2304]{1,0:T(8,128)(2,1)S(1)}, bf16[32,2304]{1,0:T(8,128)(2,1)S(1)}, u32[]{:S(2)}, u32[]{:S(2)}) collective-permute-start(bf16[32,2304]{1,0:T(8,128)(2,1)S(1)} %add_convert_fusion.1), channel_id=1, source_target_pairs={{0,1},{1,0},{2,3},{3,2},{4,5},{5,4},{6,7},{7,6},{8,9},{9,8},{10,11... | collective-permute-start | bytes 442376 | tf_op jit(solution)/shard_map/ppermute | solution.py:362
  52.7 6.1 %collective-permute-start.21 = (bf16[32,2304]{1,0:T(8,128)(2,1)S(1)}, bf16[32,2304]{1,0:T(8,128)(2,1)S(1)}, u32[]{:S(2)}, u32[]{:S(2)}) collective-permute-start(bf16[32,2304]{1,0:T(8,128)(2,1)S(1)} %add_convert_fusion.1), channel_id=1, source_target_pairs={{0,65},{1,16},{2,67},{3,18},{4,69},{5,20},{6,71},{7,22},{8,73},{9,... | collective-permute-start | bytes 442376 | tf_op jit(solution)/shard_map/ppermute | solution.py:361
  54.3 6.1 %collective-permute-start.20 = (bf16[32,2304]{1,0:T(8,128)(2,1)S(1)}, bf16[32,2304]{1,0:T(8,128)(2,1)S(1)}, u32[]{:S(2)}, u32[]{:S(2)}) collective-permute-start(bf16[32,2304]{1,0:T(8,128)(2,1)S(1)} %add_convert_fusion.1), channel_id=1, source_target_pairs={{0,97},{1,24},{2,99},{3,26},{4,101},{5,28},{6,103},{7,30},{8,105},... | collective-permute-start | bytes 442376 | tf_op jit(solution)/shard_map/ppermute | solution.py:361
  55.6 4.8 %collective-permute-start.19 = (bf16[32,2304]{1,0:T(8,128)(2,1)S(1)}, bf16[32,2304]{1,0:T(8,128)(2,1)S(1)}, u32[]{:S(2)}, u32[]{:S(2)}) collective-permute-start(bf16[32,2304]{1,0:T(8,128)(2,1)S(1)} %add_convert_fusion.1), channel_id=1, source_target_pairs={{0,33},{1,8},{2,35},{3,10},{4,37},{5,12},{6,39},{7,14},{8,41},{9,0... | collective-permute-start | bytes 442376 | tf_op jit(solution)/shard_map/ppermute | solution.py:361
  60.5 6.7 %collective-permute-start.25 = (bf16[32,2304]{1,0:T(8,128)(2,1)S(1)}, bf16[32,2304]{1,0:T(8,128)(2,1)S(1)}, u32[]{:S(2)}, u32[]{:S(2)}) collective-permute-start(bf16[32,2304]{1,0:T(8,128)(2,1)S(1)} %add_convert_fusion.d_ref), channel_id=1, source_target_pairs={{0,64},{1,5},{2,66},{3,7},{4,68},{5,1},{6,70},{7,3},{8,72},{9,13},... | collective-permute-start | bytes 442376 | tf_op jit(solution)/shard_map/ppermute | solution.py:361
  62.2 6.6 %collective-permute-start.24 = (bf16[32,2304]{1,0:T(8,128)(2,1)S(1)}, bf16[32,2304]{1,0:T(8,128)(2,1)S(1)}, u32[]{:S(2)}, u32[]{:S(2)}) collective-permute-start(bf16[32,2304]{1,0:T(8,128)(2,1)S(1)} %add_convert_fusion.d_ref), channel_id=1, source_target_pairs={{0,96},{1,7},{2,98},{3,5},{4,100},{5,3},{6,102},{7,1},{8,104},{9,1... | collective-permute-start | bytes 442376 | tf_op jit(solution)/shard_map/ppermute | solution.py:361
  63.8 5.1 %collective-permute-start.23 = (bf16[32,2304]{1,0:T(8,128)(2,1)S(1)}, bf16[32,2304]{1,0:T(8,128)(2,1)S(1)}, u32[]{:S(2)}, u32[]{:S(2)}) collective-permute-start(bf16[32,2304]{1,0:T(8,128)(2,1)S(1)} %add_convert_fusion.d_ref), channel_id=1, source_target_pairs={{0,32},{1,3},{2,34},{3,1},{4,36},{5,7},{6,38},{7,5},{8,40},{9,11},... | collective-permute-start | bytes 442376 | tf_op jit(solution)/shard_map/ppermute | solution.py:361

commit v7 on v5

--- a/solution.py
+++ b/solution.py
@@ -73,7 +73,7 @@
     return pl.ds(pl.multiple_of(i * size, size), size)
 
 
-def load_kernel(far_order, far_fac, far_err, far_acts, far_grad, left_ref, own_ref, err_ref, acts_ref, grad_ref, fac, order_ref, sems):
+def load_kernel(far_order, far_fac, far_err, far_acts, far_grad, left_ref, own_ref, err_ref, acts_ref, grad_ref, fac_own_ref, fac, order_ref, sems):
     chunks = ROWS // BIG
 
     def fetch(i):
@@ -93,6 +93,7 @@
     me = lax.axis_index("tensor")
     others[0].wait()
     others[1].wait()
+    regroup(order_ref, fac, fac_own_ref, me * QUARTER)
 
     @pl.loop(0, chunks)
     def _(i):
@@ -116,6 +117,7 @@
             pltpu.VMEM((ROWS, WIDTH), BF),
             pltpu.VMEM((TOK, ROWS), BF),
             pltpu.VMEM((TOK, WIDTH), BF),
+            pltpu.VMEM((RANK, HALF), BF),
         ],
         [
             pltpu.VMEM((RANK, WIDTH), BF),
@@ -129,7 +131,7 @@
 
 def term_kernel(order_ref, fac_ref, other_ref, left_ref, acts_ref, grad_ref, keep_ref, give_ref, fac_new, total):
     me = lax.axis_index("tensor")
-    regroup(order_ref, fac_ref, fac_new.at[:, columns(me)], me * QUARTER)
+    fac_new[:, columns(me)] = fac_ref[...]
     regroup(order_ref, other_ref, fac_new.at[:, columns(1 - me)], me * QUARTER)
     u = dot(fac_new[...], grad_ref[...], ((1,), (1,)))
     high = u.astype(BF)
@@ -151,7 +153,7 @@
         [pltpu.VMEM((RANK, WIDTH), BF), pltpu.VMEM((RANK, ROWS), F32)],
         flops=4 * RANK * ROWS * TOK,
         bytes_accessed=5 * 10**6,
-    )(order, old_factor, other_factor, in_vmem(left), in_vmem(acts), in_vmem(grad_out))
+    )(order, in_vmem(old_factor), other_factor, in_vmem(left), in_vmem(acts), in_vmem(grad_out))
 
 
 def send_kernel(order_ref, after_ref, err_ref, send_ref):
@@ -384,8 +386,8 @@
 
 def body(acts, grad_out, old_error, old_factor, piece_order):
     other_factor = lax.ppermute(old_factor, "tensor", SWAP)
-    left, own_err, err, acts, grad_out = load_part(piece_order, old_factor, old_error, acts, grad_out)
-    keep, give = term_part(piece_order, old_factor, other_factor, left, acts, grad_out)
+    left, own_err, err, acts, grad_out, own_factor = load_part(piece_order, old_factor, old_error, acts, grad_out)
+    keep, give = term_part(piece_order, own_factor, other_factor, left, acts, grad_out)
     part = keep + lax.ppermute(give, "tensor", SWAP)
     first, second, third = stages((1, 0, 1))
     terms = spread(part, first)

time: 73.2 us -> 73.1 us (level)
  no operation moved by 1% of the time
where the time goes in v7:
time: 73.1 us; the launch traced here: 73 us
  starting transfers between devices  28.9 us (40%)
  Pallas kernels  26.2 us (36%)
  waiting for transfers between devices  15.9 us (22%)
  between operations  0.98 us (1%)
    ppermute x18, starting transfers between devices, spread(): lax.ppermute(x, AXES, ring_pairs(axes, flip, cross))  25.5 us
    ppermute x18, waiting for transfers between devices, spread(): lax.ppermute(x, AXES, ring_pairs(axes, flip, cross))  13.8 us
    pallas_call x2, Pallas kernels, corrected_half(): call(functools.partial(half_kernel, other), 'corrected_other' if other el...  7.4 us
    pallas_call x1, Pallas kernels, load_part(): call(load_kernel, 'load_part', [FAR] * 5, [pltpu.VMEM((RANK, ROWS), F32),...  6.05 us
    pallas_call x1, Pallas kernels, residue(): call(functools.partial(residue_kernel, scale), 'residue', [WHOLE] * 7, [p...  4.59 us
    pallas_call x1, Pallas kernels, send_part(): call(send_kernel, 'send_part', [SCALARS, pl.BlockSpec(memory_space=pl.ANY...  3.12 us
    pallas_call x1, Pallas kernels, right_part(): call(right_kernel, 'right_part', [WHOLE] * 4, [pltpu.VMEM((RANK, RANK), F...  2.74 us
    pallas_call x1, Pallas kernels, term_part(): call(term_kernel, 'term_part', [SCALARS] + [WHOLE] * 5, [half, half], [pl...  1.88 us
  transfers between devices with their start and end apart: 26, of which 12 were waited for; matrix products, arithmetic and copies ran while one was open for 1% of the time, Pallas kernels for 23%

profile of v7, /device:TPU:0, one launch (start us, length us, event | category | flops | bytes accessed | tf_op | source)
XLA Modules:
  0.0 73.0 jit_solution(2665444791560292860)
XLA Ops:
  0.6 0.1 collective-permute-start
  0.7 6.0 %load_part.1 = (f32[32,2304]{1,0:T(8,128)S(1)}, bf16[2304,1152]{1,0:T(8,128)(2,1)S(1)}, bf16[2304,2304]{1,0:T(8,128)(2,1)S(1)}, bf16[512,2304]{1,0:T(8,128)(2,1)...) custom-call(s32[8]{0:T(128)} %order_ref.3, bf16[32,2304]{1,0:T(8,128)(2,1)} %far_fac.1, ...), custom_call_target="tpu_custom_call" | custom-call | flops 339738624 | bytes 10616832 | tf_op jit(solution)/shard_map/load_part/pallas_call | solution.py:110
  6.8 0.0 collective-permute-done.other_ref
  6.8 1.9 %term_part.1 = (f32[16,2304]{1,0:T(8,128)S(1)}, f32[16,2304]{1,0:T(8,128)S(1)}) custom-call(s32[8]{0:T(128)S(1)} %copy-done, bf16[32,1152]{1,0:T(8,128)(2,1)S(1)} %get-tuple-element.24.fac_ref, bf16[32,2304]{1,0:T(8,128)(2,1)S(1)} %collective-permute-done.other_ref, f32[32,2304]{1,0:T(8,128)S(1)} %get-tuple-element.25.left_ref, ...), custom_call_target="tpu_custom_call" | custom-call | flops 150994944 | bytes 5000000 | tf_op jit(solution)/shard_map/term_part/pallas_call | solution.py:148
  8.7 0.6 collective-permute-start.1
  9.3 1.0 %collective-permute-done.1 = f32[16,2304]{1,0:T(8,128)S(1)} collective-permute-done((f32[16,2304]{1,0:T(8,128)S(1)}, f32[16,2304]{1,0:T(8,128)S(1)}, u32[]{:S(2)}, u32[]{:S(2)}) %collective-permute-start.1) | collective-permute-done | bytes 147488 | tf_op jit(solution)/shard_map/ppermute | solution.py:391
  10.3 3.1 %collective-permute-start.5 = (f32[16,2304]{1,0:T(8,128)S(1)}, f32[16,2304]{1,0:T(8,128)S(1)}, u32[]{:S(2)}, u32[]{:S(2)}) collective-permute-start(f32[16,2304]{1,0:T(8,128)S(1)} %add.21.after_ref), channel_id=1, source_target_pairs={{0,5},{1,16},{2,7},{3,18},{4,1},{5,20},{6,3},{7,22},{8,13},{9,24},... | collective-permute-start | bytes 442376 | tf_op jit(solution)/shard_map/ppermute | solution.py:363
  13.5 2.7 %collective-permute-start.4 = (f32[16,2304]{1,0:T(8,128)S(1)}, f32[16,2304]{1,0:T(8,128)S(1)}, u32[]{:S(2)}, u32[]{:S(2)}) collective-permute-start(f32[16,2304]{1,0:T(8,128)S(1)} %add.21.after_ref), channel_id=1, source_target_pairs={{0,7},{1,24},{2,5},{3,26},{4,3},{5,28},{6,1},{7,30},{8,15},{9,16},... | collective-permute-start | bytes 442376 | tf_op jit(solution)/shard_map/ppermute | solution.py:363
  16.1 0.6 collective-permute-start.3
  16.8 0.1 collective-permute-start.2
  16.9 3.1 %send_part.1.work_ref = bf16[2304,1152]{1,0:T(8,128)(2,1)S(1)} custom-call(s32[8]{0:T(128)S(1)} %copy-done, f32[16,2304]{1,0:T(8,128)S(1)} %add.21.after_ref, bf16[2304,2304]{1,0:T(8,128)(2,1)S(1)} %get-tuple-element.30.err_ref), custom_call_target="tpu_custom_call" | custom-call | flops 1000000000 | bytes 4000000 | tf_op jit(solution)/shard_map/send_part/pallas_call | solution.py:168
  20.1 0.6 collective-permute-done.3.b_ref
  20.8 0.5 collective-permute-start.13
  21.3 3.9 %collective-permute-start.8 = (f32[16,2304]{1,0:T(8,128)S(1)}, f32[16,2304]{1,0:T(8,128)S(1)}, u32[]{:S(2)}, u32[]{:S(2)}) collective-permute-start(f32[16,2304]{1,0:T(8,128)S(1)} %get-tuple-element.31.after_ref.a_ref), channel_id=1, source_target_pairs={{0,64},{1,17},{2,66},{3,19},{4,68},{5,21},{6,70},{7,23},{8,72},{9,... | collective-permute-start | bytes 442376 | tf_op jit(solution)/shard_map/ppermute | solution.py:363
  25.2 0.7 collective-permute-start.7
  25.9 0.3 collective-permute-start.6
  26.2 3.7 %corrected_own.1.work_ref = bf16[2304,1152]{1,0:T(8,128)(2,1)S(1)} custom-call(f32[16,2304]{1,0:T(8,128)S(1)} %get-tuple-element.31.after_ref.a_ref, bf16[512,2304]{1,0:T(8,128)(2,1)S(1)} %get-tuple-element.26.acts_ref, bf16[512,2304]{1,0:T(8,128)(2,1)S(1)} %get-tuple-element.27.grad_ref, bf16[2304,1152]{1,0:T(8,128)(2,1)S(1)} %get-tuple-element.32.err_ref), custom_call_target="tpu_custom_call" | custom-call | flops 2717908992 | bytes 8000000 | tf_op jit(solution)/shard_map/corrected_own/pallas_call | solution.py:192
  29.9 1.6 %collective-permute-done.7.c_ref = f32[16,2304]{1,0:T(8,128)S(1)} collective-permute-done((f32[16,2304]{1,0:T(8,128)S(1)}, f32[16,2304]{1,0:T(8,128)S(1)}, u32[]{:S(2)}, u32[]{:S(2)}) %collective-permute-start.7) | collective-permute-done | bytes 147488 | tf_op jit(solution)/shard_map/ppermute | solution.py:363
  31.6 0.1 collective-permute-start.12
  31.6 2.9 %collective-permute-start.11 = (f32[16,2304]{1,0:T(8,128)S(1)}, f32[16,2304]{1,0:T(8,128)S(1)}, u32[]{:S(2)}, u32[]{:S(2)}) collective-permute-start(f32[16,2304]{1,0:T(8,128)S(1)} %get-tuple-element.33.after_ref), channel_id=1, source_target_pairs={{0,7},{1,96},{2,5},{3,98},{4,3},{5,100},{6,1},{7,102},{8,15},{9,10... | collective-permute-start | bytes 442376 | tf_op jit(solution)/shard_map/ppermute | solution.py:363
  34.6 1.0 %collective-permute-start.9 = (f32[16,2304]{1,0:T(8,128)S(1)}, f32[16,2304]{1,0:T(8,128)S(1)}, u32[]{:S(2)}, u32[]{:S(2)}) collective-permute-start(f32[16,2304]{1,0:T(8,128)S(1)} %get-tuple-element.33.after_ref), channel_id=1, source_target_pairs={{0,1},{1,0},{2,3},{3,2},{4,5},{5,4},{6,7},{7,6},{8,9},{9,8},{10,11... | collective-permute-start | bytes 442376 | tf_op jit(solution)/shard_map/ppermute | solution.py:364
  35.5 3.7 %corrected_other.1.work_ref = bf16[2304,1152]{1,0:T(8,128)(2,1)S(1)} custom-call(f32[16,2304]{1,0:T(8,128)S(1)} %get-tuple-element.33.after_ref, bf16[512,2304]{1,0:T(8,128)(2,1)S(1)} %get-tuple-element.26.acts_ref, bf16[512,2304]{1,0:T(8,128)(2,1)S(1)} %get-tuple-element.27.grad_ref, bf16[2304,1152]{1,0:T(8,128)(2,1)S(1)} %collective-permute-done.13.err_ref), custom_call_target="tpu_custom_call" | custom-call | flops 2717908992 | bytes 8000000 | tf_op jit(solution)/shard_map/corrected_other/pallas_call | solution.py:192
  39.3 0.4 collective-permute-start.14
  39.7 1.1 %collective-permute-done.14.took_ref = f32[16,2304]{1,0:T(8,128)S(1)} collective-permute-done((f32[16,2304]{1,0:T(8,128)S(1)}, f32[16,2304]{1,0:T(8,128)S(1)}, u32[]{:S(2)}, u32[]{:S(2)}) %collective-permute-start.14) | collective-permute-done | bytes 147488 | tf_op jit(solution)/shard_map/ppermute | solution.py:400
  40.8 2.7 %right_part.1 = (f32[32,32]{1,0:T(8,128)S(1)}, f32[32,2304]{1,0:T(8,128)S(1)}, bf16[32,2304]{1,0:T(8,128)(2,1)S(1)}) custom-call(f32[16,2304]{1,0:T(8,128)S(1)} %get-tuple-element.35.keep_ref, f32[16,2304]{1,0:T(8,128)S(1)} %collective-permute-done.14.took_ref, bf16[2304,1152]{1,0:T(8,128)(2,1)S(1)} %get-tuple-element.36.own_ref, ...), custom_call_target="tpu_custom_call" | custom-call | flops 339738624 | bytes 10616832 | tf_op jit(solution)/shard_map/right_part/pallas_call | solution.py:266
  43.5 1.7 %collective-permute-start.18 = (bf16[32,2304]{1,0:T(8,128)(2,1)S(1)}, bf16[32,2304]{1,0:T(8,128)(2,1)S(1)}, u32[]{:S(2)}, u32[]{:S(2)}) collective-permute-start(bf16[32,2304]{1,0:T(8,128)(2,1)S(1)} %get-tuple-element.38), channel_id=1, source_target_pairs={{0,5},{1,16},{2,7},{3,18},{4,1},{5,20},{6,3},{7,22},{8,13},{9,24},... | collective-permute-start | bytes 442376 | tf_op jit(solution)/shard_map/ppermute | solution.py:363
  45.2 1.3 %collective-permute-start.17 = (bf16[32,2304]{1,0:T(8,128)(2,1)S(1)}, bf16[32,2304]{1,0:T(8,128)(2,1)S(1)}, u32[]{:S(2)}, u32[]{:S(2)}) collective-permute-start(bf16[32,2304]{1,0:T(8,128)(2,1)S(1)} %get-tuple-element.38), channel_id=1, source_target_pairs={{0,7},{1,24},{2,5},{3,26},{4,3},{5,28},{6,1},{7,30},{8,15},{9,16},... | collective-permute-start | bytes 442376 | tf_op jit(solution)/shard_map/ppermute | solution.py:363
  46.5 0.7 collective-permute-start.16
  47.2 0.4 collective-permute-start.15
  47.6 2.1 %collective-permute-done.18 = bf16[32,2304]{1,0:T(8,128)(2,1)S(1)} collective-permute-done((bf16[32,2304]{1,0:T(8,128)(2,1)S(1)}, bf16[32,2304]{1,0:T(8,128)(2,1)S(1)}, u32[]{:S(2)}, u32[]{:S(2)}) %collective-permute-start.18) | collective-permute-done | bytes 147488 | tf_op jit(solution)/shard_map/ppermute | solution.py:363
  49.7 1.6 %collective-permute-done.17 = bf16[32,2304]{1,0:T(8,128)(2,1)S(1)} collective-permute-done((bf16[32,2304]{1,0:T(8,128)(2,1)S(1)}, bf16[32,2304]{1,0:T(8,128)(2,1)S(1)}, u32[]{:S(2)}, u32[]{:S(2)}) %collective-permute-start.17) | collective-permute-done | bytes 147488 | tf_op jit(solution)/shard_map/ppermute | solution.py:363
  51.3 0.1 add_convert_fusion.1
  51.3 1.7 %collective-permute-start.22 = (bf16[32,2304]{1,0:T(8,128)(2,1)S(1)}, bf16[32,2304]{1,0:T(8,128)(2,1)S(1)}, u32[]{:S(2)}, u32[]{:S(2)}) collective-permute-start(bf16[32,2304]{1,0:T(8,128)(2,1)S(1)} %add_convert_fusion.1), channel_id=1, source_target_pairs={{0,65},{1,16},{2,67},{3,18},{4,69},{5,20},{6,71},{7,22},{8,73},{9,... | collective-permute-start | bytes 442376 | tf_op jit(solution)/shard_map/ppermute | solution.py:363
  53.0 1.6 %collective-permute-start.21 = (bf16[32,2304]{1,0:T(8,128)(2,1)S(1)}, bf16[32,2304]{1,0:T(8,128)(2,1)S(1)}, u32[]{:S(2)}, u32[]{:S(2)}) collective-permute-start(bf16[32,2304]{1,0:T(8,128)(2,1)S(1)} %add_convert_fusion.1), channel_id=1, source_target_pairs={{0,97},{1,24},{2,99},{3,26},{4,101},{5,28},{6,103},{7,30},{8,105},... | collective-permute-start | bytes 442376 | tf_op jit(solution)/shard_map/ppermute | solution.py:363
  54.6 0.4 collective-permute-start.20
  55.0 0.4 collective-permute-start.19
  55.3 2.2 %collective-permute-done.22 = bf16[32,2304]{1,0:T(8,128)(2,1)S(1)} collective-permute-done((bf16[32,2304]{1,0:T(8,128)(2,1)S(1)}, bf16[32,2304]{1,0:T(8,128)(2,1)S(1)}, u32[]{:S(2)}, u32[]{:S(2)}) %collective-permute-start.22) | collective-permute-done | bytes 147488 | tf_op jit(solution)/shard_map/ppermute | solution.py:363
  57.5 1.6 %collective-permute-done.21 = bf16[32,2304]{1,0:T(8,128)(2,1)S(1)} collective-permute-done((bf16[32,2304]{1,0:T(8,128)(2,1)S(1)}, bf16[32,2304]{1,0:T(8,128)(2,1)S(1)}, u32[]{:S(2)}, u32[]{:S(2)}) %collective-permute-start.21) | collective-permute-done | bytes 147488 | tf_op jit(solution)/shard_map/ppermute | solution.py:363
  59.1 0.1 collective-permute-done.20
  59.1 0.1 add_convert_fusion.a_ref
  59.2 2.1 %collective-permute-start.25 = (bf16[32,2304]{1,0:T(8,128)(2,1)S(1)}, bf16[32,2304]{1,0:T(8,128)(2,1)S(1)}, u32[]{:S(2)}, u32[]{:S(2)}) collective-permute-start(bf16[32,2304]{1,0:T(8,128)(2,1)S(1)} %add_convert_fusion.a_ref), channel_id=1, source_target_pairs={{0,64},{1,5},{2,66},{3,7},{4,68},{5,1},{6,70},{7,3},{8,72},{9,13},... | collective-permute-start | bytes 442376 | tf_op jit(solution)/shard_map/ppermute | solution.py:363
  61.4 1.7 %collective-permute-start.24 = (bf16[32,2304]{1,0:T(8,128)(2,1)S(1)}, bf16[32,2304]{1,0:T(8,128)(2,1)S(1)}, u32[]{:S(2)}, u32[]{:S(2)}) collective-permute-start(bf16[32,2304]{1,0:T(8,128)(2,1)S(1)} %add_convert_fusion.a_ref), channel_id=1, source_target_pairs={{0,96},{1,7},{2,98},{3,5},{4,100},{5,3},{6,102},{7,1},{8,104},{9,1... | collective-permute-start | bytes 442376 | tf_op jit(solution)/shard_map/ppermute | solution.py:363
  63.1 0.4 basis_part.1
  63.5 0.7 copy.14
  64.2 1.8 %collective-permute-done.25.d_ref = bf16[32,2304]{1,0:T(8,128)(2,1)S(1)} collective-permute-done((bf16[32,2304]{1,0:T(8,128)(2,1)S(1)}, bf16[32,2304]{1,0:T(8,128)(2,1)S(1)}, u32[]{:S(2)}, u32[]{:S(2)}) %collective-permute-start.25) | collective-permute-done | bytes 147488 | tf_op jit(solution)/shard_map/ppermute | solution.py:363
  65.9 1.8 %collective-permute-done.24.c_ref = bf16[32,2304]{1,0:T(8,128)(2,1)S(1)} collective-permute-done((bf16[32,2304]{1,0:T(8,128)(2,1)S(1)}, bf16[32,2304]{1,0:T(8,128)(2,1)S(1)}, u32[]{:S(2)}, u32[]{:S(2)}) %collective-permute-start.24) | collective-permute-done | bytes 147488 | tf_op jit(solution)/shard_map/ppermute | solution.py:363
  67.7 0.5 collective-permute-done.23.b_ref
  68.2 4.6 %residue.1 = (bf16[2304,2304]{1,0:T(8,128)(2,1)}, f32[32,2304]{1,0:T(8,128)}) custom-call(bf16[32,2304]{1,0:T(8,128)(2,1)S(1)} %add_convert_fusion.a_ref, bf16[32,2304]{1,0:T(8,128)(2,1)S(1)} %collective-permute-done.23.b_ref, bf16[32,2304]{1,0:T(8,128)(2,1)S(1)} %collective-permute-done.24.c_ref, bf16[32,2304]{1,0:T(8,128)(2,1)S(1)} %collective-permute-done.25.d_ref, ...), custom_call_target="tpu_custom_call" | custom-call | flops 339738624 | bytes 10616832 | tf_op jit(solution)/shard_map/residue/pallas_call | solution.py:322
  (21 shorter events, 0.2 us)
Async XLA Ops:
  0.6 6.2 %copy-start = (s32[8]{0:T(128)S(1)}, s32[8]{0:T(128)}, u32[]{:S(2)}) copy-start(s32[8]{0:T(128)} %order_ref.3) | copy-start | bytes 100
  0.6 6.2 %collective-permute-start = (bf16[32,2304]{1,0:T(8,128)(2,1)}, bf16[32,2304]{1,0:T(8,128)(2,1)S(1)}, u32[]{:S(2)}, u32[]{:S(2)}) collective-permute-start(bf16[32,2304]{1,0:T(8,128)(2,1)} %far_fac.1), channel_id=1, source_target_pairs={{0,1},{1,0},{2,3},{3,2},{4,5},{5,4},{6,7},{7,6},{8,9},{9,8},{10,11... | collective-permute-start | bytes 442376 | tf_op jit(solution)/shard_map/ppermute | solution.py:388
  8.7 1.6 %collective-permute-start.1 = (f32[16,2304]{1,0:T(8,128)S(1)}, f32[16,2304]{1,0:T(8,128)S(1)}, u32[]{:S(2)}, u32[]{:S(2)}) collective-permute-start(f32[16,2304]{1,0:T(8,128)S(1)} %get-tuple-element.29), channel_id=1, source_target_pairs={{0,1},{1,0},{2,3},{3,2},{4,5},{5,4},{6,7},{7,6},{8,9},{9,8},{10,11... | collective-permute-start | bytes 442376 | tf_op jit(solution)/shard_map/ppermute | solution.py:391
  10.3 9.7 %collective-permute-start.5 = (f32[16,2304]{1,0:T(8,128)S(1)}, f32[16,2304]{1,0:T(8,128)S(1)}, u32[]{:S(2)}, u32[]{:S(2)}) collective-permute-start(f32[16,2304]{1,0:T(8,128)S(1)} %add.21.after_ref), channel_id=1, source_target_pairs={{0,5},{1,16},{2,7},{3,18},{4,1},{5,20},{6,3},{7,22},{8,13},{9,24},... | collective-permute-start | bytes 442376 | tf_op jit(solution)/shard_map/ppermute | solution.py:363
  13.5 6.6 %collective-permute-start.4 = (f32[16,2304]{1,0:T(8,128)S(1)}, f32[16,2304]{1,0:T(8,128)S(1)}, u32[]{:S(2)}, u32[]{:S(2)}) collective-permute-start(f32[16,2304]{1,0:T(8,128)S(1)} %add.21.after_ref), channel_id=1, source_target_pairs={{0,7},{1,24},{2,5},{3,26},{4,3},{5,28},{6,1},{7,30},{8,15},{9,16},... | collective-permute-start | bytes 442376 | tf_op jit(solution)/shard_map/ppermute | solution.py:363
  16.1 4.6 %collective-permute-start.3 = (f32[16,2304]{1,0:T(8,128)S(1)}, f32[16,2304]{1,0:T(8,128)S(1)}, u32[]{:S(2)}, u32[]{:S(2)}) collective-permute-start(f32[16,2304]{1,0:T(8,128)S(1)} %add.21.after_ref), channel_id=1, source_target_pairs={{0,3},{1,8},{2,1},{3,10},{4,7},{5,12},{6,5},{7,14},{8,11},{9,0},{1... | collective-permute-start | bytes 442376 | tf_op jit(solution)/shard_map/ppermute | solution.py:363
  16.8 3.9 %collective-permute-start.2 = (f32[16,2304]{1,0:T(8,128)S(1)}, f32[16,2304]{1,0:T(8,128)S(1)}, u32[]{:S(2)}, u32[]{:S(2)}) collective-permute-start(f32[16,2304]{1,0:T(8,128)S(1)} %add.21.after_ref), channel_id=1, source_target_pairs={{0,1},{1,0},{2,3},{3,2},{4,5},{5,4},{6,7},{7,6},{8,9},{9,8},{10,11... | collective-permute-start | bytes 442376 | tf_op jit(solution)/shard_map/ppermute | solution.py:364
  20.8 14.8 %collective-permute-start.13 = (bf16[2304,1152]{1,0:T(8,128)(2,1)S(1)}, bf16[2304,1152]{1,0:T(8,128)(2,1)S(1)}, u32[]{:S(2)}, u32[]{:S(2)}) collective-permute-start(bf16[2304,1152]{1,0:T(8,128)(2,1)S(1)} %get-tuple-element.34), channel_id=1, source_target_pairs={{0,1},{1,0},{2,3},{3,2},{4,5},{5,4},{6,7},{7,6},{8,9},{9,8},{10,11... | collective-permute-start | bytes 15925256 | tf_op jit(solution)/shard_map/ppermute | solution.py:395
  21.3 8.6 %collective-permute-start.8 = (f32[16,2304]{1,0:T(8,128)S(1)}, f32[16,2304]{1,0:T(8,128)S(1)}, u32[]{:S(2)}, u32[]{:S(2)}) collective-permute-start(f32[16,2304]{1,0:T(8,128)S(1)} %get-tuple-element.31.after_ref.a_ref), channel_id=1, source_target_pairs={{0,64},{1,17},{2,66},{3,19},{4,68},{5,21},{6,70},{7,23},{8,72},{9,... | collective-permute-start | bytes 442376 | tf_op jit(solution)/shard_map/ppermute | solution.py:363
  25.2 6.4 %collective-permute-start.7 = (f32[16,2304]{1,0:T(8,128)S(1)}, f32[16,2304]{1,0:T(8,128)S(1)}, u32[]{:S(2)}, u32[]{:S(2)}) collective-permute-start(f32[16,2304]{1,0:T(8,128)S(1)} %get-tuple-element.31.after_ref.a_ref), channel_id=1, source_target_pairs={{0,96},{1,25},{2,98},{3,27},{4,100},{5,29},{6,102},{7,31},{8,104},... | collective-permute-start | bytes 442376 | tf_op jit(solution)/shard_map/ppermute | solution.py:363
  25.9 5.6 %collective-permute-start.6 = (f32[16,2304]{1,0:T(8,128)S(1)}, f32[16,2304]{1,0:T(8,128)S(1)}, u32[]{:S(2)}, u32[]{:S(2)}) collective-permute-start(f32[16,2304]{1,0:T(8,128)S(1)} %get-tuple-element.31.after_ref.a_ref), channel_id=1, source_target_pairs={{0,32},{1,9},{2,34},{3,11},{4,36},{5,13},{6,38},{7,15},{8,40},{9,1... | collective-permute-start | bytes 442376 | tf_op jit(solution)/shard_map/ppermute | solution.py:363
  31.6 7.7 %collective-permute-start.12 = (f32[16,2304]{1,0:T(8,128)S(1)}, f32[16,2304]{1,0:T(8,128)S(1)}, u32[]{:S(2)}, u32[]{:S(2)}) collective-permute-start(f32[16,2304]{1,0:T(8,128)S(1)} %get-tuple-element.33.after_ref), channel_id=1, source_target_pairs={{0,5},{1,64},{2,7},{3,66},{4,1},{5,68},{6,3},{7,70},{8,13},{9,72},... | collective-permute-start | bytes 442376 | tf_op jit(solution)/shard_map/ppermute | solution.py:363
  31.6 7.6 %collective-permute-start.11 = (f32[16,2304]{1,0:T(8,128)S(1)}, f32[16,2304]{1,0:T(8,128)S(1)}, u32[]{:S(2)}, u32[]{:S(2)}) collective-permute-start(f32[16,2304]{1,0:T(8,128)S(1)} %get-tuple-element.33.after_ref), channel_id=1, source_target_pairs={{0,7},{1,96},{2,5},{3,98},{4,3},{5,100},{6,1},{7,102},{8,15},{9,10... | collective-permute-start | bytes 442376 | tf_op jit(solution)/shard_map/ppermute | solution.py:363
  34.6 4.7 %collective-permute-start.10 = (f32[16,2304]{1,0:T(8,128)S(1)}, f32[16,2304]{1,0:T(8,128)S(1)}, u32[]{:S(2)}, u32[]{:S(2)}) collective-permute-start(f32[16,2304]{1,0:T(8,128)S(1)} %get-tuple-element.33.after_ref), channel_id=1, source_target_pairs={{0,3},{1,32},{2,1},{3,34},{4,7},{5,36},{6,5},{7,38},{8,11},{9,40},... | collective-permute-start | bytes 442376 | tf_op jit(solution)/shard_map/ppermute | solution.py:363
  34.6 4.7 %collective-permute-start.9 = (f32[16,2304]{1,0:T(8,128)S(1)}, f32[16,2304]{1,0:T(8,128)S(1)}, u32[]{:S(2)}, u32[]{:S(2)}) collective-permute-start(f32[16,2304]{1,0:T(8,128)S(1)} %get-tuple-element.33.after_ref), channel_id=1, source_target_pairs={{0,1},{1,0},{2,3},{3,2},{4,5},{5,4},{6,7},{7,6},{8,9},{9,8},{10,11... | collective-permute-start | bytes 442376 | tf_op jit(solution)/shard_map/ppermute | solution.py:364
  39.3 1.5 %collective-permute-start.14 = (f32[16,2304]{1,0:T(8,128)S(1)}, f32[16,2304]{1,0:T(8,128)S(1)}, u32[]{:S(2)}, u32[]{:S(2)}) collective-permute-start(f32[16,2304]{1,0:T(8,128)S(1)} %get-tuple-element.35.keep_ref), channel_id=1, source_target_pairs={{0,1},{1,0},{2,3},{3,2},{4,5},{5,4},{6,7},{7,6},{8,9},{9,8},{10,11... | collective-permute-start | bytes 442376 | tf_op jit(solution)/shard_map/ppermute | solution.py:400
  43.5 6.2 %collective-permute-start.18 = (bf16[32,2304]{1,0:T(8,128)(2,1)S(1)}, bf16[32,2304]{1,0:T(8,128)(2,1)S(1)}, u32[]{:S(2)}, u32[]{:S(2)}) collective-permute-start(bf16[32,2304]{1,0:T(8,128)(2,1)S(1)} %get-tuple-element.38), channel_id=1, source_target_pairs={{0,5},{1,16},{2,7},{3,18},{4,1},{5,20},{6,3},{7,22},{8,13},{9,24},... | collective-permute-start | bytes 442376 | tf_op jit(solution)/shard_map/ppermute | solution.py:363
  45.2 6.0 %collective-permute-start.17 = (bf16[32,2304]{1,0:T(8,128)(2,1)S(1)}, bf16[32,2304]{1,0:T(8,128)(2,1)S(1)}, u32[]{:S(2)}, u32[]{:S(2)}) collective-permute-start(bf16[32,2304]{1,0:T(8,128)(2,1)S(1)} %get-tuple-element.38), channel_id=1, source_target_pairs={{0,7},{1,24},{2,5},{3,26},{4,3},{5,28},{6,1},{7,30},{8,15},{9,16},... | collective-permute-start | bytes 442376 | tf_op jit(solution)/shard_map/ppermute | solution.py:363
  46.5 4.7 %collective-permute-start.16 = (bf16[32,2304]{1,0:T(8,128)(2,1)S(1)}, bf16[32,2304]{1,0:T(8,128)(2,1)S(1)}, u32[]{:S(2)}, u32[]{:S(2)}) collective-permute-start(bf16[32,2304]{1,0:T(8,128)(2,1)S(1)} %get-tuple-element.38), channel_id=1, source_target_pairs={{0,3},{1,8},{2,1},{3,10},{4,7},{5,12},{6,5},{7,14},{8,11},{9,0},{1... | collective-permute-start | bytes 442376 | tf_op jit(solution)/shard_map/ppermute | solution.py:363
  47.2 4.1 %collective-permute-start.15 = (bf16[32,2304]{1,0:T(8,128)(2,1)S(1)}, bf16[32,2304]{1,0:T(8,128)(2,1)S(1)}, u32[]{:S(2)}, u32[]{:S(2)}) collective-permute-start(bf16[32,2304]{1,0:T(8,128)(2,1)S(1)} %get-tuple-element.38), channel_id=1, source_target_pairs={{0,1},{1,0},{2,3},{3,2},{4,5},{5,4},{6,7},{7,6},{8,9},{9,8},{10,11... | collective-permute-start | bytes 442376 | tf_op jit(solution)/shard_map/ppermute | solution.py:364
  51.3 6.2 %collective-permute-start.22 = (bf16[32,2304]{1,0:T(8,128)(2,1)S(1)}, bf16[32,2304]{1,0:T(8,128)(2,1)S(1)}, u32[]{:S(2)}, u32[]{:S(2)}) collective-permute-start(bf16[32,2304]{1,0:T(8,128)(2,1)S(1)} %add_convert_fusion.1), channel_id=1, source_target_pairs={{0,65},{1,16},{2,67},{3,18},{4,69},{5,20},{6,71},{7,22},{8,73},{9,... | collective-permute-start | bytes 442376 | tf_op jit(solution)/shard_map/ppermute | solution.py:363
  53.0 6.1 %collective-permute-start.21 = (bf16[32,2304]{1,0:T(8,128)(2,1)S(1)}, bf16[32,2304]{1,0:T(8,128)(2,1)S(1)}, u32[]{:S(2)}, u32[]{:S(2)}) collective-permute-start(bf16[32,2304]{1,0:T(8,128)(2,1)S(1)} %add_convert_fusion.1), channel_id=1, source_target_pairs={{0,97},{1,24},{2,99},{3,26},{4,101},{5,28},{6,103},{7,30},{8,105},... | collective-permute-start | bytes 442376 | tf_op jit(solution)/shard_map/ppermute | solution.py:363
  54.6 4.6 %collective-permute-start.20 = (bf16[32,2304]{1,0:T(8,128)(2,1)S(1)}, bf16[32,2304]{1,0:T(8,128)(2,1)S(1)}, u32[]{:S(2)}, u32[]{:S(2)}) collective-permute-start(bf16[32,2304]{1,0:T(8,128)(2,1)S(1)} %add_convert_fusion.1), channel_id=1, source_target_pairs={{0,33},{1,8},{2,35},{3,10},{4,37},{5,12},{6,39},{7,14},{8,41},{9,0... | collective-permute-start | bytes 442376 | tf_op jit(solution)/shard_map/ppermute | solution.py:363
  55.0 4.2 %collective-permute-start.19 = (bf16[32,2304]{1,0:T(8,128)(2,1)S(1)}, bf16[32,2304]{1,0:T(8,128)(2,1)S(1)}, u32[]{:S(2)}, u32[]{:S(2)}) collective-permute-start(bf16[32,2304]{1,0:T(8,128)(2,1)S(1)} %add_convert_fusion.1), channel_id=1, source_target_pairs={{0,1},{1,0},{2,3},{3,2},{4,5},{5,4},{6,7},{7,6},{8,9},{9,8},{10,11... | collective-permute-start | bytes 442376 | tf_op jit(solution)/shard_map/ppermute | solution.py:364
  59.2 6.7 %collective-permute-start.25 = (bf16[32,2304]{1,0:T(8,128)(2,1)S(1)}, bf16[32,2304]{1,0:T(8,128)(2,1)S(1)}, u32[]{:S(2)}, u32[]{:S(2)}) collective-permute-start(bf16[32,2304]{1,0:T(8,128)(2,1)S(1)} %add_convert_fusion.a_ref), channel_id=1, source_target_pairs={{0,64},{1,5},{2,66},{3,7},{4,68},{5,1},{6,70},{7,3},{8,72},{9,13},... | collective-permute-start | bytes 442376 | tf_op jit(solution)/shard_map/ppermute | solution.py:363
  61.4 6.4 %collective-permute-start.24 = (bf16[32,2304]{1,0:T(8,128)(2,1)S(1)}, bf16[32,2304]{1,0:T(8,128)(2,1)S(1)}, u32[]{:S(2)}, u32[]{:S(2)}) collective-permute-start(bf16[32,2304]{1,0:T(8,128)(2,1)S(1)} %add_convert_fusion.a_ref), channel_id=1, source_target_pairs={{0,96},{1,7},{2,98},{3,5},{4,100},{5,3},{6,102},{7,1},{8,104},{9,1... | collective-permute-start | bytes 442376 | tf_op jit(solution)/shard_map/ppermute | solution.py:363
  63.1 5.1 %collective-permute-start.23 = (bf16[32,2304]{1,0:T(8,128)(2,1)S(1)}, bf16[32,2304]{1,0:T(8,128)(2,1)S(1)}, u32[]{:S(2)}, u32[]{:S(2)}) collective-permute-start(bf16[32,2304]{1,0:T(8,128)(2,1)S(1)} %add_convert_fusion.a_ref), channel_id=1, source_target_pairs={{0,32},{1,3},{2,34},{3,1},{4,36},{5,7},{6,38},{7,5},{8,40},{9,11},... | collective-permute-start | bytes 442376 | tf_op jit(solution)/shard_map/ppermute | solution.py:363
